TPU v7x, 512 devices: a whole 4x8x8 slice. The times are simulated.
512 devices in a mesh: tensor: 8 (over x, core), replica: 64 (over z, y).
Axes of the slice: x: 4, y: 8, z: 8, core: 2. Of those that a mesh axis runs over, the one named last changes fastest.
Arguments:
- attention_result: bfloat16 [4096, 4096], P('replica', 'tensor'), may hold values from -6 to 6
- output_projection_weight: bfloat16 [4096, 4096], P('tensor'), may hold values from -0.09375 to 0.09375
- adapter_down_weight: bfloat16 [128, 64, 4096], P('replica', None, 'tensor'), may hold values from -0.09375 to 0.09375
- adapter_up_weight: bfloat16 [128, 64, 4096], P('replica', 'tensor'), may hold values from -0.75 to 0.75
- requested_adapters: int32 [64, 64], replicated, may hold values from 0 to 127, as said below
- slot: int32 [4096, 1], P('replica'), may hold values from 0 to 63; in each aligned block of 64 rows (0 to 63, 64 to 127, ...) at most 2 rows name the same one
Outputs:
- mixed: bfloat16 [4096, 4096], P('replica', 'tensor')
Inputs may be any that keep to these rules, and one draw needn't show every extreme that they name: `requested_adapters`: each row names 64 adapters whose owners a // 2 are all different. `slot`: within the 64 sequences of one group (the rows of one device) no entry is named by more than 2 sequences, and one entry by exactly 2 in some group.
All inputs are finite; a program needn't handle non-finite values.
Results may differ from a plain program's by a relative error of at most 0.0046.
Values may be sent and summed in bfloat16 or wider, within the bound.
No kernel may reach another device: no remote copies, remote signals or barrier semaphores. Data moves between devices by JAX's collectives and lax.ppermute only.
A program may use at most 64 MiB of HBM per device.

v0:
```python
import jax
import jax.numpy as jnp
from jax import lax
from jax.sharding import PartitionSpec as P

adapter_scale = 2.0


def rank_portion(partial_output, tensor_shard_index, rank_window):
    full_sum = lax.psum(partial_output, "tensor")
    return lax.dynamic_slice_in_dim(full_sum, tensor_shard_index * rank_window, rank_window, 1)


def wanted_pages(requested_adapters, group_index, present_adapters):
    owned_here = requested_adapters // present_adapters == group_index
    return jnp.sum(jnp.where(owned_here, requested_adapters % present_adapters, 0), axis=1)


def local(
    attention_result,
    output_projection_weight,
    adapter_down_weight,
    adapter_up_weight,
    requested_adapters,
    slot,
):
    group_index = lax.axis_index("replica")
    tensor_shard_index = lax.axis_index("tensor")
    present_adapters = adapter_down_weight.shape[0]
    rank_window = adapter_up_weight.shape[1]
    base_contribution = jnp.dot(
        attention_result, output_projection_weight, preferred_element_type=jnp.float32
    )
    group_list = jnp.take(requested_adapters, group_index, axis=0)
    selected_adapter = jnp.take(group_list, slot[:, 0], axis=0)
    owner_id = selected_adapter // present_adapters
    requested_ids = wanted_pages(requested_adapters, group_index, present_adapters)
    down_weight_pages = jnp.take(adapter_down_weight, requested_ids, axis=0)
    up_weight_pages = jnp.take(adapter_up_weight, requested_ids, axis=0)
    fetched_a, fetched_b = (
        lax.all_to_all(down_weight_pages, "replica", split_axis=0, concat_axis=0, tiled=True),
        lax.all_to_all(up_weight_pages, "replica", split_axis=0, concat_axis=0, tiled=True),
    )
    seq_pages_a = jnp.take(fetched_a, owner_id, axis=0)
    partial_output = jnp.einsum(
        "me,moe->mo", attention_result, seq_pages_a, preferred_element_type=jnp.float32
    )
    adapter_lowrank = (
        adapter_scale * rank_portion(partial_output, tensor_shard_index, rank_window)
    ).astype(jnp.bfloat16)
    sequence_up_pages = jnp.take(fetched_b, owner_id, axis=0)
    adapter_contribution = jnp.einsum(
        "zm,zml->zl", adapter_lowrank, sequence_up_pages, preferred_element_type=jnp.float32
    )
    reduced_total = lax.psum_scatter(
        base_contribution + adapter_contribution, "tensor", scatter_dimension=1, tiled=True
    )
    return reduced_total.astype(jnp.bfloat16)


def solution(mesh):
    in_specs = (
        P("replica", "tensor"),
        P("tensor", None),
        P("replica", None, "tensor"),
        P("replica", "tensor", None),
        P(),
        P("replica", None),
    )
    out_specs = P("replica", "tensor")
    return jax.shard_map(local, mesh=mesh, in_specs=in_specs, out_specs=out_specs, check_vma=False)
```

profile of v0, /device:TPU:1, one launch (start us, length us, event | category | flops | bytes accessed | tf_op | source)
XLA Modules:
  0.0 354.7 jit_solution(10881799453165968252)
XLA Ops:
  6.5 0.0 copy-start
  6.5 0.9 fusion.11
  7.5 0.7 fusion.17
  8.2 0.0 copy-done
  8.2 2.8 gather_fusion.1
  11.0 4.6 %broadcast_select_fusion.1 = bf16[64,64,512]{2,1,0:T(8,128)(2,1)} fusion(bf16[64,64,512]{2,1,0:T(8,128)(2,1)} %gather_fusion.1, pred[64]{0:T(512)(128)(4,1)S(1)} %compare_and_fusion), kind=kLoop, calls=%fused_computation.12 | loop fusion | flops 2097152 | bytes 8388672 | tf_op jit(solution)/shard_map/jit(_take)/select_n | solution.py:38
  15.6 0.0 copy-start.1
  15.6 17.5 %all-to-all-start = ((bf16[64,64,512]{2,1,0:T(8,128)(2,1)}), bf16[64,64,512]{2,1,0:T(8,128)(2,1)}, u32[]{:S(2)}, u32[]{:S(2)}) async-start(bf16[64,64,512]{2,1,0:T(8,128)(2,1)} %broadcast_select_fusion.1), calls=%async_computation | async-start | bytes 8388608 | tf_op jit(solution)/shard_map/all_to_all | solution.py:41
  33.1 0.0 copy-done.1
  33.1 2.8 gather_fusion.3
  35.9 4.6 %broadcast_select_fusion = bf16[64,8,4096]{2,1,0:T(8,128)(2,1)} fusion(bf16[64,8,4096]{2,1,0:T(8,128)(2,1)} %gather_fusion.3, pred[64]{0:T(512)(128)(4,1)S(1)} %compare_and_fusion), kind=kLoop, calls=%fused_computation.10 | loop fusion | flops 2097152 | bytes 8388672 | tf_op jit(solution)/shard_map/jit(_take)/select_n | solution.py:39
  40.4 0.0 copy-start.4
  40.5 99.7 %all-to-all-done = bf16[64,64,512]{2,1,0:T(8,128)(2,1)} async-done(((bf16[64,64,512]{2,1,0:T(8,128)(2,1)}), bf16[64,64,512]{2,1,0:T(8,128)(2,1)}, u32[]{:S(2)}, u32[]{:S(2)}) %all-to-all-start) | async-done | bytes 4194336 | tf_op jit(solution)/shard_map/all_to_all | solution.py:41
  140.2 28.7 %all-to-all-start.1 = ((bf16[64,8,4096]{2,1,0:T(8,128)(2,1)}), bf16[64,8,4096]{2,1,0:T(8,128)(2,1)}, u32[]{:S(2)}, u32[]{:S(2)}) async-start(bf16[64,8,4096]{2,1,0:T(8,128)(2,1)} %broadcast_select_fusion), calls=%async_computation.1 | async-start | bytes 8388608 | tf_op jit(solution)/shard_map/all_to_all | solution.py:42
  168.8 0.0 reduce-scatter.2.cloned.1.call-start
  168.9 0.7 fusion.16
  169.6 0.8 gather_fusion
  170.4 0.0 copy-done.4
  170.4 0.0 copy-start.3
  170.4 5.0 %gather_fusion.2 = bf16[64,64,512]{2,1,0:T(8,128)(2,1)} fusion(bf16[64,64,512]{2,1,0:T(8,128)(2,1)} %all-to-all-done, s32[1024]{0:T(1024)S(1)} %pad_clamp_fusion), kind=kCustom, calls=%fused_computation.2 | custom fusion | bytes 8388864 | tf_op jit(solution)/shard_map/jit(_take)/gather | solution.py:44
  175.4 0.0 copy-done.3
  175.4 3.4 fusion.2
  178.9 24.0 %psum.7 = f32[64,64]{1,0:T(8,128)S(1)} all-reduce(f32[64,64]{1,0:T(8,128)S(1)} %bitcast.26), channel_id=1, replica_groups=mesh['tensor'=8,'replica'=64] {'tensor'}, use_global_device_ids=true, to_apply=%region_1.2 | all-reduce | flops 4096 | bytes 32768 | tf_op jit(solution)/shard_map/psum | solution.py:10
  202.8 0.1 fusion.15
  202.9 70.5 %all-to-all-done.1 = bf16[64,8,4096]{2,1,0:T(8,128)(2,1)} async-done(((bf16[64,8,4096]{2,1,0:T(8,128)(2,1)}), bf16[64,8,4096]{2,1,0:T(8,128)(2,1)}, u32[]{:S(2)}, u32[]{:S(2)}) %all-to-all-start.1) | async-done | bytes 4194336 | tf_op jit(solution)/shard_map/all_to_all | solution.py:42
  273.4 4.9 %gather_fusion.4 = bf16[64,8,4096]{2,1,0:T(8,128)(2,1)} fusion(bf16[64,8,4096]{2,1,0:T(8,128)(2,1)} %all-to-all-done.1, s32[1024]{0:T(1024)S(1)} %pad_clamp_fusion), kind=kCustom, calls=%fused_computation.4 | custom fusion | bytes 8388864 | tf_op jit(solution)/shard_map/jit(_take)/gather | solution.py:51
  278.3 0.0 copy-start.2
  278.3 3.6 %fusion = f32[64,1,4096]{2,1,0:T(1,128)S(1)} fusion(bf16[64,8,4096]{2,1,0:T(8,128)(2,1)} %gather_fusion.4, pred[64]{0:T(512)(128)(4,1)S(1)} %get-tuple-element.16, bf16[64,8,1]{1,0,2:T(8,128)(2,1)S(1)} %fusion.15), kind=kOutput, calls=%fused_computation.6 | convolution fusion | flops 6291456 | bytes 5243968 | tf_op jit(solution)/shard_map/zm,zml->zl/dot_general | solution.py:52
  282.0 0.0 copy-done.2
  282.0 2.2 convolution_add_fusion
  284.2 0.0 reduce-scatter.2.cloned.1.call-update
  284.2 62.1 %reduce-scatter.2.cloned.1.call-done = f32[64,512]{1,0:T(8,128)} async-done(((f32[64,4096]{1,0:T(8,128)}), f32[64,512]{1,0:T(8,128)}) %reduce-scatter.2.cloned.1.call-update) | async-done | bytes 131088 | tf_op jit(solution)/shard_map/reduce_scatter | solution.py:55
  346.3 1.5 convert_element_type.7
  (5 shorter events, 0.0 us)
Async XLA Ops:
  6.5 1.6 copy-start
  15.6 17.5 %copy-start.1 = (bf16[2,8,4096]{2,1,0:T(8,128)(2,1)S(1)}, bf16[2,8,4096]{2,1,0:T(8,128)(2,1)}, u32[]{:S(2)}) copy-start(bf16[2,8,4096]{2,1,0:T(8,128)(2,1)} %param.9) | copy-start | bytes 393220
  15.6 124.6 %all-to-all-start = ((bf16[64,64,512]{2,1,0:T(8,128)(2,1)}), bf16[64,64,512]{2,1,0:T(8,128)(2,1)}, u32[]{:S(2)}, u32[]{:S(2)}) async-start(bf16[64,64,512]{2,1,0:T(8,128)(2,1)} %broadcast_select_fusion.1), calls=%async_computation | async-start | bytes 8388608 | tf_op jit(solution)/shard_map/all_to_all | solution.py:41
  40.4 129.9 %copy-start.4 = (s32[64,1]{0,1:T(1,128)S(1)}, s32[64,1]{0,1:T(1,128)}, u32[]{:S(2)}) copy-start(s32[64,1]{0,1:T(1,128)} %param.11) | copy-start | bytes 772
  140.2 133.2 %all-to-all-start.1 = ((bf16[64,8,4096]{2,1,0:T(8,128)(2,1)}), bf16[64,8,4096]{2,1,0:T(8,128)(2,1)}, u32[]{:S(2)}, u32[]{:S(2)}) async-start(bf16[64,8,4096]{2,1,0:T(8,128)(2,1)} %broadcast_select_fusion), calls=%async_computation.1 | async-start | bytes 8388608 | tf_op jit(solution)/shard_map/all_to_all | solution.py:42
  168.8 177.5 %reduce-scatter.2.cloned.1.call-start = ((), (), s32[]{:S(2)}) async-start(), calls=%async_computation.3 | async-start | bytes 1179648 | tf_op jit(solution)/shard_map/reduce_scatter | solution.py:55
  170.4 5.0 %copy-start.3 = (bf16[64,512]{1,0:T(8,128)(2,1)S(1)}, bf16[64,512]{1,0:T(8,128)(2,1)}, u32[]{:S(2)}) copy-start(bf16[64,512]{1,0:T(8,128)(2,1)} %param.6) | copy-start | bytes 196612
  278.3 3.7 %copy-start.2 = (bf16[512,4096]{1,0:T(8,128)(2,1)S(1)}, bf16[512,4096]{1,0:T(8,128)(2,1)}, u32[]{:S(2)}) copy-start(bf16[512,4096]{1,0:T(8,128)(2,1)} %param.7) | copy-start | bytes 12582916
Sparse Core Ops, SparseCore 0:
  284.3 61.9 reduce-scatter.1
where the time goes:
time: 356 us; the launch traced here: 355 us
  waiting for transfers between devices  232 us (65%)
  starting transfers between devices  46.2 us (13%)
  blocking collectives  24 us (7%)
  local copies, waits for them, and re-layouts  16.3 us (5%)
  between operations  13.5 us (4%)
  other arithmetic  13.1 us (4%)
  matrix products  9.28 us (3%)
    all_to_all x1, waiting for transfers between devices, local(): lax.all_to_all(down_weight_pages, 'replica', split_axis=0, concat_axis=0,...  99.7 us
    all_to_all x1, waiting for transfers between devices, local(): lax.all_to_all(up_weight_pages, 'replica', split_axis=0, concat_axis=0, t...  70.5 us
    reduce_scatter x1, waiting for transfers between devices, local(): lax.psum_scatter(base_contribution + adapter_contribution, 'tensor', scat...  62.1 us
    all_to_all x1, starting transfers between devices, local(): lax.all_to_all(up_weight_pages, 'replica', split_axis=0, concat_axis=0, t...  28.7 us
    psum x1, blocking collectives, rank_portion(): full_sum = lax.psum(partial_output, 'tensor')  24 us
    all_to_all x1, starting transfers between devices, local(): lax.all_to_all(down_weight_pages, 'replica', split_axis=0, concat_axis=0,...  17.5 us
  transfers between devices with their start and end apart: 3, of which 3 were waited for; matrix products, arithmetic and copies ran while one was open for 5% of the time, Pallas kernels for 0%

commit v1 on v0

v1 whole, which is shorter than its diff:
```python
import jax
import jax.numpy as jnp
from jax import lax
from jax.sharding import PartitionSpec as P

adapter_scale = 2.0
most = 2
bf16 = jnp.bfloat16
f32 = jnp.float32


def local(attention, weight, down, up, requested, slot):
    group = lax.axis_index("replica")
    rows, features = attention.shape
    present, rank, _ = down.shape
    owners = requested.shape[0]
    columns = weight.shape[1] // lax.axis_size("tensor")

    entries = jnp.take(requested, group, axis=0)
    named = (slot == jnp.arange(entries.shape[0])[None, :]).astype(bf16)
    earlier = jnp.dot(jnp.tril(jnp.ones((rows, rows), bf16), -1), named, preferred_element_type=f32)
    place = jnp.sum(earlier * named, axis=1).astype(jnp.int32)
    owner = jnp.sum(named.astype(jnp.int32) * (entries // present)[None, :], axis=1)
    goes = (owner * most + place)[:, None] == jnp.arange(owners * most)[None, :]
    goes = goes.astype(bf16)
    sent = jnp.dot(goes.T, attention, preferred_element_type=f32).astype(bf16)
    here = lax.all_to_all(sent.reshape(owners, most, features), "replica", 0, 0, tiled=True)

    base = jnp.dot(attention, weight, preferred_element_type=f32).astype(bf16)
    base = lax.psum_scatter(base, "tensor", scatter_dimension=1, tiled=True)

    mine = requested // present == group
    which = jnp.sum(jnp.where(mine, requested % present, 0), axis=1)
    which = jnp.repeat(which, most)
    chosen = which[:, None] == jnp.arange(present)[None, :]

    low = jnp.dot(
        here.reshape(owners * most, features),
        down.reshape(present * rank, features).T,
        preferred_element_type=f32,
    ).reshape(owners * most, present, rank)
    low = jnp.sum(jnp.where(chosen[:, :, None], low, 0.0), axis=1).astype(bf16)
    shards = lax.axis_size("tensor")
    low = lax.all_to_all(
        jnp.broadcast_to(low, (shards,) + low.shape), "tensor", 0, 0, tiled=True
    )
    low = (adapter_scale * jnp.sum(low.astype(f32), axis=0)).astype(bf16)

    up = up.reshape(present, up.shape[1], shards, columns).transpose(2, 0, 1, 3)
    up = lax.all_to_all(up, "tensor", 0, 0, tiled=True)
    up = up.transpose(1, 0, 2, 3).reshape(present * rank, columns)
    low = jnp.where(chosen[:, :, None], low[:, None, :], jnp.zeros((), bf16))
    out = jnp.dot(
        low.reshape(owners * most, present * rank), up, preferred_element_type=f32
    ).astype(bf16)
    back = lax.all_to_all(out.reshape(owners, most, columns), "replica", 0, 0, tiled=True)
    out = jnp.dot(goes, back.reshape(owners * most, columns), preferred_element_type=f32)
    return (base.astype(f32) + out).astype(bf16)


def solution(mesh):
    in_specs = (
        P("replica", "tensor"),
        P("tensor", None),
        P("replica", None, "tensor"),
        P("replica", "tensor", None),
        P(),
        P("replica", None),
    )
    out_specs = P("replica", "tensor")
    return jax.shard_map(local, mesh=mesh, in_specs=in_specs, out_specs=out_specs, check_vma=False)
```

time: 356 us -> 96.1 us (0.27)
  waiting for transfers between devices: 232 us -> 24.4 us
  starting transfers between devices: 46.2 us -> 27.7 us
  local copies, waits for them, and re-layouts: 16.3 us -> 3.42 us
  other arithmetic: 13.1 us -> 2.43 us
  blocking collectives: 24 us -> 15.3 us
    all_to_all x2 -> x3, waiting for transfers between devices: 170 us -> 15.2 us  [the longest x1 8.76 us: local(): lax.all_to_all(sent.reshape(owners, most, features), 'replica', 0, 0, til...]
    reduce_scatter x1, waiting for transfers between devices: 62.1 us -> 9.21 us  [local(): base = lax.psum_scatter(base, 'tensor', scatter_dimension=1, tiled=True)]
    psum x1 -> x0, blocking collectives: 24 us -> none  [rank_portion(): full_sum = lax.psum(partial_output, 'tensor')]
    all_to_all x2 -> x3, starting transfers between devices: 46.2 us -> 27.7 us  [the longest x1 17.1 us: local(): lax.all_to_all(sent.reshape(owners, most, features), 'replica', 0, 0, til...]
    gather x5 -> x0, local copies, waits for them, and re-layouts: 16.3 us -> none  [the longest x1 4.99 us: local(): seq_pages_a = jnp.take(fetched_a, owner_id, axis=0)]
    all_to_all x0 -> x1, blocking collectives: none -> 15.3 us  [local(): lax.all_to_all(out.reshape(owners, most, columns), 'replica', 0, 0, tiled...]
    select_n x4 -> x2, other arithmetic: 10.5 us -> 0.74 us  [the longest x1 0.73 us: local(): entries // present]
    dot_general x3 -> x6, matrix products: 9.28 us -> 8.01 us  [the longest x1 3.86 us: local(): base = jnp.dot(attention, weight, preferred_element_type=f32).astype(bf16)]
  transfers between devices with their start and end apart: 3 -> 4, of which waited for: 3 -> 4; matrix products, arithmetic and copies ran while one was open for 5% -> 8% of each run, Pallas kernels for 0% -> 0%
where the time goes in v1:
time: 96.1 us; the launch traced here: 94.8 us
  starting transfers between devices  27.7 us (29%)
  waiting for transfers between devices  24.4 us (25%)
  blocking collectives  15.3 us (16%)
  between operations  13.5 us (14%)
  matrix products  8.01 us (8%)
  local copies, waits for them, and re-layouts  3.42 us (4%)
  other arithmetic  2.43 us (3%)
    all_to_all x1, starting transfers between devices, local(): lax.all_to_all(sent.reshape(owners, most, features), 'replica', 0, 0, til...  17.1 us
    all_to_all x1, blocking collectives, local(): lax.all_to_all(out.reshape(owners, most, columns), 'replica', 0, 0, tiled...  15.3 us
    reduce_scatter x1, waiting for transfers between devices, local(): base = lax.psum_scatter(base, 'tensor', scatter_dimension=1, tiled=True)  9.21 us
    all_to_all x1, waiting for transfers between devices, local(): lax.all_to_all(sent.reshape(owners, most, features), 'replica', 0, 0, til...  8.76 us
    all_to_all x1, starting transfers between devices, local(): up = lax.all_to_all(up, 'tensor', 0, 0, tiled=True)  6.42 us
    all_to_all x1, waiting for transfers between devices, local(): up = lax.all_to_all(up, 'tensor', 0, 0, tiled=True)  5.01 us
    all_to_all x1, starting transfers between devices, local(): lax.all_to_all(jnp.broadcast_to(low, (shards,) + low.shape), 'tensor', 0,...  4.14 us
    dot_general x1, matrix products, local(): base = jnp.dot(attention, weight, preferred_element_type=f32).astype(bf16)  3.86 us
  transfers between devices with their start and end apart: 4, of which 4 were waited for; matrix products, arithmetic and copies ran while one was open for 8% of the time, Pallas kernels for 0%

profile of v1, /device:TPU:1, one launch (start us, length us, event | category | flops | bytes accessed | tf_op | source)
XLA Modules:
  0.0 94.8 jit_solution(4079653445852311685)
XLA Ops:
  6.5 0.0 copy-start
  6.5 0.7 and_select_fusion
  7.3 0.8 multiply_reduce_fusion
  8.0 0.9 fusion.2
  9.0 1.1 %convolution_convert_fusion.2 = bf16[128,512]{1,0:T(8,128)(2,1)S(1)} fusion(bf16[64,512]{1,0:T(8,128)(2,1)} %param.6, s32[64]{0:T(128)S(1)} %convert_add_fusion), kind=kOutput, calls=%fused_computation.2 | convolution fusion | flops 8462336 | bytes 196864 | tf_op jit(solution)/shard_map/dot_general | solution.py:26
  10.1 0.7 reshape.89
  10.8 17.1 %all-to-all-start = ((bf16[64,2,512]{2,1,0:T(2,128)(2,1)}), bf16[64,2,512]{2,1,0:T(2,128)(2,1)S(1)}, u32[]{:S(2)}, u32[]{:S(2)}) async-start(bf16[64,2,512]{2,1,0:T(2,128)(2,1)} %reshape.89), calls=%async_computation.1 | async-start | bytes 262144 | tf_op jit(solution)/shard_map/all_to_all | solution.py:27
  28.0 0.9 fusion.5
  28.9 0.1 broadcast_in_dim.70
  28.9 0.2 eq.64
  29.1 1.0 %copy.11 = bf16[2,8,8,512]{3,2,1,0:T(8,128)(2,1)S(1)} copy(bf16[2,8,8,512]{3,1,2,0:T(8,128)(2,1)} %bitcast.29) | data formatting | bytes 262144
  30.0 0.7 copy.7
  30.7 8.8 %all-to-all-done = bf16[64,2,512]{2,1,0:T(2,128)(2,1)S(1)} async-done(((bf16[64,2,512]{2,1,0:T(2,128)(2,1)}), bf16[64,2,512]{2,1,0:T(2,128)(2,1)S(1)}, u32[]{:S(2)}, u32[]{:S(2)}) %all-to-all-start) | async-done | bytes 131104 | tf_op jit(solution)/shard_map/all_to_all | solution.py:27
  39.5 6.4 %all-to-all-start.2 = ((bf16[8,2,8,512]{3,2,1,0:T(8,128)(2,1)}), bf16[8,2,8,512]{3,2,1,0:T(8,128)(2,1)S(1)}, u32[]{:S(2)}, u32[]{:S(2)}) async-start(bf16[8,2,8,512]{3,2,1,0:T(8,128)(2,1)} %copy.7), calls=%async_computation.3 | async-start | bytes 262144 | tf_op jit(solution)/shard_map/all_to_all | solution.py:50
  45.9 0.1 reshape.125
  46.0 0.0 copy-done
  46.0 0.2 fusion.1
  46.2 5.0 %all-to-all-done.2 = bf16[8,2,8,512]{3,2,1,0:T(8,128)(2,1)S(1)} async-done(((bf16[8,2,8,512]{3,2,1,0:T(8,128)(2,1)}), bf16[8,2,8,512]{3,2,1,0:T(8,128)(2,1)S(1)}, u32[]{:S(2)}, u32[]{:S(2)}) %all-to-all-start.2) | async-done | bytes 131104 | tf_op jit(solution)/shard_map/all_to_all | solution.py:50
  51.2 0.7 broadcast_in_dim.73
  51.9 4.1 %all-to-all-start.1 = ((bf16[8,128,64]{1,2,0:T(8,128)(2,1)}), bf16[8,128,64]{1,2,0:T(8,128)(2,1)S(1)}, u32[]{:S(2)}, u32[]{:S(2)}) async-start(bf16[8,128,64]{1,2,0:T(8,128)(2,1)} %broadcast_in_dim.73), calls=%async_computation.2 | async-start | bytes 262144 | tf_op jit(solution)/shard_map/all_to_all | solution.py:44
  56.0 0.0 reduce-scatter.2.cloned.1.call-start
  56.0 3.9 %convolution_convert_fusion = bf16[64,4096]{1,0:T(8,128)(2,1)} fusion(bf16[64,512]{1,0:T(8,128)(2,1)} %param.6, bf16[512,4096]{1,0:T(8,128)(2,1)} %param.7), kind=kOutput, calls=%fused_computation | convolution fusion | flops 268697600 | bytes 4784128 | tf_op jit(solution)/shard_map/dot_general | solution.py:29
  59.9 0.0 reduce-scatter.2.cloned.1.call-update
  59.9 1.4 %all-to-all-done.1 = bf16[8,128,64]{1,2,0:T(8,128)(2,1)S(1)} async-done(((bf16[8,128,64]{1,2,0:T(8,128)(2,1)}), bf16[8,128,64]{1,2,0:T(8,128)(2,1)S(1)}, u32[]{:S(2)}, u32[]{:S(2)}) %all-to-all-start.1) | async-done | bytes 131104 | tf_op jit(solution)/shard_map/all_to_all | solution.py:44
  61.4 0.2 convolution_convert_fusion.1
  61.6 0.1 reshape.93
  61.6 15.3 %all_to_all.20 = bf16[64,2,512]{2,1,0:T(2,128)(2,1)S(1)} all-to-all(bf16[64,2,512]{2,1,0:T(2,128)(2,1)S(1)} %reshape.93), channel_id=1, replica_groups=mesh['tensor'=8,'replica'=64] {'replica'}, dimensions={0} | all-to-all | bytes 262144 | tf_op jit(solution)/shard_map/all_to_all | solution.py:56
  77.0 0.1 reshape.94
  77.0 9.2 %reduce-scatter.2.cloned.1.call-done = bf16[64,512]{1,0:T(8,128)(2,1)} async-done(((bf16[64,4096]{1,0:T(8,128)(2,1)}), bf16[64,512]{1,0:T(8,128)(2,1)}) %reduce-scatter.2.cloned.1.call-update) | async-done | bytes 65552 | tf_op jit(solution)/shard_map/reduce_scatter | solution.py:30
  86.3 1.7 %fusion = bf16[64,512]{1,0:T(8,128)(2,1)} fusion(bf16[128,512]{1,0:T(8,128)(2,1)S(1)} %reshape.94, bf16[64,512]{1,0:T(8,128)(2,1)} %reduce-scatter.2.cloned.1.call-done, s32[64]{0:T(128)S(1)} %convert_add_fusion), kind=kOutput, calls=%fused_computation.4 | convolution fusion | flops 8495104 | bytes 262400 | tf_op jit(solution)/shard_map/dot_general | solution.py:57
  (7 shorter events, 0.1 us)
Async XLA Ops:
  6.5 39.5 %copy-start = (bf16[2,64,512]{2,1,0:T(8,128)(2,1)S(1)}, bf16[2,64,512]{2,1,0:T(8,128)(2,1)}, u32[]{:S(2)}) copy-start(bf16[2,64,512]{2,1,0:T(8,128)(2,1)} %param.8) | copy-start | bytes 393220
  10.8 28.7 %all-to-all-start = ((bf16[64,2,512]{2,1,0:T(2,128)(2,1)}), bf16[64,2,512]{2,1,0:T(2,128)(2,1)S(1)}, u32[]{:S(2)}, u32[]{:S(2)}) async-start(bf16[64,2,512]{2,1,0:T(2,128)(2,1)} %reshape.89), calls=%async_computation.1 | async-start | bytes 262144 | tf_op jit(solution)/shard_map/all_to_all | solution.py:27
  39.5 11.7 %all-to-all-start.2 = ((bf16[8,2,8,512]{3,2,1,0:T(8,128)(2,1)}), bf16[8,2,8,512]{3,2,1,0:T(8,128)(2,1)S(1)}, u32[]{:S(2)}, u32[]{:S(2)}) async-start(bf16[8,2,8,512]{3,2,1,0:T(8,128)(2,1)} %copy.7), calls=%async_computation.3 | async-start | bytes 262144 | tf_op jit(solution)/shard_map/all_to_all | solution.py:50
  51.9 9.4 %all-to-all-start.1 = ((bf16[8,128,64]{1,2,0:T(8,128)(2,1)}), bf16[8,128,64]{1,2,0:T(8,128)(2,1)S(1)}, u32[]{:S(2)}, u32[]{:S(2)}) async-start(bf16[8,128,64]{1,2,0:T(8,128)(2,1)} %broadcast_in_dim.73), calls=%async_computation.2 | async-start | bytes 262144 | tf_op jit(solution)/shard_map/all_to_all | solution.py:44
  56.0 30.2 %reduce-scatter.2.cloned.1.call-start = ((), (), s32[]{:S(2)}) async-start(), calls=%async_computation.5 | async-start | bytes 589824 | tf_op jit(solution)/shard_map/reduce_scatter | solution.py:30
Sparse Core Ops, SparseCore 0:
  60.0 26.1 reduce-scatter.1

commit v2 on v1

v2 whole, which is shorter than its diff:
```python
import functools

import jax
import jax.numpy as jnp
from jax import lax
from jax.experimental import pallas as pl
from jax.experimental.pallas import tpu as pltpu
from jax.sharding import PartitionSpec as P

adapter_scale = 2.0
most = 2
lanes = 128
block = 16
bf16 = jnp.bfloat16
f32 = jnp.float32
i32 = jnp.int32


def iota(shape, axis):
    return lax.broadcasted_iota(i32, shape, axis)


def one_hot(hit):
    return jnp.where(hit, 1.0, 0.0).astype(bf16)


def times(a, b):
    return jnp.dot(a, b, preferred_element_type=f32)


def place_rows(present, requested_ref, slot_ref):
    group = lax.axis_index("replica")
    owners = requested_ref.shape[0]
    count = slot_ref.shape[0]
    square = (count, count)
    slot = jnp.sum(
        jnp.where(iota(square, 0) == iota(square, 1), slot_ref[...], 0), axis=0, keepdims=True
    )
    mine = iota(requested_ref.shape, 0) == group
    entries = jnp.sum(jnp.where(mine, requested_ref[...], 0), axis=0, keepdims=True)
    named = iota((owners, count), 0) == slot
    before = one_hot(iota(square, 0) < iota(square, 1))
    earlier = times(one_hot(named), before)
    place = jnp.sum(jnp.where(named, earlier, 0.0), axis=0, keepdims=True)
    owner = lax.div(entries, jnp.int32(present)).astype(f32).astype(bf16)
    owner = times(jnp.broadcast_to(owner, (block, owners)), one_hot(named))[:1]
    return (owner * float(most) + place).astype(i32)


def send_kernel(present, requested_ref, slot_ref, attention_ref, sent_ref, goes_ref):
    goes = place_rows(present, requested_ref, slot_ref)
    count, features = attention_ref.shape
    chunks = features // lanes
    goes_ref[...] = jnp.sum(
        jnp.where(iota((count, count), 0) == iota((count, count), 1), goes, 0), axis=1, keepdims=True
    )
    target = jnp.concatenate([goes * chunks + k for k in range(chunks)], axis=1)
    stacked = jnp.concatenate(
        [attention_ref[:, k * lanes : (k + 1) * lanes] for k in range(chunks)], axis=0
    )
    pick = one_hot(iota((sent_ref.shape[0], chunks * count), 0) == target)
    sent_ref[...] = times(pick, stacked).astype(bf16)


def base_kernel(attention_ref, weight_ref, up_ref, out_ref):
    rows = attention_ref.shape[0]
    chunks = weight_ref.shape[1] // lanes
    base = times(attention_ref[...], weight_ref[...]).astype(bf16)
    for k in range(chunks):
        out_ref[0, k * rows : (k + 1) * rows, :] = base[:, k * lanes : (k + 1) * lanes]
    up = jnp.concatenate([up_ref[a] for a in range(up_ref.shape[0])], axis=0)
    height = up.shape[0]
    for k in range(chunks):
        out_ref[0, chunks * rows + k * height : chunks * rows + (k + 1) * height, :] = up[
            :, k * lanes : (k + 1) * lanes
        ]


def named_here(requested_ref, present):
    owner = lax.axis_index("replica")
    requested = requested_ref[...]
    mine = lax.div(requested, jnp.int32(present)) == owner
    return jnp.sum(
        jnp.where(mine, lax.rem(requested, jnp.int32(present)), 0), axis=1, keepdims=True
    )


def interleave(parts, backward):
    shape = (parts * block, parts * block)
    row, column = iota(shape, 0), iota(shape, 1)
    if backward:
        row, column = column, row
    return one_hot(lax.rem(row, jnp.int32(parts)) * block + lax.div(row, jnp.int32(parts)) == column)


def low_kernel(requested_ref, here_ref, down_ref, message_ref, out_ref, rows_ref):
    del message_ref
    present, rank, features = down_ref.shape
    groups = requested_ref.shape[0]
    chunks = features // lanes
    parts = most * chunks
    order = interleave(parts, True)
    for b in range(groups // block):
        rows = times(order, here_ref[b * parts * block : (b + 1) * parts * block, :]).astype(bf16)
        for j in range(parts):
            place, k = divmod(j, chunks)
            rows_ref[
                place * groups + b * block : place * groups + (b + 1) * block,
                k * lanes : (k + 1) * lanes,
            ] = rows[j * block : (j + 1) * block, :]
    down = jnp.concatenate([down_ref[a] for a in range(present)], axis=0)
    low = lax.dot_general(
        rows_ref[...], down, (((1,), (1,)), ((), ())), preferred_element_type=f32
    )
    which = named_here(requested_ref, present)
    places = []
    for place in range(most):
        one = low[place * groups : (place + 1) * groups, :]
        places.append(
            sum(
                jnp.where(which == a, one[:, a * rank : (a + 1) * rank], 0.0)
                for a in range(present)
            )
        )
    low = jnp.concatenate(places, axis=1).astype(bf16)
    for peer in range(out_ref.shape[0]):
        out_ref[peer] = low


def result_kernel(present, requested_ref, low_ref, up_ref, out_ref, rows_ref):
    shards, groups, width = low_ref.shape
    rank = width // most
    window = rank // shards
    depth = shards * present * window
    chunks = up_ref.shape[1] // (present * window)
    parts = most * chunks
    low = low_ref[0].astype(f32)
    for peer in range(1, shards):
        low = low + low_ref[peer].astype(f32)
    low = (adapter_scale * low).astype(bf16)
    up = jnp.concatenate(
        [
            jnp.concatenate(
                [up_ref[peer, k * present * window : (k + 1) * present * window, :] for peer in range(shards)],
                axis=0,
            )
            for k in range(chunks)
        ],
        axis=1,
    )
    which = named_here(requested_ref, present)
    source, target = iota((width, depth), 0), iota((width, depth), 1)
    shard = lax.div(target, jnp.int32(present * window))
    rank_of = shard * window + lax.rem(target, jnp.int32(window))
    adapter = iota((groups, depth), 1)
    adapter = lax.rem(lax.div(adapter, jnp.int32(window)), jnp.int32(present))
    order = interleave(parts, False)
    results = []
    for place in range(most):
        spread = times(low, one_hot(source == place * rank + rank_of)).astype(bf16)
        spread = jnp.where(adapter == which, spread, jnp.zeros_like(spread))
        results.append(times(spread, up).astype(bf16))
    for b in range(groups // block):
        for j in range(parts):
            place, k = divmod(j, chunks)
            rows_ref[j * block : (j + 1) * block, :] = results[place][
                b * block : (b + 1) * block, k * lanes : (k + 1) * lanes
            ]
        out_ref[b * parts * block : (b + 1) * parts * block, :] = times(order, rows_ref[...]).astype(bf16)


def sum_kernel(base_ref, out_ref):
    total = base_ref[0].astype(f32)
    for peer in range(1, base_ref.shape[0]):
        total = total + base_ref[peer].astype(f32)
    out_ref[...] = total


def finish_kernel(goes_ref, base_ref, back_ref, out_ref):
    rows, columns = out_ref.shape
    chunks = columns // lanes
    goes = goes_ref[...] * chunks
    for k in range(chunks):
        pick = one_hot(iota((rows, back_ref.shape[0]), 1) == goes + k)
        total = base_ref[k * rows : (k + 1) * rows, :] + times(pick, back_ref[...])
        out_ref[:, k * lanes : (k + 1) * lanes] = total.astype(bf16)


def whole(shape):
    return pl.BlockSpec(shape, lambda *_: (0,) * len(shape))


def local(attention, weight, down, up, requested, slot):
    rows, features = attention.shape
    present, rank, _ = down.shape
    window = up.shape[1]
    groups = requested.shape[0]
    shards = lax.axis_size("tensor")
    columns = weight.shape[1] // shards
    parts = most * features // lanes
    out_parts = most * columns // lanes
    call = pl.pallas_call

    sent, goes = call(
        functools.partial(send_kernel, present),
        grid=(),
        out_shape=(
            jax.ShapeDtypeStruct((groups * parts, lanes), bf16),
            jax.ShapeDtypeStruct((rows, 1), i32),
        ),
        in_specs=[whole(requested.shape), whole(slot.shape), whole(attention.shape)],
        out_specs=(whole((groups * parts, lanes)), whole((rows, 1))),
    )(requested, slot, attention)
    here = lax.all_to_all(sent.reshape(groups, parts, lanes), "replica", 0, 0, tiled=True)

    chunks = columns // lanes
    base_rows = chunks * rows
    up_rows = chunks * present * window
    low_rows = groups
    total_rows = base_rows + up_rows + low_rows
    message = call(
        base_kernel,
        grid=(shards,),
        out_shape=jax.ShapeDtypeStruct((shards, total_rows, lanes), bf16),
        in_specs=[
            whole(attention.shape),
            pl.BlockSpec((features, columns), lambda i: (0, i)),
            pl.BlockSpec((present, window, columns), lambda i: (0, 0, i)),
        ],
        out_specs=pl.BlockSpec((1, total_rows, lanes), lambda i: (i, 0, 0)),
        cost_estimate=pl.CostEstimate(
            flops=2 * rows * features * weight.shape[1],
            bytes_accessed=2 * weight.size + 2 * shards * total_rows * lanes,
            transcendentals=0,
        ),
    )(attention, weight, up)

    low_block = pl.BlockSpec(
        (shards, low_rows, lanes), lambda *_: (0, (base_rows + up_rows) // low_rows, 0)
    )
    message = call(
        low_kernel,
        grid=(1,),
        out_shape=jax.ShapeDtypeStruct(message.shape, bf16),
        in_specs=[
            whole(requested.shape),
            whole((groups * parts, lanes)),
            whole(down.shape),
            pl.BlockSpec(memory_space=pl.ANY),
        ],
        out_specs=low_block,
        scratch_shapes=[pltpu.VMEM((most * groups, features), bf16)],
        input_output_aliases={3: 0},
    )(requested, here.reshape(groups * parts, lanes), down, message)
    message = lax.all_to_all(message, "tensor", 0, 0, tiled=True)

    result = call(
        functools.partial(result_kernel, present),
        grid=(1,),
        out_shape=jax.ShapeDtypeStruct((groups * out_parts, lanes), bf16),
        in_specs=[
            whole(requested.shape),
            low_block,
            pl.BlockSpec((shards, up_rows, lanes), lambda *_: (0, base_rows // up_rows, 0)),
        ],
        out_specs=whole((groups * out_parts, lanes)),
        scratch_shapes=[pltpu.VMEM((out_parts * block, lanes), bf16)],
    )(requested, message, message)
    back = lax.all_to_all(result.reshape(groups, out_parts, lanes), "replica", 0, 0, tiled=True)

    base = call(
        sum_kernel,
        grid=(1,),
        out_shape=jax.ShapeDtypeStruct((base_rows, lanes), f32),
        in_specs=[whole((shards, base_rows, lanes))],
        out_specs=whole((base_rows, lanes)),
        cost_estimate=pl.CostEstimate(
            flops=shards * base_rows * lanes,
            bytes_accessed=2 * shards * base_rows * lanes,
            transcendentals=0,
        ),
    )(message)
    return call(
        finish_kernel,
        grid=(),
        out_shape=jax.ShapeDtypeStruct((rows, columns), bf16),
        in_specs=[
            whole((rows, 1)),
            whole((base_rows, lanes)),
            whole((groups * out_parts, lanes)),
        ],
        out_specs=whole((rows, columns)),
    )(goes, base, back.reshape(groups * out_parts, lanes))


def solution(mesh):
    in_specs = (
        P("replica", "tensor"),
        P("tensor", None),
        P("replica", None, "tensor"),
        P("replica", "tensor", None),
        P(),
        P("replica", None),
    )
    out_specs = P("replica", "tensor")
    return jax.shard_map(local, mesh=mesh, in_specs=in_specs, out_specs=out_specs, check_vma=False)
```

time: 96.1 us -> 77 us (0.80)
  Pallas kernels: 0 us -> 16.7 us
  between operations: 13.5 us -> 0.02 us
  waiting for transfers between devices: 24.4 us -> 14.6 us
  matrix products: 8.01 us -> 0 us
  starting transfers between devices: 27.7 us -> 23.5 us
  blocking collectives: 15.3 us -> 18.7 us
  other arithmetic: 2.43 us -> 0 us
    pallas_call x0 -> x6, Pallas kernels: none -> 16.7 us  [the longest x1 6.67 us: local(): call(base_kernel, grid=(shards,), out_shape=jax.ShapeDtypeStruct((shards,...]
    reduce_scatter x1 -> x0, waiting for transfers between devices: 9.21 us -> none  [local(): base = lax.psum_scatter(base, 'tensor', scatter_dimension=1, tiled=True)]
    dot_general x6 -> x0, matrix products: 8.01 us -> none  [the longest x1 3.86 us: local(): base = jnp.dot(attention, weight, preferred_element_type=f32).astype(bf16)]
    all_to_all x3 -> x2, starting transfers between devices: 27.7 us -> 23.5 us  [the longest x1 17.1 us: local(): lax.all_to_all(sent.reshape(groups, parts, lanes), 'replica', 0, 0, tiled...]
    all_to_all x1, blocking collectives: 15.3 us -> 18.7 us  [local(): message = lax.all_to_all(message, 'tensor', 0, 0, tiled=True)]
    unnamed x3 -> x5, local copies, waits for them, and re-layouts: 0.95 us -> 2.66 us
    reduce_sum x3 -> x0, other arithmetic: 1.67 us -> none  [the longest x1 0.89 us: local(): which = jnp.sum(jnp.where(mine, requested % present, 0), axis=1)]
    all_to_all x3 -> x2, waiting for transfers between devices: 15.2 us -> 14.6 us  [the longest x1 9.78 us: local(): lax.all_to_all(result.reshape(groups, out_parts, lanes), 'replica', 0, 0,...]
  transfers between devices with their start and end apart: 4 -> 2, of which waited for: 4 -> 2; matrix products, arithmetic and copies ran while one was open for 8% -> 0% of each run, Pallas kernels for 0% -> 11%
where the time goes in v2:
time: 77 us; the launch traced here: 76.3 us
  starting transfers between devices  23.5 us (31%)
  blocking collectives  18.7 us (24%)
  Pallas kernels  16.7 us (22%)
  waiting for transfers between devices  14.6 us (19%)
  local copies, waits for them, and re-layouts  2.66 us (3%)
    all_to_all x1, blocking collectives, local(): message = lax.all_to_all(message, 'tensor', 0, 0, tiled=True)  18.7 us
    all_to_all x1, starting transfers between devices, local(): lax.all_to_all(sent.reshape(groups, parts, lanes), 'replica', 0, 0, tiled...  17.1 us
    all_to_all x1, waiting for transfers between devices, local(): lax.all_to_all(result.reshape(groups, out_parts, lanes), 'replica', 0, 0,...  9.78 us
    pallas_call x1, Pallas kernels, local(): call(base_kernel, grid=(shards,), out_shape=jax.ShapeDtypeStruct((shards,...  6.67 us
    all_to_all x1, starting transfers between devices, local(): lax.all_to_all(result.reshape(groups, out_parts, lanes), 'replica', 0, 0,...  6.38 us
    all_to_all x1, waiting for transfers between devices, local(): lax.all_to_all(sent.reshape(groups, parts, lanes), 'replica', 0, 0, tiled...  4.87 us
    unnamed x5, local copies, waits for them, and re-layouts  2.66 us
    pallas_call x1, Pallas kernels, local(): call(functools.partial(result_kernel, present), grid=(1,), out_shape=jax....  2.22 us
  transfers between devices with their start and end apart: 2, of which 2 were waited for; matrix products, arithmetic and copies ran while one was open for 0% of the time, Pallas kernels for 11%

profile of v2, /device:TPU:1, one launch (start us, length us, event | category | flops | bytes accessed | tf_op | source)
XLA Modules:
  0.0 76.3 jit_solution(12393630363344445117)
XLA Ops:
  0.0 1.4 %copy.8.slot_ref = s32[64,1]{1,0:T(8,128)} copy(s32[64,1]{0,1:T(1,128)} %param.11) | data formatting | bytes 512 | tf_op args[5]
  1.4 2.0 %shard_map.64 = (bf16[512,128]{1,0:T(8,128)(2,1)}, s32[64,1]{1,0:T(8,128)}) custom-call(s32[64,64]{1,0:T(8,128)} %requested_ref.5, s32[64,1]{1,0:T(8,128)} %copy.8.slot_ref, bf16[64,512]{1,0:T(8,128)(2,1)} %attention_ref.3), custom_call_target="tpu_custom_call" | custom-call | tf_op jit(solution)/shard_map/pallas_call | solution.py:204
  3.4 17.1 %all-to-all-start = ((bf16[64,8,128]{2,1,0:T(8,128)(2,1)}), bf16[64,8,128]{2,1,0:T(8,128)(2,1)S(1)}, u32[]{:S(2)}, u32[]{:S(2)}) async-start(bf16[64,8,128]{2,1,0:T(8,128)(2,1)} %bitcast.7), calls=%async_computation | async-start | bytes 262144 | tf_op jit(solution)/shard_map/all_to_all | solution.py:214
  20.5 6.7 %shard_map.65.message_ref = bf16[8,384,128]{2,1,0:T(8,128)(2,1)} custom-call(bf16[64,512]{1,0:T(8,128)(2,1)} %attention_ref.3, bf16[512,4096]{1,0:T(8,128)(2,1)} %weight_ref.1, bf16[2,8,4096]{2,1,0:T(8,128)(2,1)} %up_ref.1), custom_call_target="tpu_custom_call" | custom-call | flops 268435456 | bytes 4980736 | tf_op jit(solution)/shard_map/pallas_call | solution.py:221
  27.2 4.9 %all-to-all-done = bf16[64,8,128]{2,1,0:T(8,128)(2,1)S(1)} async-done(((bf16[64,8,128]{2,1,0:T(8,128)(2,1)}), bf16[64,8,128]{2,1,0:T(8,128)(2,1)S(1)}, u32[]{:S(2)}, u32[]{:S(2)}) %all-to-all-start) | async-done | bytes 131104 | tf_op jit(solution)/shard_map/all_to_all | solution.py:214
  32.1 0.0 copy-start
  32.1 0.7 copy-done
  32.7 2.1 %shard_map.66 = bf16[8,384,128]{2,1,0:T(8,128)(2,1)} custom-call(s32[64,64]{1,0:T(8,128)} %requested_ref.5, bf16[512,128]{1,0:T(8,128)(2,1)} %bitcast.4, bf16[2,64,512]{2,1,0:T(8,128)(2,1)} %down_ref.1, bf16[8,384,128]{2,1,0:T(8,128)(2,1)} %shard_map.65.message_ref), custom_call_target="tpu_custom_call", output_to_operand_aliasing={{}: (3, {})} | custom-call | tf_op jit(solution)/shard_map/pallas_call | solution.py:241
  34.8 18.7 %all_to_all.15.base_ref.low_ref.up_ref = bf16[8,384,128]{2,1,0:T(8,128)(2,1)} all-to-all(bf16[8,384,128]{2,1,0:T(8,128)(2,1)} %shard_map.66), channel_id=1, replica_groups=mesh['tensor'=8,'replica'=64] {'tensor'}, dimensions={0} | all-to-all | bytes 1572864 | tf_op jit(solution)/shard_map/all_to_all | solution.py:255
  53.6 2.2 %shard_map.68 = bf16[512,128]{1,0:T(8,128)(2,1)} custom-call(s32[64,64]{1,0:T(8,128)} %requested_ref.5, bf16[8,384,128]{2,1,0:T(8,128)(2,1)} %all_to_all.15.base_ref.low_ref.up_ref, bf16[8,384,128]{2,1,0:T(8,128)(2,1)} %all_to_all.15.base_ref.low_ref.up_ref), custom_call_target="tpu_custom_call" | custom-call | tf_op jit(solution)/shard_map/pallas_call | solution.py:257
  55.8 6.4 %all-to-all-start.2 = ((bf16[64,8,128]{2,1,0:T(8,128)(2,1)}), bf16[64,8,128]{2,1,0:T(8,128)(2,1)S(1)}, u32[]{:S(2)}, u32[]{:S(2)}) async-start(bf16[64,8,128]{2,1,0:T(8,128)(2,1)} %bitcast.6), calls=%async_computation.2 | async-start | bytes 262144 | tf_op jit(solution)/shard_map/all_to_all | solution.py:269
  62.2 1.8 %shard_map.67.base_ref = f32[256,128]{1,0:T(8,128)} custom-call(bf16[8,384,128]{2,1,0:T(8,128)(2,1)} %all_to_all.15.base_ref.low_ref.up_ref), custom_call_target="tpu_custom_call" | custom-call | flops 262144 | bytes 524288 | tf_op jit(solution)/shard_map/pallas_call | solution.py:271
  63.9 9.8 %all-to-all-done.2 = bf16[64,8,128]{2,1,0:T(8,128)(2,1)S(1)} async-done(((bf16[64,8,128]{2,1,0:T(8,128)(2,1)}), bf16[64,8,128]{2,1,0:T(8,128)(2,1)S(1)}, u32[]{:S(2)}, u32[]{:S(2)}) %all-to-all-start.2) | async-done | bytes 131104 | tf_op jit(solution)/shard_map/all_to_all | solution.py:269
  73.7 0.0 copy-start.1
  73.7 0.6 copy-done.1
  74.4 1.9 %shard_map.69 = bf16[64,512]{1,0:T(8,128)(2,1)} custom-call(s32[64,1]{1,0:T(8,128)} %get-tuple-element.7.goes_ref, f32[256,128]{1,0:T(8,128)} %shard_map.67.base_ref, bf16[512,128]{1,0:T(8,128)(2,1)} %bitcast.5), custom_call_target="tpu_custom_call" | custom-call | tf_op jit(solution)/shard_map/pallas_call | solution.py:283
Async XLA Ops:
  3.4 28.7 %all-to-all-start = ((bf16[64,8,128]{2,1,0:T(8,128)(2,1)}), bf16[64,8,128]{2,1,0:T(8,128)(2,1)S(1)}, u32[]{:S(2)}, u32[]{:S(2)}) async-start(bf16[64,8,128]{2,1,0:T(8,128)(2,1)} %bitcast.7), calls=%async_computation | async-start | bytes 262144 | tf_op jit(solution)/shard_map/all_to_all | solution.py:214
  32.1 0.7 copy-start
  55.8 17.9 %all-to-all-start.2 = ((bf16[64,8,128]{2,1,0:T(8,128)(2,1)}), bf16[64,8,128]{2,1,0:T(8,128)(2,1)S(1)}, u32[]{:S(2)}, u32[]{:S(2)}) async-start(bf16[64,8,128]{2,1,0:T(8,128)(2,1)} %bitcast.6), calls=%async_computation.2 | async-start | bytes 262144 | tf_op jit(solution)/shard_map/all_to_all | solution.py:269
  73.7 0.7 copy-start.1

commit v3 on v2

v3 whole, which is shorter than its diff:
```python
import functools

import jax
import jax.numpy as jnp
from jax import lax
from jax.experimental import pallas as pl
from jax.experimental.pallas import tpu as pltpu
from jax.sharding import PartitionSpec as P

adapter_scale = 2.0
most = 2
lanes = 128
block = 16
ahead = 3
bf16 = jnp.bfloat16
f32 = jnp.float32
i32 = jnp.int32


def iota(shape, axis):
    return lax.broadcasted_iota(i32, shape, axis)


def one_hot(hit):
    return jnp.where(hit, 1.0, 0.0).astype(bf16)


def times(a, b):
    return jnp.dot(a, b, preferred_element_type=f32)


def column_of(row):
    size = row.shape[1]
    square = (size, size)
    return jnp.sum(jnp.where(iota(square, 0) == iota(square, 1), row, 0), axis=1, keepdims=True)


def place_rows(present, requested_ref, slot_ref):
    group = lax.axis_index("replica")
    owners = requested_ref.shape[0]
    count = slot_ref.shape[1]
    mine = iota(requested_ref.shape, 0) == group
    entries = jnp.sum(jnp.where(mine, requested_ref[...], 0), axis=0, keepdims=True)
    named = iota((owners, count), 0) == slot_ref[...]
    before = one_hot(iota((count, count), 0) < iota((count, count), 1))
    earlier = times(one_hot(named), before)
    place = jnp.sum(jnp.where(named, earlier, 0.0), axis=0, keepdims=True)
    owner = lax.div(entries, jnp.int32(present)).astype(f32).astype(bf16)
    owner = times(jnp.broadcast_to(owner, (block, owners)), one_hot(named))[:1]
    return (owner * float(most) + place).astype(i32)


def send_kernel(present, requested_ref, slot_ref, attention_ref, sent_ref, goes_ref):
    goes = place_rows(present, requested_ref, slot_ref)
    count, features = attention_ref.shape
    chunks = features // lanes
    goes_ref[...] = goes
    target = jnp.concatenate([goes * chunks + k for k in range(chunks)], axis=1)
    stacked = jnp.concatenate(
        [attention_ref[:, k * lanes : (k + 1) * lanes] for k in range(chunks)], axis=0
    )
    pick = one_hot(iota((sent_ref.shape[0], chunks * count), 0) == target)
    sent_ref[...] = times(pick, stacked).astype(bf16)


def base_kernel(
    attention_ref, weight_ref, mine_ref, other_ref, rows, weights, arrived
):
    chips, _, columns = mine_ref.shape
    index = lax.axis_index("tensor")
    core = lax.rem(index, 2)
    chip = lax.div(index, 2)

    def fetch(slot):
        away = (0, 2, 1, 3)[slot // 2]
        device = 2 * (chip ^ away) + (core if slot % 2 else 1 - core)
        start = pl.multiple_of(device * columns, columns)
        return pltpu.make_async_copy(
            weight_ref.at[:, pl.ds(start, columns)], weights.at[slot], arrived.at[slot]
        )

    load = pltpu.make_async_copy(attention_ref, rows, arrived.at[2 * chips])
    load.start()
    for slot in range(ahead):
        fetch(slot).start()
    load.wait()
    for slot in range(2 * chips):
        fetch(slot).wait()
        if slot + ahead < 2 * chips:
            fetch(slot + ahead).start()
        base = times(rows[...], weights[slot])
        if slot % 2:
            mine_ref[slot // 2] = base
        else:
            other_ref[slot // 2] = base.astype(bf16)


def chip_kernel(mine_ref, got_ref, near_ref, far_ref):
    half = near_ref.shape[0]
    near_ref[...] = mine_ref[:half] + got_ref[:half].astype(f32)
    far_ref[...] = (mine_ref[half:] + got_ref[half:].astype(f32)).astype(bf16)


def pair_kernel(goes_ref, near_ref, got_ref, mine_ref, send_ref, pick_ref):
    mine_ref[...] = near_ref[0] + got_ref[0].astype(f32)
    send_ref[...] = (near_ref[1] + got_ref[1].astype(f32)).astype(bf16)
    rows, columns = mine_ref.shape
    chunks = columns // lanes
    goes = column_of(goes_ref[...]) * chunks
    for k in range(chunks):
        pick_ref[k * rows : (k + 1) * rows, :] = one_hot(
            iota((rows, pick_ref.shape[1]), 1) == goes + k
        )


def named_here(requested_ref, present):
    owner = lax.axis_index("replica")
    requested = requested_ref[...]
    mine = lax.div(requested, jnp.int32(present)) == owner
    return jnp.sum(
        jnp.where(mine, lax.rem(requested, jnp.int32(present)), 0), axis=1, keepdims=True
    )


def interleave(parts, backward):
    shape = (parts * block, parts * block)
    row, column = iota(shape, 0), iota(shape, 1)
    if backward:
        row, column = column, row
    return one_hot(lax.rem(row, jnp.int32(parts)) * block + lax.div(row, jnp.int32(parts)) == column)


def low_kernel(requested_ref, here_ref, down_ref, up_ref, out_ref, rows_ref):
    present, rank, features = down_ref.shape
    groups = requested_ref.shape[0]
    chunks = features // lanes
    parts = most * chunks
    order = interleave(parts, True)
    for b in range(groups // block):
        rows = times(order, here_ref[b * parts * block : (b + 1) * parts * block, :]).astype(bf16)
        for j in range(parts):
            place, k = divmod(j, chunks)
            rows_ref[
                place * groups + b * block : place * groups + (b + 1) * block,
                k * lanes : (k + 1) * lanes,
            ] = rows[j * block : (j + 1) * block, :]
    down = jnp.concatenate([down_ref[a] for a in range(present)], axis=0)
    low = lax.dot_general(
        rows_ref[...], down, (((1,), (1,)), ((), ())), preferred_element_type=f32
    )
    which = named_here(requested_ref, present)
    places = []
    for place in range(most):
        one = low[place * groups : (place + 1) * groups, :]
        places.append(
            sum(
                jnp.where(which == a, one[:, a * rank : (a + 1) * rank], 0.0)
                for a in range(present)
            )
        )
    low = jnp.concatenate(places, axis=1).astype(bf16)
    up = jnp.concatenate([up_ref[a] for a in range(present)], axis=0)
    height = up.shape[0]
    shards = out_ref.shape[0]
    columns = up.shape[1] // shards
    for peer in range(shards):
        for k in range(columns // lanes):
            out_ref[peer, k * height : (k + 1) * height, :] = up[
                :, peer * columns + k * lanes : peer * columns + (k + 1) * lanes
            ]
        out_ref[peer, out_ref.shape[1] - groups :, :] = low


def result_kernel(present, requested_ref, low_ref, up_ref, out_ref, rows_ref):
    shards, groups, width = low_ref.shape
    rank = width // most
    window = rank // shards
    depth = shards * present * window
    chunks = up_ref.shape[1] // (present * window)
    parts = most * chunks
    low = low_ref[0].astype(f32)
    for peer in range(1, shards):
        low = low + low_ref[peer].astype(f32)
    low = (adapter_scale * low).astype(bf16)
    up = jnp.concatenate(
        [
            jnp.concatenate(
                [up_ref[peer, k * present * window : (k + 1) * present * window, :] for peer in range(shards)],
                axis=0,
            )
            for k in range(chunks)
        ],
        axis=1,
    )
    which = named_here(requested_ref, present)
    source, target = iota((width, depth), 0), iota((width, depth), 1)
    shard = lax.div(target, jnp.int32(present * window))
    rank_of = shard * window + lax.rem(target, jnp.int32(window))
    adapter = iota((groups, depth), 1)
    adapter = lax.rem(lax.div(adapter, jnp.int32(window)), jnp.int32(present))
    order = interleave(parts, False)
    results = []
    for place in range(most):
        spread = times(low, one_hot(source == place * rank + rank_of)).astype(bf16)
        spread = jnp.where(adapter == which, spread, jnp.zeros_like(spread))
        results.append(times(spread, up).astype(bf16))
    for b in range(groups // block):
        for j in range(parts):
            place, k = divmod(j, chunks)
            rows_ref[j * block : (j + 1) * block, :] = results[place][
                b * block : (b + 1) * block, k * lanes : (k + 1) * lanes
            ]
        out_ref[b * parts * block : (b + 1) * parts * block, :] = times(order, rows_ref[...]).astype(bf16)


def lora_kernel(pick_ref, back_ref, out_ref):
    rows, columns = out_ref.shape
    mine = times(pick_ref[...], back_ref[...])
    for k in range(columns // lanes):
        out_ref[:, k * lanes : (k + 1) * lanes] = mine[k * rows : (k + 1) * rows, :]


def finish_kernel(lora_ref, mine_ref, got_ref, out_ref):
    out_ref[...] = (mine_ref[...] + got_ref[...].astype(f32) + lora_ref[...]).astype(bf16)


def whole(shape):
    return pl.BlockSpec(shape, lambda *_: (0,) * len(shape))


def call(kernel, out_shape, in_specs, out_specs, cost=(0, 0), limit=4, **options):
    return pl.pallas_call(
        kernel,
        grid=(1,),
        out_shape=out_shape,
        in_specs=in_specs,
        out_specs=out_specs,
        compiler_params=pltpu.CompilerParams(vmem_limit_bytes=limit << 20),
        cost_estimate=pl.CostEstimate(flops=cost[0], bytes_accessed=cost[1], transcendentals=0),
        **options,
    )


def local(attention, weight, down, up, requested, slot):
    rows, features = attention.shape
    present, rank, _ = down.shape
    window = up.shape[1]
    groups = requested.shape[0]
    shards = lax.axis_size("tensor")
    columns = weight.shape[1] // shards
    parts = most * features // lanes
    out_parts = most * columns // lanes
    chunks = columns // lanes
    shape = jax.ShapeDtypeStruct

    sent, goes = call(
        functools.partial(send_kernel, present),
        (shape((groups * parts, lanes), bf16), shape((1, rows), i32)),
        [whole(requested.shape), whole((1, rows)), whole(attention.shape)],
        (whole((groups * parts, lanes)), whole((1, rows))),
        cost=(1 << 34, 1 << 20),
        limit=56,
    )(requested, slot.reshape(1, rows), attention)
    here = lax.all_to_all(sent.reshape(groups, parts, lanes), "replica", 0, 0, tiled=True)

    chips = shards // 2
    tile = (rows, columns)
    mine, other = call(
        base_kernel,
        (shape((chips,) + tile, f32), shape((chips,) + tile, bf16)),
        [pl.BlockSpec(memory_space=pl.ANY), pl.BlockSpec(memory_space=pl.ANY)],
        (whole((chips,) + tile), whole((chips,) + tile)),
        cost=(1 << 34, 1 << 20),
        limit=10,
        scratch_shapes=[
            pltpu.VMEM((rows, features), bf16),
            pltpu.VMEM((shards, features, columns), bf16),
            pltpu.SemaphoreType.DMA((shards + 1,)),
        ],
    )(attention, weight)
    got = lax.ppermute(other, "tensor", [(i, i ^ 1) for i in range(shards)])

    up_rows = chunks * present * window
    message = call(
        low_kernel,
        shape((shards, up_rows + groups, lanes), bf16),
        [whole(requested.shape), whole((groups * parts, lanes)), whole(down.shape), whole(up.shape)],
        whole((shards, up_rows + groups, lanes)),
        cost=(6 * groups * parts * lanes * lanes, 6 * groups * parts * lanes),
        scratch_shapes=[pltpu.VMEM((most * groups, features), bf16)],
    )(requested, here.reshape(groups * parts, lanes), down, up)
    message = lax.all_to_all(message, "tensor", 0, 0, tiled=True)

    near, far = call(
        chip_kernel,
        (shape((chips // 2,) + tile, f32), shape((chips // 2,) + tile, bf16)),
        [whole((chips,) + tile), whole((chips,) + tile)],
        (whole((chips // 2,) + tile), whole((chips // 2,) + tile)),
        cost=(1 << 34, 1 << 20),
    )(mine, got)
    got = lax.ppermute(far, "tensor", [(i, i ^ 2) for i in range(shards)])

    result = call(
        functools.partial(result_kernel, present),
        shape((groups * out_parts, lanes), bf16),
        [
            whole(requested.shape),
            pl.BlockSpec((shards, groups, lanes), lambda *_: (0, up_rows // groups, 0)),
            pl.BlockSpec((shards, up_rows, lanes), lambda *_: (0, 0, 0)),
        ],
        whole((groups * out_parts, lanes)),
        cost=(6 * groups * parts * lanes * lanes, 6 * groups * parts * lanes),
        scratch_shapes=[pltpu.VMEM((out_parts * block, lanes), bf16)],
    )(requested, message, message)
    back = lax.all_to_all(result.reshape(groups, out_parts, lanes), "replica", 0, 0, tiled=True)

    mine, send, pick = call(
        pair_kernel,
        (shape(tile, f32), shape(tile, bf16), shape((chunks * rows, groups * out_parts), bf16)),
        [whole((1, rows)), whole((chips // 2,) + tile), whole((chips // 2,) + tile)],
        (whole(tile), whole(tile), whole((chunks * rows, groups * out_parts))),
        cost=(1 << 34, 1 << 20),
    )(goes, near, got)
    got = lax.ppermute(send, "tensor", [(i, i ^ 4) for i in range(shards)])

    lora = call(
        lora_kernel,
        shape(tile, f32),
        [whole((chunks * rows, groups * out_parts)), whole((groups * out_parts, lanes))],
        whole(tile),
        cost=(2 * chunks * rows * groups * out_parts * lanes, 4 * chunks * rows * groups * out_parts),
    )(pick, back.reshape(groups * out_parts, lanes))
    return call(
        finish_kernel,
        shape(tile, bf16),
        [whole(tile), whole(tile), whole(tile)],
        whole(tile),
    )(lora, mine, got)


def solution(mesh):
    in_specs = (
        P("replica", "tensor"),
        P("tensor", None),
        P("replica", None, "tensor"),
        P("replica", "tensor", None),
        P(),
        P("replica", None),
    )
    out_specs = P("replica", "tensor")
    return jax.shard_map(local, mesh=mesh, in_specs=in_specs, out_specs=out_specs, check_vma=False)
```

time: 77 us -> 66 us (0.86)
  blocking collectives: 18.7 us -> 0 us
  starting transfers between devices: 23.5 us -> 38.6 us
  Pallas kernels: 16.7 us -> 7.98 us
  waiting for transfers between devices: 14.6 us -> 16 us
    all_to_all x1 -> x0, blocking collectives: 18.7 us -> none  [local(): message = lax.all_to_all(message, 'tensor', 0, 0, tiled=True)]
    pallas_call x6 -> x8, Pallas kernels: 16.7 us -> 7.98 us  [the longest x1 2.48 us: local(): call(base_kernel, (shape((chips,) + tile, f32), shape((chips,) + tile, bf...]
    ppermute x0 -> x3, starting transfers between devices: none -> 8.61 us  [the longest x1 3.29 us: local(): got = lax.ppermute(far, 'tensor', [(i, i ^ 2) for i in range(shards)])]
    all_to_all x0 -> x1, starting transfers between devices: none -> 6.42 us  [local(): message = lax.all_to_all(message, 'tensor', 0, 0, tiled=True)]
    all_to_all x0 -> x1, waiting for transfers between devices: none -> 3.14 us  [local(): message = lax.all_to_all(message, 'tensor', 0, 0, tiled=True)]
    all_to_all x1, waiting for transfers between devices: 4.87 us -> 3.97 us  [local(): lax.all_to_all(sent.reshape(groups, parts, lanes), 'replica', 0, 0, tiled...]
    all_to_all x1, waiting for transfers between devices: 9.78 us -> 8.91 us  [local(): lax.all_to_all(result.reshape(groups, out_parts, lanes), 'replica', 0, 0,...]
    unnamed x5 -> x12, local copies, waits for them, and re-layouts: 2.66 us -> 2.2 us
  transfers between devices with their start and end apart: 2 -> 6, of which waited for: 2 -> 3; matrix products, arithmetic and copies ran while one was open for 0% -> 0% of each run, Pallas kernels for 11% -> 8%
where the time goes in v3:
time: 66 us; the launch traced here: 65 us
  starting transfers between devices  38.6 us (58%)
  waiting for transfers between devices  16 us (24%)
  Pallas kernels  7.98 us (12%)
  local copies, waits for them, and re-layouts  2.2 us (3%)
    all_to_all x1, starting transfers between devices, local(): lax.all_to_all(sent.reshape(groups, parts, lanes), 'replica', 0, 0, tiled...  17.1 us
    all_to_all x1, waiting for transfers between devices, local(): lax.all_to_all(result.reshape(groups, out_parts, lanes), 'replica', 0, 0,...  8.91 us
    all_to_all x1, starting transfers between devices, local(): lax.all_to_all(result.reshape(groups, out_parts, lanes), 'replica', 0, 0,...  6.46 us
    all_to_all x1, starting transfers between devices, local(): message = lax.all_to_all(message, 'tensor', 0, 0, tiled=True)  6.42 us
    all_to_all x1, waiting for transfers between devices, local(): lax.all_to_all(sent.reshape(groups, parts, lanes), 'replica', 0, 0, tiled...  3.97 us
    ppermute x1, starting transfers between devices, local(): got = lax.ppermute(far, 'tensor', [(i, i ^ 2) for i in range(shards)])  3.29 us
    all_to_all x1, waiting for transfers between devices, local(): message = lax.all_to_all(message, 'tensor', 0, 0, tiled=True)  3.14 us
    ppermute x1, starting transfers between devices, local(): got = lax.ppermute(other, 'tensor', [(i, i ^ 1) for i in range(shards)])  2.87 us
  transfers between devices with their start and end apart: 6, of which 3 were waited for; matrix products, arithmetic and copies ran while one was open for 0% of the time, Pallas kernels for 8%

profile of v3, /device:TPU:1, one launch (start us, length us, event | category | flops | bytes accessed | tf_op | source)
XLA Modules:
  0.0 65.0 jit_solution(6497551670961620101)
XLA Ops:
  0.0 0.0 copy-start.4
  0.0 2.0 %shard_map.64 = (bf16[512,128]{1,0:T(8,128)(2,1)}, s32[1,64]{1,0:T(1,128)}) custom-call(s32[64,64]{1,0:T(8,128)} %requested_ref.5, s32[1,64]{1,0:T(1,128)} %bitcast.8, bf16[64,512]{1,0:T(8,128)(2,1)} %attention_ref.3), custom_call_target="tpu_custom_call" | custom-call | flops 17179869184 | bytes 1048576 | tf_op jit(solution)/shard_map/pallas_call | solution.py:256
  2.0 17.1 %all-to-all-start = ((bf16[64,8,128]{2,1,0:T(8,128)(2,1)}), bf16[64,8,128]{2,1,0:T(8,128)(2,1)S(1)}, u32[]{:S(2)}, u32[]{:S(2)}) async-start(bf16[64,8,128]{2,1,0:T(8,128)(2,1)} %bitcast.7), calls=%async_computation | async-start | bytes 262144 | tf_op jit(solution)/shard_map/all_to_all | solution.py:264
  19.2 0.0 copy-done.4
  19.2 0.0 copy-start.3
  19.2 2.2 %copy-done.3 = bf16[512,4096]{1,0:T(8,128)(2,1)S(1)} copy-done((bf16[512,4096]{1,0:T(8,128)(2,1)S(1)}, bf16[512,4096]{1,0:T(8,128)(2,1)}, u32[]{:S(2)}) %copy-start.3) | copy-done | bytes 4194328
  21.4 0.0 copy-start
  21.4 0.0 copy-start.1
  21.4 0.0 copy-start.2
  21.4 2.5 %shard_map.65 = (f32[4,64,512]{2,1,0:T(8,128)S(1)}, bf16[4,64,512]{2,1,0:T(8,128)(2,1)S(1)}) custom-call(bf16[64,512]{1,0:T(8,128)(2,1)S(1)} %copy-done.4, bf16[512,4096]{1,0:T(8,128)(2,1)S(1)} %copy-done.3), custom_call_target="tpu_custom_call" | custom-call | flops 17179869184 | bytes 1048576 | tf_op jit(solution)/shard_map/pallas_call | solution.py:268
  23.8 2.9 %collective-permute-start = (bf16[4,64,512]{2,1,0:T(8,128)(2,1)S(1)}, bf16[4,64,512]{2,1,0:T(8,128)(2,1)S(1)}, u32[]{:S(2)}, u32[]{:S(2)}) collective-permute-start(bf16[4,64,512]{2,1,0:T(8,128)(2,1)S(1)} %get-tuple-element.16), channel_id=1, source_target_pairs={{0,64},{64,0},{128,192},{192,128},{256,320},{320,256},{384,448},{4... | collective-permute-start | bytes 786440 | tf_op jit(solution)/shard_map/ppermute | solution.py:281
  26.7 4.0 %all-to-all-done = bf16[64,8,128]{2,1,0:T(8,128)(2,1)S(1)} async-done(((bf16[64,8,128]{2,1,0:T(8,128)(2,1)}), bf16[64,8,128]{2,1,0:T(8,128)(2,1)S(1)}, u32[]{:S(2)}, u32[]{:S(2)}) %all-to-all-start) | async-done | bytes 131104 | tf_op jit(solution)/shard_map/all_to_all | solution.py:264
  30.7 0.0 copy-done
  30.7 0.0 copy-done.1
  30.7 0.0 copy-done.2
  30.7 1.2 %shard_map.68 = bf16[8,128,128]{2,1,0:T(8,128)(2,1)} custom-call(s32[64,64]{1,0:T(8,128)S(1)} %copy-done.2, bf16[512,128]{1,0:T(8,128)(2,1)S(1)} %bitcast.6, bf16[2,64,512]{2,1,0:T(8,128)(2,1)S(1)} %copy-done, bf16[2,8,4096]{2,1,0:T(8,128)(2,1)S(1)} %copy-done.1), custom_call_target="tpu_custom_call" | custom-call | flops 50331648 | bytes 393216 | tf_op jit(solution)/shard_map/pallas_call | solution.py:284
  31.9 6.4 %all-to-all-start.1 = ((bf16[8,128,128]{2,1,0:T(8,128)(2,1)}), bf16[8,128,128]{2,1,0:T(8,128)(2,1)S(1)}, u32[]{:S(2)}, u32[]{:S(2)}) async-start(bf16[8,128,128]{2,1,0:T(8,128)(2,1)} %shard_map.68), calls=%async_computation.1 | async-start | bytes 524288 | tf_op jit(solution)/shard_map/all_to_all | solution.py:292
  38.3 0.0 collective-permute-done.got_ref
  38.3 0.0 copy-start.5
  38.4 3.3 %collective-permute-start.1 = (bf16[2,64,512]{2,1,0:T(8,128)(2,1)S(1)}, bf16[2,64,512]{2,1,0:T(8,128)(2,1)S(1)}, u32[]{:S(2)}, u32[]{:S(2)}) collective-permute-start(bf16[2,64,512]{2,1,0:T(8,128)(2,1)S(1)} %get-tuple-element.18), channel_id=1, source_target_pairs={{0,128},{64,192},{128,0},{192,64},{256,384},{320,448},{384,256},{4... | collective-permute-start | bytes 393224 | tf_op jit(solution)/shard_map/ppermute | solution.py:301
  41.7 3.1 %all-to-all-done.1.low_ref.up_ref = bf16[8,128,128]{2,1,0:T(8,128)(2,1)S(1)} async-done(((bf16[8,128,128]{2,1,0:T(8,128)(2,1)}), bf16[8,128,128]{2,1,0:T(8,128)(2,1)S(1)}, u32[]{:S(2)}, u32[]{:S(2)}) %all-to-all-start.1) | async-done | bytes 262176 | tf_op jit(solution)/shard_map/all_to_all | solution.py:292
  44.8 1.3 %shard_map.69 = bf16[512,128]{1,0:T(8,128)(2,1)} custom-call(s32[64,64]{1,0:T(8,128)S(1)} %copy-done.2, bf16[8,128,128]{2,1,0:T(8,128)(2,1)S(1)} %all-to-all-done.1.low_ref.up_ref, bf16[8,128,128]{2,1,0:T(8,128)(2,1)S(1)} %all-to-all-done.1.low_ref.up_ref), custom_call_target="tpu_custom_call" | custom-call | flops 50331648 | bytes 393216 | tf_op jit(solution)/shard_map/pallas_call | solution.py:303
  46.1 6.5 %all-to-all-start.2 = ((bf16[64,8,128]{2,1,0:T(8,128)(2,1)}), bf16[64,8,128]{2,1,0:T(8,128)(2,1)S(1)}, u32[]{:S(2)}, u32[]{:S(2)}) async-start(bf16[64,8,128]{2,1,0:T(8,128)(2,1)} %bitcast.3), calls=%async_computation.2 | async-start | bytes 262144 | tf_op jit(solution)/shard_map/all_to_all | solution.py:315
  52.5 0.0 collective-permute-done.1.got_ref
  52.5 0.0 copy-done.5
  52.5 0.2 shard_map.67
  52.7 2.4 %collective-permute-start.2 = (bf16[64,512]{1,0:T(8,128)(2,1)S(1)}, bf16[64,512]{1,0:T(8,128)(2,1)S(1)}, u32[]{:S(2)}, u32[]{:S(2)}) collective-permute-start(bf16[64,512]{1,0:T(8,128)(2,1)S(1)} %get-tuple-element.22), channel_id=1, source_target_pairs={{0,256},{64,320},{128,384},{192,448},{256,0},{320,64},{384,128},{4... | collective-permute-start | bytes 196616 | tf_op jit(solution)/shard_map/ppermute | solution.py:324
  55.2 8.9 %all-to-all-done.2 = bf16[64,8,128]{2,1,0:T(8,128)(2,1)S(1)} async-done(((bf16[64,8,128]{2,1,0:T(8,128)(2,1)}), bf16[64,8,128]{2,1,0:T(8,128)(2,1)S(1)}, u32[]{:S(2)}, u32[]{:S(2)}) %all-to-all-start.2) | async-done | bytes 131104 | tf_op jit(solution)/shard_map/all_to_all | solution.py:315
  64.1 0.2 shard_map.70.lora_ref
  64.3 0.0 collective-permute-done.2.got_ref
  64.3 0.7 %shard_map.71 = bf16[64,512]{1,0:T(8,128)(2,1)} custom-call(f32[64,512]{1,0:T(8,128)S(1)} %shard_map.70.lora_ref, f32[64,512]{1,0:T(8,128)S(1)} %get-tuple-element.21.mine_ref, bf16[64,512]{1,0:T(8,128)(2,1)S(1)} %collective-permute-done.2.got_ref), custom_call_target="tpu_custom_call" | custom-call | tf_op jit(solution)/shard_map/pallas_call | solution.py:333
  (1 shorter events, 0.0 us)
Async XLA Ops:
  0.0 19.2 %copy-start.4 = (bf16[64,512]{1,0:T(8,128)(2,1)S(1)}, bf16[64,512]{1,0:T(8,128)(2,1)}, u32[]{:S(2)}) copy-start(bf16[64,512]{1,0:T(8,128)(2,1)} %attention_ref.3) | copy-start | bytes 196612
  2.0 28.7 %all-to-all-start = ((bf16[64,8,128]{2,1,0:T(8,128)(2,1)}), bf16[64,8,128]{2,1,0:T(8,128)(2,1)S(1)}, u32[]{:S(2)}, u32[]{:S(2)}) async-start(bf16[64,8,128]{2,1,0:T(8,128)(2,1)} %bitcast.7), calls=%async_computation | async-start | bytes 262144 | tf_op jit(solution)/shard_map/all_to_all | solution.py:264
  19.2 2.2 %copy-start.3 = (bf16[512,4096]{1,0:T(8,128)(2,1)S(1)}, bf16[512,4096]{1,0:T(8,128)(2,1)}, u32[]{:S(2)}) copy-start(bf16[512,4096]{1,0:T(8,128)(2,1)} %weight_ref.1) | copy-start | bytes 12582916
  21.4 9.3 %copy-start = (bf16[2,64,512]{2,1,0:T(8,128)(2,1)S(1)}, bf16[2,64,512]{2,1,0:T(8,128)(2,1)}, u32[]{:S(2)}) copy-start(bf16[2,64,512]{2,1,0:T(8,128)(2,1)} %down_ref.1) | copy-start | bytes 393220
  21.4 9.3 %copy-start.1 = (bf16[2,8,4096]{2,1,0:T(8,128)(2,1)S(1)}, bf16[2,8,4096]{2,1,0:T(8,128)(2,1)}, u32[]{:S(2)}) copy-start(bf16[2,8,4096]{2,1,0:T(8,128)(2,1)} %up_ref.1) | copy-start | bytes 393220
  21.4 9.3 %copy-start.2 = (s32[64,64]{1,0:T(8,128)S(1)}, s32[64,64]{1,0:T(8,128)}, u32[]{:S(2)}) copy-start(s32[64,64]{1,0:T(8,128)} %requested_ref.5) | copy-start | bytes 49156
  23.8 14.4 %collective-permute-start = (bf16[4,64,512]{2,1,0:T(8,128)(2,1)S(1)}, bf16[4,64,512]{2,1,0:T(8,128)(2,1)S(1)}, u32[]{:S(2)}, u32[]{:S(2)}) collective-permute-start(bf16[4,64,512]{2,1,0:T(8,128)(2,1)S(1)} %get-tuple-element.16), channel_id=1, source_target_pairs={{0,64},{64,0},{128,192},{192,128},{256,320},{320,256},{384,448},{4... | collective-permute-start | bytes 786440 | tf_op jit(solution)/shard_map/ppermute | solution.py:281
  31.9 12.9 %all-to-all-start.1 = ((bf16[8,128,128]{2,1,0:T(8,128)(2,1)}), bf16[8,128,128]{2,1,0:T(8,128)(2,1)S(1)}, u32[]{:S(2)}, u32[]{:S(2)}) async-start(bf16[8,128,128]{2,1,0:T(8,128)(2,1)} %shard_map.68), calls=%async_computation.1 | async-start | bytes 524288 | tf_op jit(solution)/shard_map/all_to_all | solution.py:292
  38.3 14.2 %copy-start.5 = (s32[1,64]{1,0:T(1,128)S(1)}, s32[1,64]{1,0:T(1,128)}, u32[]{:S(2)}) copy-start(s32[1,64]{1,0:T(1,128)} %get-tuple-element.14.goes_ref) | copy-start | bytes 772
  38.4 14.2 %collective-permute-start.1 = (bf16[2,64,512]{2,1,0:T(8,128)(2,1)S(1)}, bf16[2,64,512]{2,1,0:T(8,128)(2,1)S(1)}, u32[]{:S(2)}, u32[]{:S(2)}) collective-permute-start(bf16[2,64,512]{2,1,0:T(8,128)(2,1)S(1)} %get-tuple-element.18), channel_id=1, source_target_pairs={{0,128},{64,192},{128,0},{192,64},{256,384},{320,448},{384,256},{4... | collective-permute-start | bytes 393224 | tf_op jit(solution)/shard_map/ppermute | solution.py:301
  46.1 18.0 %all-to-all-start.2 = ((bf16[64,8,128]{2,1,0:T(8,128)(2,1)}), bf16[64,8,128]{2,1,0:T(8,128)(2,1)S(1)}, u32[]{:S(2)}, u32[]{:S(2)}) async-start(bf16[64,8,128]{2,1,0:T(8,128)(2,1)} %bitcast.3), calls=%async_computation.2 | async-start | bytes 262144 | tf_op jit(solution)/shard_map/all_to_all | solution.py:315
  52.7 11.6 %collective-permute-start.2 = (bf16[64,512]{1,0:T(8,128)(2,1)S(1)}, bf16[64,512]{1,0:T(8,128)(2,1)S(1)}, u32[]{:S(2)}, u32[]{:S(2)}) collective-permute-start(bf16[64,512]{1,0:T(8,128)(2,1)S(1)} %get-tuple-element.22), channel_id=1, source_target_pairs={{0,256},{64,320},{128,384},{192,448},{256,0},{320,64},{384,128},{4... | collective-permute-start | bytes 196616 | tf_op jit(solution)/shard_map/ppermute | solution.py:324

commit v4 on v3

--- a/solution.py
+++ b/solution.py
@@ -11,7 +11,7 @@
 most = 2
 lanes = 128
 block = 16
-ahead = 3
+ahead = 8
 bf16 = jnp.bfloat16
 f32 = jnp.float32
 i32 = jnp.int32
@@ -271,7 +271,7 @@
         [pl.BlockSpec(memory_space=pl.ANY), pl.BlockSpec(memory_space=pl.ANY)],
         (whole((chips,) + tile), whole((chips,) + tile)),
         cost=(1 << 34, 1 << 20),
-        limit=10,
+        limit=51,
         scratch_shapes=[
             pltpu.VMEM((rows, features), bf16),
             pltpu.VMEM((shards, features, columns), bf16),

time: 66 us -> 64.1 us (0.971)
  local copies, waits for them, and re-layouts: 2.2 us -> 0.03 us
  waiting for transfers between devices: 16 us -> 17.8 us
  starting transfers between devices: 38.6 us -> 36.9 us
    unnamed x12 -> x10, local copies, waits for them, and re-layouts: 2.2 us -> 0.03 us
    all_to_all x1, waiting for transfers between devices: 3.97 us -> 5.71 us  [local(): lax.all_to_all(sent.reshape(groups, parts, lanes), 'replica', 0, 0, tiled...]
    all_to_all x1, starting transfers between devices: 6.46 us -> 4.72 us  [local(): lax.all_to_all(result.reshape(groups, out_parts, lanes), 'replica', 0, 0,...]
  transfers between devices with their start and end apart: 6 -> 6, of which waited for: 3 -> 3; matrix products, arithmetic and copies ran while one was open for 0% -> 0% of each run, Pallas kernels for 8% -> 9%
where the time goes in v4:
time: 64.1 us; the launch traced here: 63.2 us
  starting transfers between devices  36.9 us (58%)
  waiting for transfers between devices  17.8 us (28%)
  Pallas kernels  8.35 us (13%)
    all_to_all x1, starting transfers between devices, local(): lax.all_to_all(sent.reshape(groups, parts, lanes), 'replica', 0, 0, tiled...  17.1 us
    all_to_all x1, waiting for transfers between devices, local(): lax.all_to_all(result.reshape(groups, out_parts, lanes), 'replica', 0, 0,...  8.91 us
    all_to_all x1, starting transfers between devices, local(): message = lax.all_to_all(message, 'tensor', 0, 0, tiled=True)  6.42 us
    all_to_all x1, waiting for transfers between devices, local(): lax.all_to_all(sent.reshape(groups, parts, lanes), 'replica', 0, 0, tiled...  5.71 us
    all_to_all x1, starting transfers between devices, local(): lax.all_to_all(result.reshape(groups, out_parts, lanes), 'replica', 0, 0,...  4.72 us
    ppermute x1, starting transfers between devices, local(): got = lax.ppermute(far, 'tensor', [(i, i ^ 2) for i in range(shards)])  3.29 us
    all_to_all x1, waiting for transfers between devices, local(): message = lax.all_to_all(message, 'tensor', 0, 0, tiled=True)  3.14 us
    pallas_call x1, Pallas kernels, local(): call(base_kernel, (shape((chips,) + tile, f32), shape((chips,) + tile, bf...  2.9 us
  transfers between devices with their start and end apart: 6, of which 3 were waited for; matrix products, arithmetic and copies ran while one was open for 0% of the time, Pallas kernels for 9%

profile of v4, /device:TPU:1, one launch (start us, length us, event | category | flops | bytes accessed | tf_op | source)
XLA Modules:
  0.0 63.2 jit_solution(15737981081825921824)
XLA Ops:
  0.0 0.0 copy-start.3
  0.0 2.0 %shard_map.64 = (bf16[512,128]{1,0:T(8,128)(2,1)}, s32[1,64]{1,0:T(1,128)}) custom-call(s32[64,64]{1,0:T(8,128)} %requested_ref.5, s32[1,64]{1,0:T(1,128)} %bitcast.8, bf16[64,512]{1,0:T(8,128)(2,1)} %attention_ref.3), custom_call_target="tpu_custom_call" | custom-call | flops 17179869184 | bytes 1048576 | tf_op jit(solution)/shard_map/pallas_call | solution.py:256
  2.0 17.1 %all-to-all-start = ((bf16[64,8,128]{2,1,0:T(8,128)(2,1)}), bf16[64,8,128]{2,1,0:T(8,128)(2,1)S(1)}, u32[]{:S(2)}, u32[]{:S(2)}) async-start(bf16[64,8,128]{2,1,0:T(8,128)(2,1)} %bitcast.7), calls=%async_computation | async-start | bytes 262144 | tf_op jit(solution)/shard_map/all_to_all | solution.py:264
  19.1 0.0 copy-done.3
  19.1 0.0 copy-start
  19.2 0.0 copy-start.1
  19.2 0.0 copy-start.2
  19.2 2.9 %shard_map.65 = (f32[4,64,512]{2,1,0:T(8,128)S(1)}, bf16[4,64,512]{2,1,0:T(8,128)(2,1)S(1)}) custom-call(bf16[64,512]{1,0:T(8,128)(2,1)S(1)} %copy-done.3, bf16[512,4096]{1,0:T(8,128)(2,1)} %weight_ref.1), custom_call_target="tpu_custom_call" | custom-call | flops 17179869184 | bytes 1048576 | tf_op jit(solution)/shard_map/pallas_call | solution.py:268
  22.1 2.9 %collective-permute-start = (bf16[4,64,512]{2,1,0:T(8,128)(2,1)S(1)}, bf16[4,64,512]{2,1,0:T(8,128)(2,1)S(1)}, u32[]{:S(2)}, u32[]{:S(2)}) collective-permute-start(bf16[4,64,512]{2,1,0:T(8,128)(2,1)S(1)} %get-tuple-element.16), channel_id=1, source_target_pairs={{0,64},{64,0},{128,192},{192,128},{256,320},{320,256},{384,448},{4... | collective-permute-start | bytes 786440 | tf_op jit(solution)/shard_map/ppermute | solution.py:281
  25.0 5.7 %all-to-all-done = bf16[64,8,128]{2,1,0:T(8,128)(2,1)S(1)} async-done(((bf16[64,8,128]{2,1,0:T(8,128)(2,1)}), bf16[64,8,128]{2,1,0:T(8,128)(2,1)S(1)}, u32[]{:S(2)}, u32[]{:S(2)}) %all-to-all-start) | async-done | bytes 131104 | tf_op jit(solution)/shard_map/all_to_all | solution.py:264
  30.7 0.0 copy-done
  30.7 0.0 copy-done.1
  30.7 0.0 copy-done.2
  30.7 1.2 %shard_map.68 = bf16[8,128,128]{2,1,0:T(8,128)(2,1)} custom-call(s32[64,64]{1,0:T(8,128)S(1)} %copy-done.2, bf16[512,128]{1,0:T(8,128)(2,1)S(1)} %bitcast.6, bf16[2,64,512]{2,1,0:T(8,128)(2,1)S(1)} %copy-done, bf16[2,8,4096]{2,1,0:T(8,128)(2,1)S(1)} %copy-done.1), custom_call_target="tpu_custom_call" | custom-call | flops 50331648 | bytes 393216 | tf_op jit(solution)/shard_map/pallas_call | solution.py:284
  31.8 6.4 %all-to-all-start.1 = ((bf16[8,128,128]{2,1,0:T(8,128)(2,1)}), bf16[8,128,128]{2,1,0:T(8,128)(2,1)S(1)}, u32[]{:S(2)}, u32[]{:S(2)}) async-start(bf16[8,128,128]{2,1,0:T(8,128)(2,1)} %shard_map.68), calls=%async_computation.1 | async-start | bytes 524288 | tf_op jit(solution)/shard_map/all_to_all | solution.py:292
  38.3 0.0 collective-permute-done.got_ref
  38.3 0.0 copy-start.4
  38.3 3.3 %collective-permute-start.1 = (bf16[2,64,512]{2,1,0:T(8,128)(2,1)S(1)}, bf16[2,64,512]{2,1,0:T(8,128)(2,1)S(1)}, u32[]{:S(2)}, u32[]{:S(2)}) collective-permute-start(bf16[2,64,512]{2,1,0:T(8,128)(2,1)S(1)} %get-tuple-element.18), channel_id=1, source_target_pairs={{0,128},{64,192},{128,0},{192,64},{256,384},{320,448},{384,256},{4... | collective-permute-start | bytes 393224 | tf_op jit(solution)/shard_map/ppermute | solution.py:301
  41.6 3.1 %all-to-all-done.1.low_ref.up_ref = bf16[8,128,128]{2,1,0:T(8,128)(2,1)S(1)} async-done(((bf16[8,128,128]{2,1,0:T(8,128)(2,1)}), bf16[8,128,128]{2,1,0:T(8,128)(2,1)S(1)}, u32[]{:S(2)}, u32[]{:S(2)}) %all-to-all-start.1) | async-done | bytes 262176 | tf_op jit(solution)/shard_map/all_to_all | solution.py:292
  44.8 1.2 %shard_map.69 = bf16[512,128]{1,0:T(8,128)(2,1)} custom-call(s32[64,64]{1,0:T(8,128)S(1)} %copy-done.2, bf16[8,128,128]{2,1,0:T(8,128)(2,1)S(1)} %all-to-all-done.1.low_ref.up_ref, bf16[8,128,128]{2,1,0:T(8,128)(2,1)S(1)} %all-to-all-done.1.low_ref.up_ref), custom_call_target="tpu_custom_call" | custom-call | flops 50331648 | bytes 393216 | tf_op jit(solution)/shard_map/pallas_call | solution.py:303
  46.0 4.7 %all-to-all-start.2 = ((bf16[64,8,128]{2,1,0:T(8,128)(2,1)}), bf16[64,8,128]{2,1,0:T(8,128)(2,1)S(1)}, u32[]{:S(2)}, u32[]{:S(2)}) async-start(bf16[64,8,128]{2,1,0:T(8,128)(2,1)} %bitcast.3), calls=%async_computation.2 | async-start | bytes 262144 | tf_op jit(solution)/shard_map/all_to_all | solution.py:315
  50.7 0.0 collective-permute-done.1.got_ref
  50.7 0.0 copy-done.4
  50.7 0.2 shard_map.67
  50.9 2.5 %collective-permute-start.2 = (bf16[64,512]{1,0:T(8,128)(2,1)S(1)}, bf16[64,512]{1,0:T(8,128)(2,1)S(1)}, u32[]{:S(2)}, u32[]{:S(2)}) collective-permute-start(bf16[64,512]{1,0:T(8,128)(2,1)S(1)} %get-tuple-element.22), channel_id=1, source_target_pairs={{0,256},{64,320},{128,384},{192,448},{256,0},{320,64},{384,128},{4... | collective-permute-start | bytes 196616 | tf_op jit(solution)/shard_map/ppermute | solution.py:324
  53.4 8.9 %all-to-all-done.2 = bf16[64,8,128]{2,1,0:T(8,128)(2,1)S(1)} async-done(((bf16[64,8,128]{2,1,0:T(8,128)(2,1)}), bf16[64,8,128]{2,1,0:T(8,128)(2,1)S(1)}, u32[]{:S(2)}, u32[]{:S(2)}) %all-to-all-start.2) | async-done | bytes 131104 | tf_op jit(solution)/shard_map/all_to_all | solution.py:315
  62.3 0.2 shard_map.70.lora_ref
  62.5 0.0 collective-permute-done.2.got_ref
  62.5 0.7 %shard_map.71 = bf16[64,512]{1,0:T(8,128)(2,1)} custom-call(f32[64,512]{1,0:T(8,128)S(1)} %shard_map.70.lora_ref, f32[64,512]{1,0:T(8,128)S(1)} %get-tuple-element.21.mine_ref, bf16[64,512]{1,0:T(8,128)(2,1)S(1)} %collective-permute-done.2.got_ref), custom_call_target="tpu_custom_call" | custom-call | tf_op jit(solution)/shard_map/pallas_call | solution.py:333
  (1 shorter events, 0.0 us)
Async XLA Ops:
  0.0 19.1 %copy-start.3 = (bf16[64,512]{1,0:T(8,128)(2,1)S(1)}, bf16[64,512]{1,0:T(8,128)(2,1)}, u32[]{:S(2)}) copy-start(bf16[64,512]{1,0:T(8,128)(2,1)} %attention_ref.3) | copy-start | bytes 196612
  2.0 28.7 %all-to-all-start = ((bf16[64,8,128]{2,1,0:T(8,128)(2,1)}), bf16[64,8,128]{2,1,0:T(8,128)(2,1)S(1)}, u32[]{:S(2)}, u32[]{:S(2)}) async-start(bf16[64,8,128]{2,1,0:T(8,128)(2,1)} %bitcast.7), calls=%async_computation | async-start | bytes 262144 | tf_op jit(solution)/shard_map/all_to_all | solution.py:264
  19.1 11.5 %copy-start = (bf16[2,64,512]{2,1,0:T(8,128)(2,1)S(1)}, bf16[2,64,512]{2,1,0:T(8,128)(2,1)}, u32[]{:S(2)}) copy-start(bf16[2,64,512]{2,1,0:T(8,128)(2,1)} %down_ref.1) | copy-start | bytes 393220
  19.2 11.5 %copy-start.1 = (bf16[2,8,4096]{2,1,0:T(8,128)(2,1)S(1)}, bf16[2,8,4096]{2,1,0:T(8,128)(2,1)}, u32[]{:S(2)}) copy-start(bf16[2,8,4096]{2,1,0:T(8,128)(2,1)} %up_ref.1) | copy-start | bytes 393220
  19.2 11.5 %copy-start.2 = (s32[64,64]{1,0:T(8,128)S(1)}, s32[64,64]{1,0:T(8,128)}, u32[]{:S(2)}) copy-start(s32[64,64]{1,0:T(8,128)} %requested_ref.5) | copy-start | bytes 49156
  22.1 16.2 %collective-permute-start = (bf16[4,64,512]{2,1,0:T(8,128)(2,1)S(1)}, bf16[4,64,512]{2,1,0:T(8,128)(2,1)S(1)}, u32[]{:S(2)}, u32[]{:S(2)}) collective-permute-start(bf16[4,64,512]{2,1,0:T(8,128)(2,1)S(1)} %get-tuple-element.16), channel_id=1, source_target_pairs={{0,64},{64,0},{128,192},{192,128},{256,320},{320,256},{384,448},{4... | collective-permute-start | bytes 786440 | tf_op jit(solution)/shard_map/ppermute | solution.py:281
  31.8 12.9 %all-to-all-start.1 = ((bf16[8,128,128]{2,1,0:T(8,128)(2,1)}), bf16[8,128,128]{2,1,0:T(8,128)(2,1)S(1)}, u32[]{:S(2)}, u32[]{:S(2)}) async-start(bf16[8,128,128]{2,1,0:T(8,128)(2,1)} %shard_map.68), calls=%async_computation.1 | async-start | bytes 524288 | tf_op jit(solution)/shard_map/all_to_all | solution.py:292
  38.3 12.5 %copy-start.4 = (s32[1,64]{1,0:T(1,128)S(1)}, s32[1,64]{1,0:T(1,128)}, u32[]{:S(2)}) copy-start(s32[1,64]{1,0:T(1,128)} %get-tuple-element.14.goes_ref) | copy-start | bytes 772
  38.3 12.4 %collective-permute-start.1 = (bf16[2,64,512]{2,1,0:T(8,128)(2,1)S(1)}, bf16[2,64,512]{2,1,0:T(8,128)(2,1)S(1)}, u32[]{:S(2)}, u32[]{:S(2)}) collective-permute-start(bf16[2,64,512]{2,1,0:T(8,128)(2,1)S(1)} %get-tuple-element.18), channel_id=1, source_target_pairs={{0,128},{64,192},{128,0},{192,64},{256,384},{320,448},{384,256},{4... | collective-permute-start | bytes 393224 | tf_op jit(solution)/shard_map/ppermute | solution.py:301
  46.0 16.3 %all-to-all-start.2 = ((bf16[64,8,128]{2,1,0:T(8,128)(2,1)}), bf16[64,8,128]{2,1,0:T(8,128)(2,1)S(1)}, u32[]{:S(2)}, u32[]{:S(2)}) async-start(bf16[64,8,128]{2,1,0:T(8,128)(2,1)} %bitcast.3), calls=%async_computation.2 | async-start | bytes 262144 | tf_op jit(solution)/shard_map/all_to_all | solution.py:315
  50.9 11.6 %collective-permute-start.2 = (bf16[64,512]{1,0:T(8,128)(2,1)S(1)}, bf16[64,512]{1,0:T(8,128)(2,1)S(1)}, u32[]{:S(2)}, u32[]{:S(2)}) collective-permute-start(bf16[64,512]{1,0:T(8,128)(2,1)S(1)} %get-tuple-element.22), channel_id=1, source_target_pairs={{0,256},{64,320},{128,384},{192,448},{256,0},{320,64},{384,128},{4... | collective-permute-start | bytes 196616 | tf_op jit(solution)/shard_map/ppermute | solution.py:324

commit v5 on v4

--- a/solution.py
+++ b/solution.py
@@ -1,4 +1,5 @@
 import functools
+import math
 
 import jax
 import jax.numpy as jnp
@@ -11,6 +12,7 @@
 most = 2
 lanes = 128
 block = 16
+first_z, first_y = 6, 4
 ahead = 8
 bf16 = jnp.bfloat16
 f32 = jnp.float32
@@ -27,6 +29,24 @@
 
 def times(a, b):
     return jnp.dot(a, b, preferred_element_type=f32)
+
+
+def ring_order(count):
+    side = math.isqrt(count)
+    if side * side != count:
+        return list(range(count))
+    return [
+        (first_z + z) % side * side + (first_y + y) % side for z in range(side) for y in range(side)
+    ]
+
+
+def place_in_order(device, count):
+    side = math.isqrt(count)
+    if side * side != count:
+        return device
+    z, y = lax.div(device, jnp.int32(side)), lax.rem(device, jnp.int32(side))
+    z = lax.rem(z + (side - first_z % side), jnp.int32(side))
+    return z * side + lax.rem(y + (side - first_y % side), jnp.int32(side))
 
 
 def column_of(row):
@@ -45,7 +65,7 @@
     before = one_hot(iota((count, count), 0) < iota((count, count), 1))
     earlier = times(one_hot(named), before)
     place = jnp.sum(jnp.where(named, earlier, 0.0), axis=0, keepdims=True)
-    owner = lax.div(entries, jnp.int32(present)).astype(f32).astype(bf16)
+    owner = place_in_order(lax.div(entries, jnp.int32(present)), owners).astype(f32).astype(bf16)
     owner = times(jnp.broadcast_to(owner, (block, owners)), one_hot(named))[:1]
     return (owner * float(most) + place).astype(i32)
 
@@ -64,7 +84,16 @@
 
 
 def base_kernel(
-    attention_ref, weight_ref, mine_ref, other_ref, rows, weights, arrived
+    present,
+    requested_ref,
+    attention_ref,
+    weight_ref,
+    mine_ref,
+    other_ref,
+    which_ref,
+    rows,
+    weights,
+    arrived,
 ):
     chips, _, columns = mine_ref.shape
     index = lax.axis_index("tensor")
@@ -72,7 +101,7 @@
     chip = lax.div(index, 2)
 
     def fetch(slot):
-        away = (0, 2, 1, 3)[slot // 2]
+        away = slot // 2
         device = 2 * (chip ^ away) + (core if slot % 2 else 1 - core)
         start = pl.multiple_of(device * columns, columns)
         return pltpu.make_async_copy(
@@ -83,6 +112,7 @@
     load.start()
     for slot in range(ahead):
         fetch(slot).start()
+    which_ref[...] = named_here(requested_ref, present)
     load.wait()
     for slot in range(2 * chips):
         fetch(slot).wait()
@@ -116,10 +146,14 @@
 def named_here(requested_ref, present):
     owner = lax.axis_index("replica")
     requested = requested_ref[...]
+    groups = requested.shape[0]
     mine = lax.div(requested, jnp.int32(present)) == owner
-    return jnp.sum(
+    which = jnp.sum(
         jnp.where(mine, lax.rem(requested, jnp.int32(present)), 0), axis=1, keepdims=True
     )
+    placed = iota((groups, groups), 1) == place_in_order(iota((groups, groups), 0), groups)
+    which = jnp.sum(jnp.where(placed, which, 0), axis=0, keepdims=True)
+    return column_of(which)
 
 
 def interleave(parts, backward):
@@ -130,9 +164,9 @@
     return one_hot(lax.rem(row, jnp.int32(parts)) * block + lax.div(row, jnp.int32(parts)) == column)
 
 
-def low_kernel(requested_ref, here_ref, down_ref, up_ref, out_ref, rows_ref):
+def low_kernel(which_ref, here_ref, down_ref, up_ref, out_ref, rows_ref):
     present, rank, features = down_ref.shape
-    groups = requested_ref.shape[0]
+    groups = which_ref.shape[0]
     chunks = features // lanes
     parts = most * chunks
     order = interleave(parts, True)
@@ -148,7 +182,7 @@
     low = lax.dot_general(
         rows_ref[...], down, (((1,), (1,)), ((), ())), preferred_element_type=f32
     )
-    which = named_here(requested_ref, present)
+    which = which_ref[...]
     places = []
     for place in range(most):
         one = low[place * groups : (place + 1) * groups, :]
@@ -171,7 +205,7 @@
         out_ref[peer, out_ref.shape[1] - groups :, :] = low
 
 
-def result_kernel(present, requested_ref, low_ref, up_ref, out_ref, rows_ref):
+def result_kernel(present, which_ref, low_ref, up_ref, out_ref, rows_ref):
     shards, groups, width = low_ref.shape
     rank = width // most
     window = rank // shards
@@ -192,7 +226,7 @@
         ],
         axis=1,
     )
-    which = named_here(requested_ref, present)
+    which = which_ref[...]
     source, target = iota((width, depth), 0), iota((width, depth), 1)
     shard = lax.div(target, jnp.int32(present * window))
     rank_of = shard * window + lax.rem(target, jnp.int32(window))
@@ -252,6 +286,7 @@
     out_parts = most * columns // lanes
     chunks = columns // lanes
     shape = jax.ShapeDtypeStruct
+    order = [ring_order(groups)]
 
     sent, goes = call(
         functools.partial(send_kernel, present),
@@ -261,15 +296,19 @@
         cost=(1 << 34, 1 << 20),
         limit=56,
     )(requested, slot.reshape(1, rows), attention)
-    here = lax.all_to_all(sent.reshape(groups, parts, lanes), "replica", 0, 0, tiled=True)
+    here = lax.all_to_all(sent.reshape(groups, parts, lanes), "replica", 0, 0, axis_index_groups=order, tiled=True)
 
     chips = shards // 2
     tile = (rows, columns)
-    mine, other = call(
-        base_kernel,
-        (shape((chips,) + tile, f32), shape((chips,) + tile, bf16)),
-        [pl.BlockSpec(memory_space=pl.ANY), pl.BlockSpec(memory_space=pl.ANY)],
-        (whole((chips,) + tile), whole((chips,) + tile)),
+    mine, other, which = call(
+        functools.partial(base_kernel, present),
+        (shape((chips,) + tile, f32), shape((chips,) + tile, bf16), shape((groups, 1), i32)),
+        [
+            whole(requested.shape),
+            pl.BlockSpec(memory_space=pl.ANY),
+            pl.BlockSpec(memory_space=pl.ANY),
+        ],
+        (whole((chips,) + tile), whole((chips,) + tile), whole((groups, 1))),
         cost=(1 << 34, 1 << 20),
         limit=51,
         scratch_shapes=[
@@ -277,18 +316,18 @@
             pltpu.VMEM((shards, features, columns), bf16),
             pltpu.SemaphoreType.DMA((shards + 1,)),
         ],
-    )(attention, weight)
+    )(requested, attention, weight)
     got = lax.ppermute(other, "tensor", [(i, i ^ 1) for i in range(shards)])
 
     up_rows = chunks * present * window
     message = call(
         low_kernel,
         shape((shards, up_rows + groups, lanes), bf16),
-        [whole(requested.shape), whole((groups * parts, lanes)), whole(down.shape), whole(up.shape)],
+        [whole((groups, 1)), whole((groups * parts, lanes)), whole(down.shape), whole(up.shape)],
         whole((shards, up_rows + groups, lanes)),
         cost=(6 * groups * parts * lanes * lanes, 6 * groups * parts * lanes),
         scratch_shapes=[pltpu.VMEM((most * groups, features), bf16)],
-    )(requested, here.reshape(groups * parts, lanes), down, up)
+    )(which, here.reshape(groups * parts, lanes), down, up)
     message = lax.all_to_all(message, "tensor", 0, 0, tiled=True)
 
     near, far = call(
@@ -298,21 +337,21 @@
         (whole((chips // 2,) + tile), whole((chips // 2,) + tile)),
         cost=(1 << 34, 1 << 20),
     )(mine, got)
-    got = lax.ppermute(far, "tensor", [(i, i ^ 2) for i in range(shards)])
+    got = lax.ppermute(far, "tensor", [(i, i ^ 4) for i in range(shards)])
 
     result = call(
         functools.partial(result_kernel, present),
         shape((groups * out_parts, lanes), bf16),
         [
-            whole(requested.shape),
+            whole((groups, 1)),
             pl.BlockSpec((shards, groups, lanes), lambda *_: (0, up_rows // groups, 0)),
             pl.BlockSpec((shards, up_rows, lanes), lambda *_: (0, 0, 0)),
         ],
         whole((groups * out_parts, lanes)),
         cost=(6 * groups * parts * lanes * lanes, 6 * groups * parts * lanes),
         scratch_shapes=[pltpu.VMEM((out_parts * block, lanes), bf16)],
-    )(requested, message, message)
-    back = lax.all_to_all(result.reshape(groups, out_parts, lanes), "replica", 0, 0, tiled=True)
+    )(which, message, message)
+    back = lax.all_to_all(result.reshape(groups, out_parts, lanes), "replica", 0, 0, axis_index_groups=order, tiled=True)
 
     mine, send, pick = call(
         pair_kernel,
@@ -321,7 +360,7 @@
         (whole(tile), whole(tile), whole((chunks * rows, groups * out_parts))),
         cost=(1 << 34, 1 << 20),
     )(goes, near, got)
-    got = lax.ppermute(send, "tensor", [(i, i ^ 4) for i in range(shards)])
+    got = lax.ppermute(send, "tensor", [(i, i ^ 2) for i in range(shards)])
 
     lora = call(
         lora_kernel,

time: 64.1 us -> 59.5 us (0.928)
  waiting for transfers between devices: 17.8 us -> 4.77 us
  starting transfers between devices: 36.9 us -> 45.3 us
    all_to_all x1, starting transfers between devices: 4.72 us -> 11.6 us  [local(): lax.all_to_all(result.reshape(groups, out_parts, lanes), 'replica', 0, 0,...]
    all_to_all x1, waiting for transfers between devices: 8.91 us -> 2.49 us  [local(): lax.all_to_all(result.reshape(groups, out_parts, lanes), 'replica', 0, 0,...]
    all_to_all x1, waiting for transfers between devices: 5.71 us -> 0.01 us  [local(): lax.all_to_all(sent.reshape(groups, parts, lanes), 'replica', 0, 0, axis_...]
    all_to_all x1, starting transfers between devices: 17.1 us -> 19 us  [local(): lax.all_to_all(sent.reshape(groups, parts, lanes), 'replica', 0, 0, axis_...]
    all_to_all x1, starting transfers between devices: 6.42 us -> 5.02 us  [local(): message = lax.all_to_all(message, 'tensor', 0, 0, tiled=True)]
    all_to_all x1, waiting for transfers between devices: 3.14 us -> 1.75 us  [local(): message = lax.all_to_all(message, 'tensor', 0, 0, tiled=True)]
    ppermute x2, starting transfers between devices: 5.74 us -> 6.87 us  [the longest x1 4.8 us: local(): got = lax.ppermute(far, 'tensor', [(i, i ^ 4) for i in range(shards)])]
  transfers between devices with their start and end apart: 6 -> 6, of which waited for: 3 -> 3; matrix products, arithmetic and copies ran while one was open for 0% -> 0% of each run, Pallas kernels for 9% -> 10%
where the time goes in v5:
time: 59.5 us; the launch traced here: 58.6 us
  starting transfers between devices  45.3 us (76%)
  Pallas kernels  8.35 us (14%)
  waiting for transfers between devices  4.77 us (8%)
    all_to_all x1, starting transfers between devices, local(): lax.all_to_all(sent.reshape(groups, parts, lanes), 'replica', 0, 0, axis_...  19 us
    all_to_all x1, starting transfers between devices, local(): lax.all_to_all(result.reshape(groups, out_parts, lanes), 'replica', 0, 0,...  11.6 us
    all_to_all x1, starting transfers between devices, local(): message = lax.all_to_all(message, 'tensor', 0, 0, tiled=True)  5.02 us
    ppermute x1, starting transfers between devices, local(): got = lax.ppermute(far, 'tensor', [(i, i ^ 4) for i in range(shards)])  4.8 us
    pallas_call x1, Pallas kernels, local(): call(functools.partial(base_kernel, present), (shape((chips,) + tile, f32...  2.9 us
    ppermute x1, starting transfers between devices, local(): got = lax.ppermute(other, 'tensor', [(i, i ^ 1) for i in range(shards)])  2.86 us
    all_to_all x1, waiting for transfers between devices, local(): lax.all_to_all(result.reshape(groups, out_parts, lanes), 'replica', 0, 0,...  2.49 us
    ppermute x1, starting transfers between devices, local(): got = lax.ppermute(send, 'tensor', [(i, i ^ 2) for i in range(shards)])  2.07 us
  transfers between devices with their start and end apart: 6, of which 3 were waited for; matrix products, arithmetic and copies ran while one was open for 0% of the time, Pallas kernels for 10%

profile of v5, /device:TPU:1, one launch (start us, length us, event | category | flops | bytes accessed | tf_op | source)
XLA Modules:
  0.0 58.6 jit_solution(8392981099153964006)
XLA Ops:
  0.0 0.0 copy-start.2
  0.0 0.0 copy-start.3
  0.0 2.0 %shard_map.64 = (bf16[512,128]{1,0:T(8,128)(2,1)}, s32[1,64]{1,0:T(1,128)}) custom-call(s32[64,64]{1,0:T(8,128)} %requested_ref.3, s32[1,64]{1,0:T(1,128)} %bitcast.8, bf16[64,512]{1,0:T(8,128)(2,1)} %attention_ref.3), custom_call_target="tpu_custom_call" | custom-call | flops 17179869184 | bytes 1048576 | tf_op jit(solution)/shard_map/pallas_call | solution.py:291
  2.0 19.0 %all-to-all-start = ((bf16[64,8,128]{2,1,0:T(8,128)(2,1)}), bf16[64,8,128]{2,1,0:T(8,128)(2,1)S(1)}, u32[]{:S(2)}, u32[]{:S(2)}) async-start(bf16[64,8,128]{2,1,0:T(8,128)(2,1)} %bitcast.7), calls=%async_computation | async-start | bytes 262144 | tf_op jit(solution)/shard_map/all_to_all | solution.py:299
  21.0 0.0 copy-done.2
  21.0 0.0 copy-done.3
  21.0 0.0 copy-start
  21.1 0.0 copy-start.1
  21.1 2.9 %shard_map.65 = (f32[4,64,512]{2,1,0:T(8,128)S(1)}, bf16[4,64,512]{2,1,0:T(8,128)(2,1)S(1)}, s32[64,1]{1,0:T(8,128)S(1)}) custom-call(s32[64,64]{1,0:T(8,128)S(1)} %copy-done.3, bf16[64,512]{1,0:T(8,128)(2,1)S(1)} %copy-done.2, bf16[512,4096]{1,0:T(8,128)(2,1)} %weight_ref.1), custom_call_target="tpu_custom_call" | custom-call | flops 17179869184 | bytes 1048576 | tf_op jit(solution)/shard_map/pallas_call | solution.py:303
  24.0 2.9 %collective-permute-start = (bf16[4,64,512]{2,1,0:T(8,128)(2,1)S(1)}, bf16[4,64,512]{2,1,0:T(8,128)(2,1)S(1)}, u32[]{:S(2)}, u32[]{:S(2)}) collective-permute-start(bf16[4,64,512]{2,1,0:T(8,128)(2,1)S(1)} %get-tuple-element.17), channel_id=1, source_target_pairs={{0,64},{64,0},{128,192},{192,128},{256,320},{320,256},{384,448},{4... | collective-permute-start | bytes 786440 | tf_op jit(solution)/shard_map/ppermute | solution.py:320
  26.8 0.0 all-to-all-done
  26.9 0.0 copy-done
  26.9 0.0 copy-done.1
  26.9 1.1 %shard_map.68 = bf16[8,128,128]{2,1,0:T(8,128)(2,1)} custom-call(s32[64,1]{1,0:T(8,128)S(1)} %get-tuple-element.21.which_ref, bf16[512,128]{1,0:T(8,128)(2,1)S(1)} %bitcast.6, bf16[2,64,512]{2,1,0:T(8,128)(2,1)S(1)} %copy-done, bf16[2,8,4096]{2,1,0:T(8,128)(2,1)S(1)} %copy-done.1), custom_call_target="tpu_custom_call" | custom-call | flops 50331648 | bytes 393216 | tf_op jit(solution)/shard_map/pallas_call | solution.py:323
  28.0 5.0 %all-to-all-start.1 = ((bf16[8,128,128]{2,1,0:T(8,128)(2,1)}), bf16[8,128,128]{2,1,0:T(8,128)(2,1)S(1)}, u32[]{:S(2)}, u32[]{:S(2)}) async-start(bf16[8,128,128]{2,1,0:T(8,128)(2,1)} %shard_map.68), calls=%async_computation.1 | async-start | bytes 524288 | tf_op jit(solution)/shard_map/all_to_all | solution.py:331
  33.0 0.0 collective-permute-done.got_ref
  33.0 0.0 copy-start.4
  33.0 0.1 shard_map.66
  33.1 4.8 %collective-permute-start.1 = (bf16[2,64,512]{2,1,0:T(8,128)(2,1)S(1)}, bf16[2,64,512]{2,1,0:T(8,128)(2,1)S(1)}, u32[]{:S(2)}, u32[]{:S(2)}) collective-permute-start(bf16[2,64,512]{2,1,0:T(8,128)(2,1)S(1)} %get-tuple-element.19), channel_id=1, source_target_pairs={{0,256},{64,320},{128,384},{192,448},{256,0},{320,64},{384,128},{4... | collective-permute-start | bytes 393224 | tf_op jit(solution)/shard_map/ppermute | solution.py:340
  37.9 1.8 %all-to-all-done.1.low_ref.up_ref = bf16[8,128,128]{2,1,0:T(8,128)(2,1)S(1)} async-done(((bf16[8,128,128]{2,1,0:T(8,128)(2,1)}), bf16[8,128,128]{2,1,0:T(8,128)(2,1)S(1)}, u32[]{:S(2)}, u32[]{:S(2)}) %all-to-all-start.1) | async-done | bytes 262176 | tf_op jit(solution)/shard_map/all_to_all | solution.py:331
  39.7 1.2 %shard_map.69 = bf16[512,128]{1,0:T(8,128)(2,1)} custom-call(s32[64,1]{1,0:T(8,128)S(1)} %get-tuple-element.21.which_ref, bf16[8,128,128]{2,1,0:T(8,128)(2,1)S(1)} %all-to-all-done.1.low_ref.up_ref, bf16[8,128,128]{2,1,0:T(8,128)(2,1)S(1)} %all-to-all-done.1.low_ref.up_ref), custom_call_target="tpu_custom_call" | custom-call | flops 50331648 | bytes 393216 | tf_op jit(solution)/shard_map/pallas_call | solution.py:342
  40.9 11.6 %all-to-all-start.2 = ((bf16[64,8,128]{2,1,0:T(8,128)(2,1)}), bf16[64,8,128]{2,1,0:T(8,128)(2,1)S(1)}, u32[]{:S(2)}, u32[]{:S(2)}) async-start(bf16[64,8,128]{2,1,0:T(8,128)(2,1)} %bitcast.3), calls=%async_computation.2 | async-start | bytes 262144 | tf_op jit(solution)/shard_map/all_to_all | solution.py:354
  52.5 0.0 collective-permute-done.1.got_ref
  52.5 0.0 copy-done.4
  52.5 0.2 shard_map.67
  52.7 2.1 %collective-permute-start.2 = (bf16[64,512]{1,0:T(8,128)(2,1)S(1)}, bf16[64,512]{1,0:T(8,128)(2,1)S(1)}, u32[]{:S(2)}, u32[]{:S(2)}) collective-permute-start(bf16[64,512]{1,0:T(8,128)(2,1)S(1)} %get-tuple-element.24), channel_id=1, source_target_pairs={{0,128},{64,192},{128,0},{192,64},{256,384},{320,448},{384,256},{4... | collective-permute-start | bytes 196616 | tf_op jit(solution)/shard_map/ppermute | solution.py:363
  54.8 2.5 %all-to-all-done.2 = bf16[64,8,128]{2,1,0:T(8,128)(2,1)S(1)} async-done(((bf16[64,8,128]{2,1,0:T(8,128)(2,1)}), bf16[64,8,128]{2,1,0:T(8,128)(2,1)S(1)}, u32[]{:S(2)}, u32[]{:S(2)}) %all-to-all-start.2) | async-done | bytes 131104 | tf_op jit(solution)/shard_map/all_to_all | solution.py:354
  57.2 0.2 shard_map.70.lora_ref
  57.5 0.5 collective-permute-done.2.got_ref
  58.0 0.6 %shard_map.71 = bf16[64,512]{1,0:T(8,128)(2,1)} custom-call(f32[64,512]{1,0:T(8,128)S(1)} %shard_map.70.lora_ref, f32[64,512]{1,0:T(8,128)S(1)} %get-tuple-element.23.mine_ref, bf16[64,512]{1,0:T(8,128)(2,1)S(1)} %collective-permute-done.2.got_ref), custom_call_target="tpu_custom_call" | custom-call | tf_op jit(solution)/shard_map/pallas_call | solution.py:372
Async XLA Ops:
  0.0 21.0 %copy-start.2 = (bf16[64,512]{1,0:T(8,128)(2,1)S(1)}, bf16[64,512]{1,0:T(8,128)(2,1)}, u32[]{:S(2)}) copy-start(bf16[64,512]{1,0:T(8,128)(2,1)} %attention_ref.3) | copy-start | bytes 196612
  0.0 21.0 %copy-start.3 = (s32[64,64]{1,0:T(8,128)S(1)}, s32[64,64]{1,0:T(8,128)}, u32[]{:S(2)}) copy-start(s32[64,64]{1,0:T(8,128)} %requested_ref.3) | copy-start | bytes 49156
  2.0 24.9 %all-to-all-start = ((bf16[64,8,128]{2,1,0:T(8,128)(2,1)}), bf16[64,8,128]{2,1,0:T(8,128)(2,1)S(1)}, u32[]{:S(2)}, u32[]{:S(2)}) async-start(bf16[64,8,128]{2,1,0:T(8,128)(2,1)} %bitcast.7), calls=%async_computation | async-start | bytes 262144 | tf_op jit(solution)/shard_map/all_to_all | solution.py:299
  21.0 5.8 %copy-start = (bf16[2,64,512]{2,1,0:T(8,128)(2,1)S(1)}, bf16[2,64,512]{2,1,0:T(8,128)(2,1)}, u32[]{:S(2)}) copy-start(bf16[2,64,512]{2,1,0:T(8,128)(2,1)} %down_ref.1) | copy-start | bytes 393220
  21.1 5.8 %copy-start.1 = (bf16[2,8,4096]{2,1,0:T(8,128)(2,1)S(1)}, bf16[2,8,4096]{2,1,0:T(8,128)(2,1)}, u32[]{:S(2)}) copy-start(bf16[2,8,4096]{2,1,0:T(8,128)(2,1)} %up_ref.1) | copy-start | bytes 393220
  24.0 9.1 %collective-permute-start = (bf16[4,64,512]{2,1,0:T(8,128)(2,1)S(1)}, bf16[4,64,512]{2,1,0:T(8,128)(2,1)S(1)}, u32[]{:S(2)}, u32[]{:S(2)}) collective-permute-start(bf16[4,64,512]{2,1,0:T(8,128)(2,1)S(1)} %get-tuple-element.17), channel_id=1, source_target_pairs={{0,64},{64,0},{128,192},{192,128},{256,320},{320,256},{384,448},{4... | collective-permute-start | bytes 786440 | tf_op jit(solution)/shard_map/ppermute | solution.py:320
  28.0 11.6 %all-to-all-start.1 = ((bf16[8,128,128]{2,1,0:T(8,128)(2,1)}), bf16[8,128,128]{2,1,0:T(8,128)(2,1)S(1)}, u32[]{:S(2)}, u32[]{:S(2)}) async-start(bf16[8,128,128]{2,1,0:T(8,128)(2,1)} %shard_map.68), calls=%async_computation.1 | async-start | bytes 524288 | tf_op jit(solution)/shard_map/all_to_all | solution.py:331
  33.0 19.5 %copy-start.4 = (s32[1,64]{1,0:T(1,128)S(1)}, s32[1,64]{1,0:T(1,128)}, u32[]{:S(2)}) copy-start(s32[1,64]{1,0:T(1,128)} %get-tuple-element.15.goes_ref) | copy-start | bytes 772
  33.1 19.4 %collective-permute-start.1 = (bf16[2,64,512]{2,1,0:T(8,128)(2,1)S(1)}, bf16[2,64,512]{2,1,0:T(8,128)(2,1)S(1)}, u32[]{:S(2)}, u32[]{:S(2)}) collective-permute-start(bf16[2,64,512]{2,1,0:T(8,128)(2,1)S(1)} %get-tuple-element.19), channel_id=1, source_target_pairs={{0,256},{64,320},{128,384},{192,448},{256,0},{320,64},{384,128},{4... | collective-permute-start | bytes 393224 | tf_op jit(solution)/shard_map/ppermute | solution.py:340
  40.9 16.3 %all-to-all-start.2 = ((bf16[64,8,128]{2,1,0:T(8,128)(2,1)}), bf16[64,8,128]{2,1,0:T(8,128)(2,1)S(1)}, u32[]{:S(2)}, u32[]{:S(2)}) async-start(bf16[64,8,128]{2,1,0:T(8,128)(2,1)} %bitcast.3), calls=%async_computation.2 | async-start | bytes 262144 | tf_op jit(solution)/shard_map/all_to_all | solution.py:354
  52.7 5.3 %collective-permute-start.2 = (bf16[64,512]{1,0:T(8,128)(2,1)S(1)}, bf16[64,512]{1,0:T(8,128)(2,1)S(1)}, u32[]{:S(2)}, u32[]{:S(2)}) collective-permute-start(bf16[64,512]{1,0:T(8,128)(2,1)S(1)} %get-tuple-element.24), channel_id=1, source_target_pairs={{0,128},{64,192},{128,0},{192,64},{256,384},{320,448},{384,256},{4... | collective-permute-start | bytes 196616 | tf_op jit(solution)/shard_map/ppermute | solution.py:363

commit v6 on v5

--- a/solution.py
+++ b/solution.py
@@ -13,7 +13,6 @@
 lanes = 128
 block = 16
 first_z, first_y = 6, 4
-ahead = 8
 bf16 = jnp.bfloat16
 f32 = jnp.float32
 i32 = jnp.int32
@@ -29,24 +28,31 @@
 
 def times(a, b):
     return jnp.dot(a, b, preferred_element_type=f32)
+
+
+def steps_of(side):
+    return [0] + sorted(range(1, side), key=lambda step: -min(step, side - step))
 
 
 def ring_order(count):
     side = math.isqrt(count)
     if side * side != count:
         return list(range(count))
-    return [
-        (first_z + z) % side * side + (first_y + y) % side for z in range(side) for y in range(side)
-    ]
+    steps = steps_of(side)
+    return [(first_z + z) % side * side + (first_y + y) % side for z in steps for y in steps]
 
 
 def place_in_order(device, count):
     side = math.isqrt(count)
     if side * side != count:
         return device
-    z, y = lax.div(device, jnp.int32(side)), lax.rem(device, jnp.int32(side))
-    z = lax.rem(z + (side - first_z % side), jnp.int32(side))
-    return z * side + lax.rem(y + (side - first_y % side), jnp.int32(side))
+
+    def place(position, first):
+        step = lax.rem(position + (side - first % side), jnp.int32(side))
+        return sum(jnp.where(step == one, n, 0) for n, one in enumerate(steps_of(side)))
+
+    z = place(lax.div(device, jnp.int32(side)), first_z)
+    return z * side + place(lax.rem(device, jnp.int32(side)), first_y)
 
 
 def column_of(row):
@@ -83,52 +89,53 @@
     sent_ref[...] = times(pick, stacked).astype(bf16)
 
 
-def base_kernel(
-    present,
-    requested_ref,
-    attention_ref,
-    weight_ref,
-    mine_ref,
-    other_ref,
-    which_ref,
-    rows,
-    weights,
-    arrived,
-):
-    chips, _, columns = mine_ref.shape
+def fetches(weight_ref, weights, arrived, other_core):
+    chips, _, columns = weights.shape
     index = lax.axis_index("tensor")
     core = lax.rem(index, 2)
     chip = lax.div(index, 2)
-
-    def fetch(slot):
-        away = slot // 2
-        device = 2 * (chip ^ away) + (core if slot % 2 else 1 - core)
+    copies = []
+    for away in range(chips):
+        device = 2 * (chip ^ away) + (1 - core if other_core else core)
         start = pl.multiple_of(device * columns, columns)
-        return pltpu.make_async_copy(
-            weight_ref.at[:, pl.ds(start, columns)], weights.at[slot], arrived.at[slot]
+        copies.append(
+            pltpu.make_async_copy(
+                weight_ref.at[:, pl.ds(start, columns)], weights.at[away], arrived.at[away]
+            )
         )
-
-    load = pltpu.make_async_copy(attention_ref, rows, arrived.at[2 * chips])
+    return copies
+
+
+def other_kernel(
+    present, requested_ref, attention_ref, weight_ref, other_ref, which_ref, rows, weights, arrived
+):
+    load = pltpu.make_async_copy(attention_ref, rows, arrived.at[weights.shape[0]])
     load.start()
-    for slot in range(ahead):
-        fetch(slot).start()
+    copies = fetches(weight_ref, weights, arrived, True)
+    for copy in copies:
+        copy.start()
     which_ref[...] = named_here(requested_ref, present)
     load.wait()
-    for slot in range(2 * chips):
-        fetch(slot).wait()
-        if slot + ahead < 2 * chips:
-            fetch(slot + ahead).start()
-        base = times(rows[...], weights[slot])
-        if slot % 2:
-            mine_ref[slot // 2] = base
+    for away, copy in enumerate(copies):
+        copy.wait()
+        other_ref[away] = times(rows[...], weights[away]).astype(bf16)
+
+
+def chip_kernel(attention_ref, weight_ref, got_ref, near_ref, far_ref, rows, weights, arrived):
+    load = pltpu.make_async_copy(attention_ref, rows, arrived.at[weights.shape[0]])
+    load.start()
+    copies = fetches(weight_ref, weights, arrived, False)
+    for copy in copies:
+        copy.start()
+    load.wait()
+    half = near_ref.shape[0]
+    for away, copy in enumerate(copies):
+        copy.wait()
+        total = times(rows[...], weights[away]) + got_ref[away].astype(f32)
+        if away < half:
+            near_ref[away] = total
         else:
-            other_ref[slot // 2] = base.astype(bf16)
-
-
-def chip_kernel(mine_ref, got_ref, near_ref, far_ref):
-    half = near_ref.shape[0]
-    near_ref[...] = mine_ref[:half] + got_ref[:half].astype(f32)
-    far_ref[...] = (mine_ref[half:] + got_ref[half:].astype(f32)).astype(bf16)
+            far_ref[away - half] = total.astype(bf16)
 
 
 def pair_kernel(goes_ref, near_ref, got_ref, mine_ref, send_ref, pick_ref):
@@ -233,16 +240,24 @@
     adapter = iota((groups, depth), 1)
     adapter = lax.rem(lax.div(adapter, jnp.int32(window)), jnp.int32(present))
     order = interleave(parts, False)
-    results = []
-    for place in range(most):
-        spread = times(low, one_hot(source == place * rank + rank_of)).astype(bf16)
-        spread = jnp.where(adapter == which, spread, jnp.zeros_like(spread))
-        results.append(times(spread, up).astype(bf16))
+    spread = times(
+        low,
+        jnp.concatenate([one_hot(source == place * rank + rank_of) for place in range(most)], axis=1),
+    ).astype(bf16)
+    spread = jnp.concatenate(
+        [
+            jnp.where(adapter == which, spread[:, place * depth : (place + 1) * depth], jnp.zeros((), bf16))
+            for place in range(most)
+        ],
+        axis=0,
+    )
+    results = times(spread, up).astype(bf16)
     for b in range(groups // block):
         for j in range(parts):
             place, k = divmod(j, chunks)
-            rows_ref[j * block : (j + 1) * block, :] = results[place][
-                b * block : (b + 1) * block, k * lanes : (k + 1) * lanes
+            start = place * groups + b * block
+            rows_ref[j * block : (j + 1) * block, :] = results[
+                start : start + block, k * lanes : (k + 1) * lanes
             ]
         out_ref[b * parts * block : (b + 1) * parts * block, :] = times(order, rows_ref[...]).astype(bf16)
 
@@ -300,22 +315,22 @@
 
     chips = shards // 2
     tile = (rows, columns)
-    mine, other, which = call(
-        functools.partial(base_kernel, present),
-        (shape((chips,) + tile, f32), shape((chips,) + tile, bf16), shape((groups, 1), i32)),
-        [
-            whole(requested.shape),
-            pl.BlockSpec(memory_space=pl.ANY),
-            pl.BlockSpec(memory_space=pl.ANY),
-        ],
-        (whole((chips,) + tile), whole((chips,) + tile), whole((groups, 1))),
+    anywhere = pl.BlockSpec(memory_space=pl.ANY)
+    streams = dict(
         cost=(1 << 34, 1 << 20),
         limit=51,
         scratch_shapes=[
             pltpu.VMEM((rows, features), bf16),
-            pltpu.VMEM((shards, features, columns), bf16),
-            pltpu.SemaphoreType.DMA((shards + 1,)),
+            pltpu.VMEM((chips, features, columns), bf16),
+            pltpu.SemaphoreType.DMA((chips + 1,)),
         ],
+    )
+    other, which = call(
+        functools.partial(other_kernel, present),
+        (shape((chips,) + tile, bf16), shape((groups, 1), i32)),
+        [whole(requested.shape), anywhere, anywhere],
+        (whole((chips,) + tile), whole((groups, 1))),
+        **streams,
     )(requested, attention, weight)
     got = lax.ppermute(other, "tensor", [(i, i ^ 1) for i in range(shards)])
 
@@ -333,10 +348,10 @@
     near, far = call(
         chip_kernel,
         (shape((chips // 2,) + tile, f32), shape((chips // 2,) + tile, bf16)),
-        [whole((chips,) + tile), whole((chips,) + tile)],
+        [anywhere, anywhere, whole((chips,) + tile)],
         (whole((chips // 2,) + tile), whole((chips // 2,) + tile)),
-        cost=(1 << 34, 1 << 20),
-    )(mine, got)
+        **streams,
+    )(attention, weight, got)
     got = lax.ppermute(far, "tensor", [(i, i ^ 4) for i in range(shards)])
 
     result = call(

time: 59.5 us -> 59.5 us (level)
  waiting for transfers between devices: 4.77 us -> 3.37 us
  Pallas kernels: 8.35 us -> 9.35 us
  starting transfers between devices: 45.3 us -> 46.1 us
    pallas_call x1, Pallas kernels: 0.05 us -> 2.02 us  [local(): call(chip_kernel, (shape((chips // 2,) + tile, f32), shape((chips // 2,)...]
    all_to_all x1, waiting for transfers between devices: 1.75 us -> 0.01 us  [local(): message = lax.all_to_all(message, 'tensor', 0, 0, tiled=True)]
    pallas_call x1, Pallas kernels: 2.9 us -> 2.03 us  [local(): call(functools.partial(other_kernel, present), (shape((chips,) + tile, bf...]
  transfers between devices with their start and end apart: 6 -> 6, of which waited for: 3 -> 2; matrix products, arithmetic and copies ran while one was open for 0% -> 0% of each run, Pallas kernels for 10% -> 11%
where the time goes in v6:
time: 59.5 us; the launch traced here: 59 us
  starting transfers between devices  46.1 us (77%)
  Pallas kernels  9.35 us (16%)
  waiting for transfers between devices  3.37 us (6%)
    all_to_all x1, starting transfers between devices, local(): lax.all_to_all(sent.reshape(groups, parts, lanes), 'replica', 0, 0, axis_...  19.1 us
    all_to_all x1, starting transfers between devices, local(): lax.all_to_all(result.reshape(groups, out_parts, lanes), 'replica', 0, 0,...  11.8 us
    all_to_all x1, starting transfers between devices, local(): message = lax.all_to_all(message, 'tensor', 0, 0, tiled=True)  5.28 us
    ppermute x1, starting transfers between devices, local(): got = lax.ppermute(far, 'tensor', [(i, i ^ 4) for i in range(shards)])  4.8 us
    all_to_all x1, waiting for transfers between devices, local(): lax.all_to_all(result.reshape(groups, out_parts, lanes), 'replica', 0, 0,...  2.95 us
    ppermute x1, starting transfers between devices, local(): got = lax.ppermute(other, 'tensor', [(i, i ^ 1) for i in range(shards)])  2.86 us
    ppermute x1, starting transfers between devices, local(): got = lax.ppermute(send, 'tensor', [(i, i ^ 2) for i in range(shards)])  2.19 us
    pallas_call x1, Pallas kernels, local(): call(functools.partial(other_kernel, present), (shape((chips,) + tile, bf...  2.03 us
  transfers between devices with their start and end apart: 6, of which 2 were waited for; matrix products, arithmetic and copies ran while one was open for 0% of the time, Pallas kernels for 11%

profile of v6, /device:TPU:1, one launch (start us, length us, event | category | flops | bytes accessed | tf_op | source)
XLA Modules:
  0.0 59.0 jit_solution(4469751364311687734)
XLA Ops:
  0.0 0.0 copy-start.2
  0.0 0.0 copy-start.3
  0.0 2.0 %shard_map.64 = (bf16[512,128]{1,0:T(8,128)(2,1)}, s32[1,64]{1,0:T(1,128)}) custom-call(s32[64,64]{1,0:T(8,128)} %requested_ref.3, s32[1,64]{1,0:T(1,128)} %bitcast.8, bf16[64,512]{1,0:T(8,128)(2,1)} %attention_ref.5), custom_call_target="tpu_custom_call" | custom-call | flops 17179869184 | bytes 1048576 | tf_op jit(solution)/shard_map/pallas_call | solution.py:306
  2.0 19.1 %all-to-all-start = ((bf16[64,8,128]{2,1,0:T(8,128)(2,1)}), bf16[64,8,128]{2,1,0:T(8,128)(2,1)S(1)}, u32[]{:S(2)}, u32[]{:S(2)}) async-start(bf16[64,8,128]{2,1,0:T(8,128)(2,1)} %bitcast.7), calls=%async_computation | async-start | bytes 262144 | tf_op jit(solution)/shard_map/all_to_all | solution.py:314
  21.1 0.0 copy-done.2
  21.1 0.0 copy-done.3
  21.1 0.0 copy-start
  21.2 0.0 copy-start.1
  21.2 2.0 %shard_map.65 = (bf16[4,64,512]{2,1,0:T(8,128)(2,1)S(1)}, s32[64,1]{1,0:T(8,128)S(1)}) custom-call(s32[64,64]{1,0:T(8,128)S(1)} %copy-done.3, bf16[64,512]{1,0:T(8,128)(2,1)S(1)} %copy-done.2, bf16[512,4096]{1,0:T(8,128)(2,1)} %weight_ref.3), custom_call_target="tpu_custom_call" | custom-call | flops 17179869184 | bytes 1048576 | tf_op jit(solution)/shard_map/pallas_call | solution.py:328
  23.2 2.9 %collective-permute-start = (bf16[4,64,512]{2,1,0:T(8,128)(2,1)S(1)}, bf16[4,64,512]{2,1,0:T(8,128)(2,1)S(1)}, u32[]{:S(2)}, u32[]{:S(2)}) collective-permute-start(bf16[4,64,512]{2,1,0:T(8,128)(2,1)S(1)} %get-tuple-element.15), channel_id=1, source_target_pairs={{0,64},{64,0},{128,192},{192,128},{256,320},{320,256},{384,448},{4... | collective-permute-start | bytes 786440 | tf_op jit(solution)/shard_map/ppermute | solution.py:335
  26.1 0.4 all-to-all-done
  26.5 0.0 copy-done
  26.5 0.0 copy-done.1
  26.5 1.1 %shard_map.68 = bf16[8,128,128]{2,1,0:T(8,128)(2,1)} custom-call(s32[64,1]{1,0:T(8,128)S(1)} %get-tuple-element.19.which_ref, bf16[512,128]{1,0:T(8,128)(2,1)S(1)} %bitcast.6, bf16[2,64,512]{2,1,0:T(8,128)(2,1)S(1)} %copy-done, bf16[2,8,4096]{2,1,0:T(8,128)(2,1)S(1)} %copy-done.1), custom_call_target="tpu_custom_call" | custom-call | flops 50331648 | bytes 393216 | tf_op jit(solution)/shard_map/pallas_call | solution.py:338
  27.6 5.3 %all-to-all-start.1 = ((bf16[8,128,128]{2,1,0:T(8,128)(2,1)}), bf16[8,128,128]{2,1,0:T(8,128)(2,1)S(1)}, u32[]{:S(2)}, u32[]{:S(2)}) async-start(bf16[8,128,128]{2,1,0:T(8,128)(2,1)} %shard_map.68), calls=%async_computation.1 | async-start | bytes 524288 | tf_op jit(solution)/shard_map/all_to_all | solution.py:346
  32.9 0.0 copy-start.4
  32.9 0.0 collective-permute-done.got_ref
  32.9 2.0 %shard_map.66 = (f32[2,64,512]{2,1,0:T(8,128)S(1)}, bf16[2,64,512]{2,1,0:T(8,128)(2,1)S(1)}) custom-call(bf16[64,512]{1,0:T(8,128)(2,1)S(1)} %copy-done.2, bf16[512,4096]{1,0:T(8,128)(2,1)} %weight_ref.3, bf16[4,64,512]{2,1,0:T(8,128)(2,1)S(1)} %collective-permute-done.got_ref), custom_call_target="tpu_custom_call" | custom-call | flops 17179869184 | bytes 1048576 | tf_op jit(solution)/shard_map/pallas_call | solution.py:348
  35.0 4.8 %collective-permute-start.1 = (bf16[2,64,512]{2,1,0:T(8,128)(2,1)S(1)}, bf16[2,64,512]{2,1,0:T(8,128)(2,1)S(1)}, u32[]{:S(2)}, u32[]{:S(2)}) collective-permute-start(bf16[2,64,512]{2,1,0:T(8,128)(2,1)S(1)} %get-tuple-element.17), channel_id=1, source_target_pairs={{0,256},{64,320},{128,384},{192,448},{256,0},{320,64},{384,128},{4... | collective-permute-start | bytes 393224 | tf_op jit(solution)/shard_map/ppermute | solution.py:355
  39.8 0.0 all-to-all-done.1.low_ref.up_ref
  39.8 1.1 %shard_map.69 = bf16[512,128]{1,0:T(8,128)(2,1)} custom-call(s32[64,1]{1,0:T(8,128)S(1)} %get-tuple-element.19.which_ref, bf16[8,128,128]{2,1,0:T(8,128)(2,1)S(1)} %all-to-all-done.1.low_ref.up_ref, bf16[8,128,128]{2,1,0:T(8,128)(2,1)S(1)} %all-to-all-done.1.low_ref.up_ref), custom_call_target="tpu_custom_call" | custom-call | flops 50331648 | bytes 393216 | tf_op jit(solution)/shard_map/pallas_call | solution.py:357
  40.9 11.8 %all-to-all-start.2 = ((bf16[64,8,128]{2,1,0:T(8,128)(2,1)}), bf16[64,8,128]{2,1,0:T(8,128)(2,1)S(1)}, u32[]{:S(2)}, u32[]{:S(2)}) async-start(bf16[64,8,128]{2,1,0:T(8,128)(2,1)} %bitcast.3), calls=%async_computation.2 | async-start | bytes 262144 | tf_op jit(solution)/shard_map/all_to_all | solution.py:369
  52.7 0.0 collective-permute-done.1.got_ref
  52.8 0.0 copy-done.4
  52.8 0.2 shard_map.67
  52.9 2.2 %collective-permute-start.2 = (bf16[64,512]{1,0:T(8,128)(2,1)S(1)}, bf16[64,512]{1,0:T(8,128)(2,1)S(1)}, u32[]{:S(2)}, u32[]{:S(2)}) collective-permute-start(bf16[64,512]{1,0:T(8,128)(2,1)S(1)} %get-tuple-element.22), channel_id=1, source_target_pairs={{0,128},{64,192},{128,0},{192,64},{256,384},{320,448},{384,256},{4... | collective-permute-start | bytes 196616 | tf_op jit(solution)/shard_map/ppermute | solution.py:378
  55.1 3.0 %all-to-all-done.2 = bf16[64,8,128]{2,1,0:T(8,128)(2,1)S(1)} async-done(((bf16[64,8,128]{2,1,0:T(8,128)(2,1)}), bf16[64,8,128]{2,1,0:T(8,128)(2,1)S(1)}, u32[]{:S(2)}, u32[]{:S(2)}) %all-to-all-start.2) | async-done | bytes 131104 | tf_op jit(solution)/shard_map/all_to_all | solution.py:369
  58.1 0.2 shard_map.70.lora_ref
  58.3 0.0 collective-permute-done.2.got_ref
  58.3 0.7 %shard_map.71 = bf16[64,512]{1,0:T(8,128)(2,1)} custom-call(f32[64,512]{1,0:T(8,128)S(1)} %shard_map.70.lora_ref, f32[64,512]{1,0:T(8,128)S(1)} %get-tuple-element.21.mine_ref, bf16[64,512]{1,0:T(8,128)(2,1)S(1)} %collective-permute-done.2.got_ref), custom_call_target="tpu_custom_call" | custom-call | tf_op jit(solution)/shard_map/pallas_call | solution.py:387
Async XLA Ops:
  0.0 21.1 %copy-start.2 = (bf16[64,512]{1,0:T(8,128)(2,1)S(1)}, bf16[64,512]{1,0:T(8,128)(2,1)}, u32[]{:S(2)}) copy-start(bf16[64,512]{1,0:T(8,128)(2,1)} %attention_ref.5) | copy-start | bytes 196612
  0.0 21.1 %copy-start.3 = (s32[64,64]{1,0:T(8,128)S(1)}, s32[64,64]{1,0:T(8,128)}, u32[]{:S(2)}) copy-start(s32[64,64]{1,0:T(8,128)} %requested_ref.3) | copy-start | bytes 49156
  2.0 24.5 %all-to-all-start = ((bf16[64,8,128]{2,1,0:T(8,128)(2,1)}), bf16[64,8,128]{2,1,0:T(8,128)(2,1)S(1)}, u32[]{:S(2)}, u32[]{:S(2)}) async-start(bf16[64,8,128]{2,1,0:T(8,128)(2,1)} %bitcast.7), calls=%async_computation | async-start | bytes 262144 | tf_op jit(solution)/shard_map/all_to_all | solution.py:314
  21.1 5.3 %copy-start = (bf16[2,64,512]{2,1,0:T(8,128)(2,1)S(1)}, bf16[2,64,512]{2,1,0:T(8,128)(2,1)}, u32[]{:S(2)}) copy-start(bf16[2,64,512]{2,1,0:T(8,128)(2,1)} %down_ref.1) | copy-start | bytes 393220
  21.2 5.3 %copy-start.1 = (bf16[2,8,4096]{2,1,0:T(8,128)(2,1)S(1)}, bf16[2,8,4096]{2,1,0:T(8,128)(2,1)}, u32[]{:S(2)}) copy-start(bf16[2,8,4096]{2,1,0:T(8,128)(2,1)} %up_ref.1) | copy-start | bytes 393220
  23.2 9.7 %collective-permute-start = (bf16[4,64,512]{2,1,0:T(8,128)(2,1)S(1)}, bf16[4,64,512]{2,1,0:T(8,128)(2,1)S(1)}, u32[]{:S(2)}, u32[]{:S(2)}) collective-permute-start(bf16[4,64,512]{2,1,0:T(8,128)(2,1)S(1)} %get-tuple-element.15), channel_id=1, source_target_pairs={{0,64},{64,0},{128,192},{192,128},{256,320},{320,256},{384,448},{4... | collective-permute-start | bytes 786440 | tf_op jit(solution)/shard_map/ppermute | solution.py:335
  27.6 12.1 %all-to-all-start.1 = ((bf16[8,128,128]{2,1,0:T(8,128)(2,1)}), bf16[8,128,128]{2,1,0:T(8,128)(2,1)S(1)}, u32[]{:S(2)}, u32[]{:S(2)}) async-start(bf16[8,128,128]{2,1,0:T(8,128)(2,1)} %shard_map.68), calls=%async_computation.1 | async-start | bytes 524288 | tf_op jit(solution)/shard_map/all_to_all | solution.py:346
  32.9 19.8 %copy-start.4 = (s32[1,64]{1,0:T(1,128)S(1)}, s32[1,64]{1,0:T(1,128)}, u32[]{:S(2)}) copy-start(s32[1,64]{1,0:T(1,128)} %get-tuple-element.14.goes_ref) | copy-start | bytes 772
  35.0 17.8 %collective-permute-start.1 = (bf16[2,64,512]{2,1,0:T(8,128)(2,1)S(1)}, bf16[2,64,512]{2,1,0:T(8,128)(2,1)S(1)}, u32[]{:S(2)}, u32[]{:S(2)}) collective-permute-start(bf16[2,64,512]{2,1,0:T(8,128)(2,1)S(1)} %get-tuple-element.17), channel_id=1, source_target_pairs={{0,256},{64,320},{128,384},{192,448},{256,0},{320,64},{384,128},{4... | collective-permute-start | bytes 393224 | tf_op jit(solution)/shard_map/ppermute | solution.py:355
  40.9 17.2 %all-to-all-start.2 = ((bf16[64,8,128]{2,1,0:T(8,128)(2,1)}), bf16[64,8,128]{2,1,0:T(8,128)(2,1)S(1)}, u32[]{:S(2)}, u32[]{:S(2)}) async-start(bf16[64,8,128]{2,1,0:T(8,128)(2,1)} %bitcast.3), calls=%async_computation.2 | async-start | bytes 262144 | tf_op jit(solution)/shard_map/all_to_all | solution.py:369
  52.9 5.4 %collective-permute-start.2 = (bf16[64,512]{1,0:T(8,128)(2,1)S(1)}, bf16[64,512]{1,0:T(8,128)(2,1)S(1)}, u32[]{:S(2)}, u32[]{:S(2)}) collective-permute-start(bf16[64,512]{1,0:T(8,128)(2,1)S(1)} %get-tuple-element.22), channel_id=1, source_target_pairs={{0,128},{64,192},{128,0},{192,64},{256,384},{320,448},{384,256},{4... | collective-permute-start | bytes 196616 | tf_op jit(solution)/shard_map/ppermute | solution.py:378

commit v7 on v5

--- a/solution.py
+++ b/solution.py
@@ -12,7 +12,7 @@
 most = 2
 lanes = 128
 block = 16
-first_z, first_y = 6, 4
+first_z, first_y = 6, 5
 ahead = 8
 bf16 = jnp.bfloat16
 f32 = jnp.float32
@@ -31,22 +31,29 @@
     return jnp.dot(a, b, preferred_element_type=f32)
 
 
+def steps_of(side):
+    return [0] + sorted(range(1, side), key=lambda step: -min(step, side - step))
+
+
 def ring_order(count):
     side = math.isqrt(count)
     if side * side != count:
         return list(range(count))
-    return [
-        (first_z + z) % side * side + (first_y + y) % side for z in range(side) for y in range(side)
-    ]
+    steps = steps_of(side)
+    return [(first_z + z) % side * side + (first_y + y) % side for z in steps for y in steps]
 
 
 def place_in_order(device, count):
     side = math.isqrt(count)
     if side * side != count:
         return device
-    z, y = lax.div(device, jnp.int32(side)), lax.rem(device, jnp.int32(side))
-    z = lax.rem(z + (side - first_z % side), jnp.int32(side))
-    return z * side + lax.rem(y + (side - first_y % side), jnp.int32(side))
+
+    def place(position, first):
+        step = lax.rem(position + (side - first % side), jnp.int32(side))
+        return sum(jnp.where(step == one, n, 0) for n, one in enumerate(steps_of(side)))
+
+    z = place(lax.div(device, jnp.int32(side)), first_z)
+    return z * side + place(lax.rem(device, jnp.int32(side)), first_y)
 
 
 def column_of(row):
@@ -233,16 +240,24 @@
     adapter = iota((groups, depth), 1)
     adapter = lax.rem(lax.div(adapter, jnp.int32(window)), jnp.int32(present))
     order = interleave(parts, False)
-    results = []
-    for place in range(most):
-        spread = times(low, one_hot(source == place * rank + rank_of)).astype(bf16)
-        spread = jnp.where(adapter == which, spread, jnp.zeros_like(spread))
-        results.append(times(spread, up).astype(bf16))
+    spread = times(
+        low,
+        jnp.concatenate([one_hot(source == place * rank + rank_of) for place in range(most)], axis=1),
+    ).astype(bf16)
+    spread = jnp.concatenate(
+        [
+            jnp.where(adapter == which, spread[:, place * depth : (place + 1) * depth], jnp.zeros((), bf16))
+            for place in range(most)
+        ],
+        axis=0,
+    )
+    results = times(spread, up).astype(bf16)
     for b in range(groups // block):
         for j in range(parts):
             place, k = divmod(j, chunks)
-            rows_ref[j * block : (j + 1) * block, :] = results[place][
-                b * block : (b + 1) * block, k * lanes : (k + 1) * lanes
+            start = place * groups + b * block
+            rows_ref[j * block : (j + 1) * block, :] = results[
+                start : start + block, k * lanes : (k + 1) * lanes
             ]
         out_ref[b * parts * block : (b + 1) * parts * block, :] = times(order, rows_ref[...]).astype(bf16)
 

time: 59.5 us -> 59.3 us (level)
  starting transfers between devices: 45.3 us -> 44.6 us
    all_to_all x1, waiting for transfers between devices: 2.49 us -> 3.25 us  [local(): lax.all_to_all(result.reshape(groups, out_parts, lanes), 'replica', 0, 0,...]
    all_to_all x1, starting transfers between devices: 19 us -> 18.3 us  [local(): lax.all_to_all(sent.reshape(groups, parts, lanes), 'replica', 0, 0, axis_...]
    all_to_all x1, starting transfers between devices: 11.6 us -> 10.9 us  [local(): lax.all_to_all(result.reshape(groups, out_parts, lanes), 'replica', 0, 0,...]
where the time goes in v7:
time: 59.3 us; the launch traced here: 58.2 us
  starting transfers between devices  44.6 us (75%)
  Pallas kernels  8.25 us (14%)
  waiting for transfers between devices  5.2 us (9%)
    all_to_all x1, starting transfers between devices, local(): lax.all_to_all(sent.reshape(groups, parts, lanes), 'replica', 0, 0, axis_...  18.3 us
    all_to_all x1, starting transfers between devices, local(): lax.all_to_all(result.reshape(groups, out_parts, lanes), 'replica', 0, 0,...  10.9 us
    all_to_all x1, starting transfers between devices, local(): message = lax.all_to_all(message, 'tensor', 0, 0, tiled=True)  5.6 us
    ppermute x1, starting transfers between devices, local(): got = lax.ppermute(far, 'tensor', [(i, i ^ 4) for i in range(shards)])  4.8 us
    all_to_all x1, waiting for transfers between devices, local(): lax.all_to_all(result.reshape(groups, out_parts, lanes), 'replica', 0, 0,...  3.25 us
    pallas_call x1, Pallas kernels, local(): call(functools.partial(base_kernel, present), (shape((chips,) + tile, f32...  2.9 us
    ppermute x1, starting transfers between devices, local(): got = lax.ppermute(other, 'tensor', [(i, i ^ 1) for i in range(shards)])  2.86 us
    ppermute x1, starting transfers between devices, local(): got = lax.ppermute(send, 'tensor', [(i, i ^ 2) for i in range(shards)])  2.07 us
  transfers between devices with their start and end apart: 6, of which 3 were waited for; matrix products, arithmetic and copies ran while one was open for 0% of the time, Pallas kernels for 10%

profile of v7, /device:TPU:1, one launch (start us, length us, event | category | flops | bytes accessed | tf_op | source)
XLA Modules:
  0.0 58.2 jit_solution(13890516940834258680)
XLA Ops:
  0.0 0.0 copy-start.2
  0.0 0.0 copy-start.3
  0.0 2.0 %shard_map.64 = (bf16[512,128]{1,0:T(8,128)(2,1)}, s32[1,64]{1,0:T(1,128)}) custom-call(s32[64,64]{1,0:T(8,128)} %requested_ref.3, s32[1,64]{1,0:T(1,128)} %bitcast.8, bf16[64,512]{1,0:T(8,128)(2,1)} %attention_ref.3), custom_call_target="tpu_custom_call" | custom-call | flops 17179869184 | bytes 1048576 | tf_op jit(solution)/shard_map/pallas_call | solution.py:306
  2.0 18.3 %all-to-all-start = ((bf16[64,8,128]{2,1,0:T(8,128)(2,1)}), bf16[64,8,128]{2,1,0:T(8,128)(2,1)S(1)}, u32[]{:S(2)}, u32[]{:S(2)}) async-start(bf16[64,8,128]{2,1,0:T(8,128)(2,1)} %bitcast.7), calls=%async_computation | async-start | bytes 262144 | tf_op jit(solution)/shard_map/all_to_all | solution.py:314
  20.3 0.0 copy-done.2
  20.4 0.0 copy-done.3
  20.4 0.0 copy-start
  20.4 0.0 copy-start.1
  20.4 2.9 %shard_map.65 = (f32[4,64,512]{2,1,0:T(8,128)S(1)}, bf16[4,64,512]{2,1,0:T(8,128)(2,1)S(1)}, s32[64,1]{1,0:T(8,128)S(1)}) custom-call(s32[64,64]{1,0:T(8,128)S(1)} %copy-done.3, bf16[64,512]{1,0:T(8,128)(2,1)S(1)} %copy-done.2, bf16[512,4096]{1,0:T(8,128)(2,1)} %weight_ref.1), custom_call_target="tpu_custom_call" | custom-call | flops 17179869184 | bytes 1048576 | tf_op jit(solution)/shard_map/pallas_call | solution.py:318
  23.3 2.9 %collective-permute-start = (bf16[4,64,512]{2,1,0:T(8,128)(2,1)S(1)}, bf16[4,64,512]{2,1,0:T(8,128)(2,1)S(1)}, u32[]{:S(2)}, u32[]{:S(2)}) collective-permute-start(bf16[4,64,512]{2,1,0:T(8,128)(2,1)S(1)} %get-tuple-element.17), channel_id=1, source_target_pairs={{0,64},{64,0},{128,192},{192,128},{256,320},{320,256},{384,448},{4... | collective-permute-start | bytes 786440 | tf_op jit(solution)/shard_map/ppermute | solution.py:335
  26.2 0.2 all-to-all-done
  26.4 0.0 copy-done
  26.4 0.0 copy-done.1
  26.4 1.1 %shard_map.68 = bf16[8,128,128]{2,1,0:T(8,128)(2,1)} custom-call(s32[64,1]{1,0:T(8,128)S(1)} %get-tuple-element.21.which_ref, bf16[512,128]{1,0:T(8,128)(2,1)S(1)} %bitcast.6, bf16[2,64,512]{2,1,0:T(8,128)(2,1)S(1)} %copy-done, bf16[2,8,4096]{2,1,0:T(8,128)(2,1)S(1)} %copy-done.1), custom_call_target="tpu_custom_call" | custom-call | flops 50331648 | bytes 393216 | tf_op jit(solution)/shard_map/pallas_call | solution.py:338
  27.5 5.6 %all-to-all-start.1 = ((bf16[8,128,128]{2,1,0:T(8,128)(2,1)}), bf16[8,128,128]{2,1,0:T(8,128)(2,1)S(1)}, u32[]{:S(2)}, u32[]{:S(2)}) async-start(bf16[8,128,128]{2,1,0:T(8,128)(2,1)} %shard_map.68), calls=%async_computation.1 | async-start | bytes 524288 | tf_op jit(solution)/shard_map/all_to_all | solution.py:346
  33.1 0.0 collective-permute-done.got_ref
  33.1 0.0 copy-start.4
  33.1 0.1 shard_map.66
  33.2 4.8 %collective-permute-start.1 = (bf16[2,64,512]{2,1,0:T(8,128)(2,1)S(1)}, bf16[2,64,512]{2,1,0:T(8,128)(2,1)S(1)}, u32[]{:S(2)}, u32[]{:S(2)}) collective-permute-start(bf16[2,64,512]{2,1,0:T(8,128)(2,1)S(1)} %get-tuple-element.19), channel_id=1, source_target_pairs={{0,256},{64,320},{128,384},{192,448},{256,0},{320,64},{384,128},{4... | collective-permute-start | bytes 393224 | tf_op jit(solution)/shard_map/ppermute | solution.py:355
  38.0 1.8 %all-to-all-done.1.low_ref.up_ref = bf16[8,128,128]{2,1,0:T(8,128)(2,1)S(1)} async-done(((bf16[8,128,128]{2,1,0:T(8,128)(2,1)}), bf16[8,128,128]{2,1,0:T(8,128)(2,1)S(1)}, u32[]{:S(2)}, u32[]{:S(2)}) %all-to-all-start.1) | async-done | bytes 262176 | tf_op jit(solution)/shard_map/all_to_all | solution.py:346
  39.7 1.1 %shard_map.69 = bf16[512,128]{1,0:T(8,128)(2,1)} custom-call(s32[64,1]{1,0:T(8,128)S(1)} %get-tuple-element.21.which_ref, bf16[8,128,128]{2,1,0:T(8,128)(2,1)S(1)} %all-to-all-done.1.low_ref.up_ref, bf16[8,128,128]{2,1,0:T(8,128)(2,1)S(1)} %all-to-all-done.1.low_ref.up_ref), custom_call_target="tpu_custom_call" | custom-call | flops 50331648 | bytes 393216 | tf_op jit(solution)/shard_map/pallas_call | solution.py:357
  40.9 10.9 %all-to-all-start.2 = ((bf16[64,8,128]{2,1,0:T(8,128)(2,1)}), bf16[64,8,128]{2,1,0:T(8,128)(2,1)S(1)}, u32[]{:S(2)}, u32[]{:S(2)}) async-start(bf16[64,8,128]{2,1,0:T(8,128)(2,1)} %bitcast.3), calls=%async_computation.2 | async-start | bytes 262144 | tf_op jit(solution)/shard_map/all_to_all | solution.py:369
  51.8 0.0 collective-permute-done.1.got_ref
  51.8 0.0 copy-done.4
  51.8 0.2 shard_map.67
  52.0 2.1 %collective-permute-start.2 = (bf16[64,512]{1,0:T(8,128)(2,1)S(1)}, bf16[64,512]{1,0:T(8,128)(2,1)S(1)}, u32[]{:S(2)}, u32[]{:S(2)}) collective-permute-start(bf16[64,512]{1,0:T(8,128)(2,1)S(1)} %get-tuple-element.24), channel_id=1, source_target_pairs={{0,128},{64,192},{128,0},{192,64},{256,384},{320,448},{384,256},{4... | collective-permute-start | bytes 196616 | tf_op jit(solution)/shard_map/ppermute | solution.py:378
  54.1 3.3 %all-to-all-done.2 = bf16[64,8,128]{2,1,0:T(8,128)(2,1)S(1)} async-done(((bf16[64,8,128]{2,1,0:T(8,128)(2,1)}), bf16[64,8,128]{2,1,0:T(8,128)(2,1)S(1)}, u32[]{:S(2)}, u32[]{:S(2)}) %all-to-all-start.2) | async-done | bytes 131104 | tf_op jit(solution)/shard_map/all_to_all | solution.py:369
  57.3 0.2 shard_map.70.lora_ref
  57.6 0.0 collective-permute-done.2.got_ref
  57.6 0.7 %shard_map.71 = bf16[64,512]{1,0:T(8,128)(2,1)} custom-call(f32[64,512]{1,0:T(8,128)S(1)} %shard_map.70.lora_ref, f32[64,512]{1,0:T(8,128)S(1)} %get-tuple-element.23.mine_ref, bf16[64,512]{1,0:T(8,128)(2,1)S(1)} %collective-permute-done.2.got_ref), custom_call_target="tpu_custom_call" | custom-call | tf_op jit(solution)/shard_map/pallas_call | solution.py:387
Async XLA Ops:
  0.0 20.3 %copy-start.2 = (bf16[64,512]{1,0:T(8,128)(2,1)S(1)}, bf16[64,512]{1,0:T(8,128)(2,1)}, u32[]{:S(2)}) copy-start(bf16[64,512]{1,0:T(8,128)(2,1)} %attention_ref.3) | copy-start | bytes 196612
  0.0 20.4 %copy-start.3 = (s32[64,64]{1,0:T(8,128)S(1)}, s32[64,64]{1,0:T(8,128)}, u32[]{:S(2)}) copy-start(s32[64,64]{1,0:T(8,128)} %requested_ref.3) | copy-start | bytes 49156
  2.0 24.3 %all-to-all-start = ((bf16[64,8,128]{2,1,0:T(8,128)(2,1)}), bf16[64,8,128]{2,1,0:T(8,128)(2,1)S(1)}, u32[]{:S(2)}, u32[]{:S(2)}) async-start(bf16[64,8,128]{2,1,0:T(8,128)(2,1)} %bitcast.7), calls=%async_computation | async-start | bytes 262144 | tf_op jit(solution)/shard_map/all_to_all | solution.py:314
  20.4 6.0 %copy-start = (bf16[2,64,512]{2,1,0:T(8,128)(2,1)S(1)}, bf16[2,64,512]{2,1,0:T(8,128)(2,1)}, u32[]{:S(2)}) copy-start(bf16[2,64,512]{2,1,0:T(8,128)(2,1)} %down_ref.1) | copy-start | bytes 393220
  20.4 6.0 %copy-start.1 = (bf16[2,8,4096]{2,1,0:T(8,128)(2,1)S(1)}, bf16[2,8,4096]{2,1,0:T(8,128)(2,1)}, u32[]{:S(2)}) copy-start(bf16[2,8,4096]{2,1,0:T(8,128)(2,1)} %up_ref.1) | copy-start | bytes 393220
  23.3 9.8 %collective-permute-start = (bf16[4,64,512]{2,1,0:T(8,128)(2,1)S(1)}, bf16[4,64,512]{2,1,0:T(8,128)(2,1)S(1)}, u32[]{:S(2)}, u32[]{:S(2)}) collective-permute-start(bf16[4,64,512]{2,1,0:T(8,128)(2,1)S(1)} %get-tuple-element.17), channel_id=1, source_target_pairs={{0,64},{64,0},{128,192},{192,128},{256,320},{320,256},{384,448},{4... | collective-permute-start | bytes 786440 | tf_op jit(solution)/shard_map/ppermute | solution.py:335
  27.5 12.2 %all-to-all-start.1 = ((bf16[8,128,128]{2,1,0:T(8,128)(2,1)}), bf16[8,128,128]{2,1,0:T(8,128)(2,1)S(1)}, u32[]{:S(2)}, u32[]{:S(2)}) async-start(bf16[8,128,128]{2,1,0:T(8,128)(2,1)} %shard_map.68), calls=%async_computation.1 | async-start | bytes 524288 | tf_op jit(solution)/shard_map/all_to_all | solution.py:346
  33.1 18.7 %copy-start.4 = (s32[1,64]{1,0:T(1,128)S(1)}, s32[1,64]{1,0:T(1,128)}, u32[]{:S(2)}) copy-start(s32[1,64]{1,0:T(1,128)} %get-tuple-element.15.goes_ref) | copy-start | bytes 772
  33.2 18.6 %collective-permute-start.1 = (bf16[2,64,512]{2,1,0:T(8,128)(2,1)S(1)}, bf16[2,64,512]{2,1,0:T(8,128)(2,1)S(1)}, u32[]{:S(2)}, u32[]{:S(2)}) collective-permute-start(bf16[2,64,512]{2,1,0:T(8,128)(2,1)S(1)} %get-tuple-element.19), channel_id=1, source_target_pairs={{0,256},{64,320},{128,384},{192,448},{256,0},{320,64},{384,128},{4... | collective-permute-start | bytes 393224 | tf_op jit(solution)/shard_map/ppermute | solution.py:355
  40.9 16.5 %all-to-all-start.2 = ((bf16[64,8,128]{2,1,0:T(8,128)(2,1)}), bf16[64,8,128]{2,1,0:T(8,128)(2,1)S(1)}, u32[]{:S(2)}, u32[]{:S(2)}) async-start(bf16[64,8,128]{2,1,0:T(8,128)(2,1)} %bitcast.3), calls=%async_computation.2 | async-start | bytes 262144 | tf_op jit(solution)/shard_map/all_to_all | solution.py:369
  52.0 5.6 %collective-permute-start.2 = (bf16[64,512]{1,0:T(8,128)(2,1)S(1)}, bf16[64,512]{1,0:T(8,128)(2,1)S(1)}, u32[]{:S(2)}, u32[]{:S(2)}) collective-permute-start(bf16[64,512]{1,0:T(8,128)(2,1)S(1)} %get-tuple-element.24), channel_id=1, source_target_pairs={{0,128},{64,192},{128,0},{192,64},{256,384},{320,448},{384,256},{4... | collective-permute-start | bytes 196616 | tf_op jit(solution)/shard_map/ppermute | solution.py:378

commit v8 on v7

--- a/solution.py
+++ b/solution.py
@@ -13,6 +13,7 @@
 lanes = 128
 block = 16
 first_z, first_y = 6, 5
+first_shard = 6
 ahead = 8
 bf16 = jnp.bfloat16
 f32 = jnp.float32
@@ -205,9 +206,10 @@
     shards = out_ref.shape[0]
     columns = up.shape[1] // shards
     for peer in range(shards):
+        device = (first_shard + peer) % shards
         for k in range(columns // lanes):
             out_ref[peer, k * height : (k + 1) * height, :] = up[
-                :, peer * columns + k * lanes : peer * columns + (k + 1) * lanes
+                :, device * columns + k * lanes : device * columns + (k + 1) * lanes
             ]
         out_ref[peer, out_ref.shape[1] - groups :, :] = low
 
@@ -235,7 +237,7 @@
     )
     which = which_ref[...]
     source, target = iota((width, depth), 0), iota((width, depth), 1)
-    shard = lax.div(target, jnp.int32(present * window))
+    shard = lax.rem(lax.div(target, jnp.int32(present * window)) + first_shard, jnp.int32(shards))
     rank_of = shard * window + lax.rem(target, jnp.int32(window))
     adapter = iota((groups, depth), 1)
     adapter = lax.rem(lax.div(adapter, jnp.int32(window)), jnp.int32(present))
@@ -343,7 +345,10 @@
         cost=(6 * groups * parts * lanes * lanes, 6 * groups * parts * lanes),
         scratch_shapes=[pltpu.VMEM((most * groups, features), bf16)],
     )(which, here.reshape(groups * parts, lanes), down, up)
-    message = lax.all_to_all(message, "tensor", 0, 0, tiled=True)
+    shard_order = [[(first_shard + n) % shards for n in range(shards)]]
+    message = lax.all_to_all(
+        message, "tensor", 0, 0, axis_index_groups=shard_order, tiled=True
+    )
 
     near, far = call(
         chip_kernel,

time: 59.3 us -> 58.6 us (0.988)
    ppermute x1, starting transfers between devices: 4.8 us -> 3.12 us  [local(): got = lax.ppermute(far, 'tensor', [(i, i ^ 4) for i in range(shards)])]
    all_to_all x1, starting transfers between devices: 5.6 us -> 7.03 us  [local(): lax.all_to_all(message, 'tensor', 0, 0, axis_index_groups=shard_order, ti...]
where the time goes in v8:
time: 58.6 us; the launch traced here: 57.9 us
  starting transfers between devices  44.2 us (75%)
  Pallas kernels  8.26 us (14%)
  waiting for transfers between devices  5.23 us (9%)
    all_to_all x1, starting transfers between devices, local(): lax.all_to_all(sent.reshape(groups, parts, lanes), 'replica', 0, 0, axis_...  18.3 us
    all_to_all x1, starting transfers between devices, local(): lax.all_to_all(result.reshape(groups, out_parts, lanes), 'replica', 0, 0,...  10.9 us
    all_to_all x1, starting transfers between devices, local(): lax.all_to_all(message, 'tensor', 0, 0, axis_index_groups=shard_order, ti...  7.03 us
    all_to_all x1, waiting for transfers between devices, local(): lax.all_to_all(result.reshape(groups, out_parts, lanes), 'replica', 0, 0,...  3.41 us
    ppermute x1, starting transfers between devices, local(): got = lax.ppermute(far, 'tensor', [(i, i ^ 4) for i in range(shards)])  3.12 us
    pallas_call x1, Pallas kernels, local(): call(functools.partial(base_kernel, present), (shape((chips,) + tile, f32...  2.9 us
    ppermute x1, starting transfers between devices, local(): got = lax.ppermute(other, 'tensor', [(i, i ^ 1) for i in range(shards)])  2.86 us
    pallas_call x1, Pallas kernels, local(): call(functools.partial(send_kernel, present), (shape((groups * parts, lan...  2 us
  transfers between devices with their start and end apart: 6, of which 3 were waited for; matrix products, arithmetic and copies ran while one was open for 0% of the time, Pallas kernels for 10%

profile of v8, /device:TPU:1, one launch (start us, length us, event | category | flops | bytes accessed | tf_op | source)
XLA Modules:
  0.0 57.9 jit_solution(11166995140828410279)
XLA Ops:
  0.0 0.0 copy-start.2
  0.0 0.0 copy-start.3
  0.0 2.0 %shard_map.64 = (bf16[512,128]{1,0:T(8,128)(2,1)}, s32[1,64]{1,0:T(1,128)}) custom-call(s32[64,64]{1,0:T(8,128)} %requested_ref.3, s32[1,64]{1,0:T(1,128)} %bitcast.8, bf16[64,512]{1,0:T(8,128)(2,1)} %attention_ref.3), custom_call_target="tpu_custom_call" | custom-call | flops 17179869184 | bytes 1048576 | tf_op jit(solution)/shard_map/pallas_call | solution.py:308
  2.0 18.3 %all-to-all-start = ((bf16[64,8,128]{2,1,0:T(8,128)(2,1)}), bf16[64,8,128]{2,1,0:T(8,128)(2,1)S(1)}, u32[]{:S(2)}, u32[]{:S(2)}) async-start(bf16[64,8,128]{2,1,0:T(8,128)(2,1)} %bitcast.7), calls=%async_computation | async-start | bytes 262144 | tf_op jit(solution)/shard_map/all_to_all | solution.py:316
  20.3 0.0 copy-done.2
  20.4 0.0 copy-done.3
  20.4 0.0 copy-start
  20.4 0.0 copy-start.1
  20.4 2.9 %shard_map.65 = (f32[4,64,512]{2,1,0:T(8,128)S(1)}, bf16[4,64,512]{2,1,0:T(8,128)(2,1)S(1)}, s32[64,1]{1,0:T(8,128)S(1)}) custom-call(s32[64,64]{1,0:T(8,128)S(1)} %copy-done.3, bf16[64,512]{1,0:T(8,128)(2,1)S(1)} %copy-done.2, bf16[512,4096]{1,0:T(8,128)(2,1)} %weight_ref.1), custom_call_target="tpu_custom_call" | custom-call | flops 17179869184 | bytes 1048576 | tf_op jit(solution)/shard_map/pallas_call | solution.py:320
  23.3 2.9 %collective-permute-start = (bf16[4,64,512]{2,1,0:T(8,128)(2,1)S(1)}, bf16[4,64,512]{2,1,0:T(8,128)(2,1)S(1)}, u32[]{:S(2)}, u32[]{:S(2)}) collective-permute-start(bf16[4,64,512]{2,1,0:T(8,128)(2,1)S(1)} %get-tuple-element.17), channel_id=1, source_target_pairs={{0,64},{64,0},{128,192},{192,128},{256,320},{320,256},{384,448},{4... | collective-permute-start | bytes 786440 | tf_op jit(solution)/shard_map/ppermute | solution.py:337
  26.2 0.2 all-to-all-done
  26.4 0.0 copy-done
  26.4 0.0 copy-done.1
  26.4 1.1 %shard_map.68 = bf16[8,128,128]{2,1,0:T(8,128)(2,1)} custom-call(s32[64,1]{1,0:T(8,128)S(1)} %get-tuple-element.21.which_ref, bf16[512,128]{1,0:T(8,128)(2,1)S(1)} %bitcast.6, bf16[2,64,512]{2,1,0:T(8,128)(2,1)S(1)} %copy-done, bf16[2,8,4096]{2,1,0:T(8,128)(2,1)S(1)} %copy-done.1), custom_call_target="tpu_custom_call" | custom-call | flops 50331648 | bytes 393216 | tf_op jit(solution)/shard_map/pallas_call | solution.py:340
  27.5 7.0 %all-to-all-start.1 = ((bf16[8,128,128]{2,1,0:T(8,128)(2,1)}), bf16[8,128,128]{2,1,0:T(8,128)(2,1)S(1)}, u32[]{:S(2)}, u32[]{:S(2)}) async-start(bf16[8,128,128]{2,1,0:T(8,128)(2,1)} %shard_map.68), calls=%async_computation.1 | async-start | bytes 524288 | tf_op jit(solution)/shard_map/all_to_all | solution.py:349
  34.5 0.0 collective-permute-done.got_ref
  34.5 0.0 copy-start.4
  34.5 0.1 shard_map.66
  34.6 3.1 %collective-permute-start.1 = (bf16[2,64,512]{2,1,0:T(8,128)(2,1)S(1)}, bf16[2,64,512]{2,1,0:T(8,128)(2,1)S(1)}, u32[]{:S(2)}, u32[]{:S(2)}) collective-permute-start(bf16[2,64,512]{2,1,0:T(8,128)(2,1)S(1)} %get-tuple-element.19), channel_id=1, source_target_pairs={{0,256},{64,320},{128,384},{192,448},{256,0},{320,64},{384,128},{4... | collective-permute-start | bytes 393224 | tf_op jit(solution)/shard_map/ppermute | solution.py:360
  37.7 1.6 %all-to-all-done.1.low_ref.up_ref = bf16[8,128,128]{2,1,0:T(8,128)(2,1)S(1)} async-done(((bf16[8,128,128]{2,1,0:T(8,128)(2,1)}), bf16[8,128,128]{2,1,0:T(8,128)(2,1)S(1)}, u32[]{:S(2)}, u32[]{:S(2)}) %all-to-all-start.1) | async-done | bytes 262176 | tf_op jit(solution)/shard_map/all_to_all | solution.py:349
  39.4 1.1 %shard_map.69 = bf16[512,128]{1,0:T(8,128)(2,1)} custom-call(s32[64,1]{1,0:T(8,128)S(1)} %get-tuple-element.21.which_ref, bf16[8,128,128]{2,1,0:T(8,128)(2,1)S(1)} %all-to-all-done.1.low_ref.up_ref, bf16[8,128,128]{2,1,0:T(8,128)(2,1)S(1)} %all-to-all-done.1.low_ref.up_ref), custom_call_target="tpu_custom_call" | custom-call | flops 50331648 | bytes 393216 | tf_op jit(solution)/shard_map/pallas_call | solution.py:362
  40.5 10.9 %all-to-all-start.2 = ((bf16[64,8,128]{2,1,0:T(8,128)(2,1)}), bf16[64,8,128]{2,1,0:T(8,128)(2,1)S(1)}, u32[]{:S(2)}, u32[]{:S(2)}) async-start(bf16[64,8,128]{2,1,0:T(8,128)(2,1)} %bitcast.3), calls=%async_computation.2 | async-start | bytes 262144 | tf_op jit(solution)/shard_map/all_to_all | solution.py:374
  51.5 0.0 collective-permute-done.1.got_ref
  51.5 0.0 copy-done.4
  51.5 0.2 shard_map.67
  51.6 1.9 %collective-permute-start.2 = (bf16[64,512]{1,0:T(8,128)(2,1)S(1)}, bf16[64,512]{1,0:T(8,128)(2,1)S(1)}, u32[]{:S(2)}, u32[]{:S(2)}) collective-permute-start(bf16[64,512]{1,0:T(8,128)(2,1)S(1)} %get-tuple-element.24), channel_id=1, source_target_pairs={{0,128},{64,192},{128,0},{192,64},{256,384},{320,448},{384,256},{4... | collective-permute-start | bytes 196616 | tf_op jit(solution)/shard_map/ppermute | solution.py:383
  53.6 3.4 %all-to-all-done.2 = bf16[64,8,128]{2,1,0:T(8,128)(2,1)S(1)} async-done(((bf16[64,8,128]{2,1,0:T(8,128)(2,1)}), bf16[64,8,128]{2,1,0:T(8,128)(2,1)S(1)}, u32[]{:S(2)}, u32[]{:S(2)}) %all-to-all-start.2) | async-done | bytes 131104 | tf_op jit(solution)/shard_map/all_to_all | solution.py:374
  57.0 0.2 shard_map.70.lora_ref
  57.2 0.0 collective-permute-done.2.got_ref
  57.2 0.7 %shard_map.71 = bf16[64,512]{1,0:T(8,128)(2,1)} custom-call(f32[64,512]{1,0:T(8,128)S(1)} %shard_map.70.lora_ref, f32[64,512]{1,0:T(8,128)S(1)} %get-tuple-element.23.mine_ref, bf16[64,512]{1,0:T(8,128)(2,1)S(1)} %collective-permute-done.2.got_ref), custom_call_target="tpu_custom_call" | custom-call | tf_op jit(solution)/shard_map/pallas_call | solution.py:392
Async XLA Ops:
  0.0 20.3 %copy-start.2 = (bf16[64,512]{1,0:T(8,128)(2,1)S(1)}, bf16[64,512]{1,0:T(8,128)(2,1)}, u32[]{:S(2)}) copy-start(bf16[64,512]{1,0:T(8,128)(2,1)} %attention_ref.3) | copy-start | bytes 196612
  0.0 20.4 %copy-start.3 = (s32[64,64]{1,0:T(8,128)S(1)}, s32[64,64]{1,0:T(8,128)}, u32[]{:S(2)}) copy-start(s32[64,64]{1,0:T(8,128)} %requested_ref.3) | copy-start | bytes 49156
  2.0 24.3 %all-to-all-start = ((bf16[64,8,128]{2,1,0:T(8,128)(2,1)}), bf16[64,8,128]{2,1,0:T(8,128)(2,1)S(1)}, u32[]{:S(2)}, u32[]{:S(2)}) async-start(bf16[64,8,128]{2,1,0:T(8,128)(2,1)} %bitcast.7), calls=%async_computation | async-start | bytes 262144 | tf_op jit(solution)/shard_map/all_to_all | solution.py:316
  20.4 6.0 %copy-start = (bf16[2,64,512]{2,1,0:T(8,128)(2,1)S(1)}, bf16[2,64,512]{2,1,0:T(8,128)(2,1)}, u32[]{:S(2)}) copy-start(bf16[2,64,512]{2,1,0:T(8,128)(2,1)} %down_ref.1) | copy-start | bytes 393220
  20.4 6.0 %copy-start.1 = (bf16[2,8,4096]{2,1,0:T(8,128)(2,1)S(1)}, bf16[2,8,4096]{2,1,0:T(8,128)(2,1)}, u32[]{:S(2)}) copy-start(bf16[2,8,4096]{2,1,0:T(8,128)(2,1)} %up_ref.1) | copy-start | bytes 393220
  23.3 11.2 %collective-permute-start = (bf16[4,64,512]{2,1,0:T(8,128)(2,1)S(1)}, bf16[4,64,512]{2,1,0:T(8,128)(2,1)S(1)}, u32[]{:S(2)}, u32[]{:S(2)}) collective-permute-start(bf16[4,64,512]{2,1,0:T(8,128)(2,1)S(1)} %get-tuple-element.17), channel_id=1, source_target_pairs={{0,64},{64,0},{128,192},{192,128},{256,320},{320,256},{384,448},{4... | collective-permute-start | bytes 786440 | tf_op jit(solution)/shard_map/ppermute | solution.py:337
  27.5 11.9 %all-to-all-start.1 = ((bf16[8,128,128]{2,1,0:T(8,128)(2,1)}), bf16[8,128,128]{2,1,0:T(8,128)(2,1)S(1)}, u32[]{:S(2)}, u32[]{:S(2)}) async-start(bf16[8,128,128]{2,1,0:T(8,128)(2,1)} %shard_map.68), calls=%async_computation.1 | async-start | bytes 524288 | tf_op jit(solution)/shard_map/all_to_all | solution.py:349
  34.5 16.9 %copy-start.4 = (s32[1,64]{1,0:T(1,128)S(1)}, s32[1,64]{1,0:T(1,128)}, u32[]{:S(2)}) copy-start(s32[1,64]{1,0:T(1,128)} %get-tuple-element.15.goes_ref) | copy-start | bytes 772
  34.6 16.9 %collective-permute-start.1 = (bf16[2,64,512]{2,1,0:T(8,128)(2,1)S(1)}, bf16[2,64,512]{2,1,0:T(8,128)(2,1)S(1)}, u32[]{:S(2)}, u32[]{:S(2)}) collective-permute-start(bf16[2,64,512]{2,1,0:T(8,128)(2,1)S(1)} %get-tuple-element.19), channel_id=1, source_target_pairs={{0,256},{64,320},{128,384},{192,448},{256,0},{320,64},{384,128},{4... | collective-permute-start | bytes 393224 | tf_op jit(solution)/shard_map/ppermute | solution.py:360
  40.5 16.5 %all-to-all-start.2 = ((bf16[64,8,128]{2,1,0:T(8,128)(2,1)}), bf16[64,8,128]{2,1,0:T(8,128)(2,1)S(1)}, u32[]{:S(2)}, u32[]{:S(2)}) async-start(bf16[64,8,128]{2,1,0:T(8,128)(2,1)} %bitcast.3), calls=%async_computation.2 | async-start | bytes 262144 | tf_op jit(solution)/shard_map/all_to_all | solution.py:374
  51.6 5.6 %collective-permute-start.2 = (bf16[64,512]{1,0:T(8,128)(2,1)S(1)}, bf16[64,512]{1,0:T(8,128)(2,1)S(1)}, u32[]{:S(2)}, u32[]{:S(2)}) collective-permute-start(bf16[64,512]{1,0:T(8,128)(2,1)S(1)} %get-tuple-element.24), channel_id=1, source_target_pairs={{0,128},{64,192},{128,0},{192,64},{256,384},{320,448},{384,256},{4... | collective-permute-start | bytes 196616 | tf_op jit(solution)/shard_map/ppermute | solution.py:383

commit v9 on v6

--- a/solution.py
+++ b/solution.py
@@ -12,7 +12,8 @@
 most = 2
 lanes = 128
 block = 16
-first_z, first_y = 6, 4
+first_z, first_y = 6, 5
+first_shard = 6
 bf16 = jnp.bfloat16
 f32 = jnp.float32
 i32 = jnp.int32
@@ -205,9 +206,10 @@
     shards = out_ref.shape[0]
     columns = up.shape[1] // shards
     for peer in range(shards):
+        device = (first_shard + peer) % shards
         for k in range(columns // lanes):
             out_ref[peer, k * height : (k + 1) * height, :] = up[
-                :, peer * columns + k * lanes : peer * columns + (k + 1) * lanes
+                :, device * columns + k * lanes : device * columns + (k + 1) * lanes
             ]
         out_ref[peer, out_ref.shape[1] - groups :, :] = low
 
@@ -235,7 +237,7 @@
     )
     which = which_ref[...]
     source, target = iota((width, depth), 0), iota((width, depth), 1)
-    shard = lax.div(target, jnp.int32(present * window))
+    shard = lax.rem(lax.div(target, jnp.int32(present * window)) + first_shard, jnp.int32(shards))
     rank_of = shard * window + lax.rem(target, jnp.int32(window))
     adapter = iota((groups, depth), 1)
     adapter = lax.rem(lax.div(adapter, jnp.int32(window)), jnp.int32(present))
@@ -343,7 +345,10 @@
         cost=(6 * groups * parts * lanes * lanes, 6 * groups * parts * lanes),
         scratch_shapes=[pltpu.VMEM((most * groups, features), bf16)],
     )(which, here.reshape(groups * parts, lanes), down, up)
-    message = lax.all_to_all(message, "tensor", 0, 0, tiled=True)
+    shard_order = [[(first_shard + n) % shards for n in range(shards)]]
+    message = lax.all_to_all(
+        message, "tensor", 0, 0, axis_index_groups=shard_order, tiled=True
+    )
 
     near, far = call(
         chip_kernel,

time: 59.5 us -> 59.1 us (level)
  starting transfers between devices: 46.1 us -> 44.2 us
  waiting for transfers between devices: 3.37 us -> 4.91 us
    all_to_all x1, starting transfers between devices: 5.28 us -> 7.03 us  [local(): lax.all_to_all(message, 'tensor', 0, 0, axis_index_groups=shard_order, ti...]
    ppermute x1, starting transfers between devices: 4.8 us -> 3.12 us  [local(): got = lax.ppermute(far, 'tensor', [(i, i ^ 4) for i in range(shards)])]
    all_to_all x1, starting transfers between devices: 11.8 us -> 10.9 us  [local(): lax.all_to_all(result.reshape(groups, out_parts, lanes), 'replica', 0, 0,...]
    all_to_all x1, waiting for transfers between devices: 2.95 us -> 3.84 us  [local(): lax.all_to_all(result.reshape(groups, out_parts, lanes), 'replica', 0, 0,...]
    all_to_all x1, starting transfers between devices: 19.1 us -> 18.3 us  [local(): lax.all_to_all(sent.reshape(groups, parts, lanes), 'replica', 0, 0, axis_...]
    all_to_all x1, waiting for transfers between devices: 0.41 us -> 1.06 us  [local(): lax.all_to_all(sent.reshape(groups, parts, lanes), 'replica', 0, 0, axis_...]
where the time goes in v9:
time: 59.1 us; the launch traced here: 58.6 us
  starting transfers between devices  44.2 us (75%)
  Pallas kernels  9.35 us (16%)
  waiting for transfers between devices  4.91 us (8%)
    all_to_all x1, starting transfers between devices, local(): lax.all_to_all(sent.reshape(groups, parts, lanes), 'replica', 0, 0, axis_...  18.3 us
    all_to_all x1, starting transfers between devices, local(): lax.all_to_all(result.reshape(groups, out_parts, lanes), 'replica', 0, 0,...  10.9 us
    all_to_all x1, starting transfers between devices, local(): lax.all_to_all(message, 'tensor', 0, 0, axis_index_groups=shard_order, ti...  7.03 us
    all_to_all x1, waiting for transfers between devices, local(): lax.all_to_all(result.reshape(groups, out_parts, lanes), 'replica', 0, 0,...  3.84 us
    ppermute x1, starting transfers between devices, local(): got = lax.ppermute(far, 'tensor', [(i, i ^ 4) for i in range(shards)])  3.12 us
    ppermute x1, starting transfers between devices, local(): got = lax.ppermute(other, 'tensor', [(i, i ^ 1) for i in range(shards)])  2.86 us
    pallas_call x1, Pallas kernels, local(): call(functools.partial(other_kernel, present), (shape((chips,) + tile, bf...  2.03 us
    pallas_call x1, Pallas kernels, local(): call(chip_kernel, (shape((chips // 2,) + tile, f32), shape((chips // 2,)...  2.02 us
  transfers between devices with their start and end apart: 6, of which 2 were waited for; matrix products, arithmetic and copies ran while one was open for 0% of the time, Pallas kernels for 11%

profile of v9, /device:TPU:1, one launch (start us, length us, event | category | flops | bytes accessed | tf_op | source)
XLA Modules:
  0.0 58.6 jit_solution(1699150479950594092)
XLA Ops:
  0.0 0.0 copy-start.2
  0.0 0.0 copy-start.3
  0.0 2.0 %shard_map.64 = (bf16[512,128]{1,0:T(8,128)(2,1)}, s32[1,64]{1,0:T(1,128)}) custom-call(s32[64,64]{1,0:T(8,128)} %requested_ref.3, s32[1,64]{1,0:T(1,128)} %bitcast.8, bf16[64,512]{1,0:T(8,128)(2,1)} %attention_ref.5), custom_call_target="tpu_custom_call" | custom-call | flops 17179869184 | bytes 1048576 | tf_op jit(solution)/shard_map/pallas_call | solution.py:308
  2.0 18.3 %all-to-all-start = ((bf16[64,8,128]{2,1,0:T(8,128)(2,1)}), bf16[64,8,128]{2,1,0:T(8,128)(2,1)S(1)}, u32[]{:S(2)}, u32[]{:S(2)}) async-start(bf16[64,8,128]{2,1,0:T(8,128)(2,1)} %bitcast.7), calls=%async_computation | async-start | bytes 262144 | tf_op jit(solution)/shard_map/all_to_all | solution.py:316
  20.3 0.0 copy-done.2
  20.4 0.0 copy-done.3
  20.4 0.0 copy-start
  20.4 0.0 copy-start.1
  20.4 2.0 %shard_map.65 = (bf16[4,64,512]{2,1,0:T(8,128)(2,1)S(1)}, s32[64,1]{1,0:T(8,128)S(1)}) custom-call(s32[64,64]{1,0:T(8,128)S(1)} %copy-done.3, bf16[64,512]{1,0:T(8,128)(2,1)S(1)} %copy-done.2, bf16[512,4096]{1,0:T(8,128)(2,1)} %weight_ref.3), custom_call_target="tpu_custom_call" | custom-call | flops 17179869184 | bytes 1048576 | tf_op jit(solution)/shard_map/pallas_call | solution.py:330
  22.4 2.9 %collective-permute-start = (bf16[4,64,512]{2,1,0:T(8,128)(2,1)S(1)}, bf16[4,64,512]{2,1,0:T(8,128)(2,1)S(1)}, u32[]{:S(2)}, u32[]{:S(2)}) collective-permute-start(bf16[4,64,512]{2,1,0:T(8,128)(2,1)S(1)} %get-tuple-element.15), channel_id=1, source_target_pairs={{0,64},{64,0},{128,192},{192,128},{256,320},{320,256},{384,448},{4... | collective-permute-start | bytes 786440 | tf_op jit(solution)/shard_map/ppermute | solution.py:337
  25.3 1.1 %all-to-all-done = bf16[64,8,128]{2,1,0:T(8,128)(2,1)S(1)} async-done(((bf16[64,8,128]{2,1,0:T(8,128)(2,1)}), bf16[64,8,128]{2,1,0:T(8,128)(2,1)S(1)}, u32[]{:S(2)}, u32[]{:S(2)}) %all-to-all-start) | async-done | bytes 131104 | tf_op jit(solution)/shard_map/all_to_all | solution.py:316
  26.4 0.0 copy-done
  26.4 0.0 copy-done.1
  26.4 1.1 %shard_map.68 = bf16[8,128,128]{2,1,0:T(8,128)(2,1)} custom-call(s32[64,1]{1,0:T(8,128)S(1)} %get-tuple-element.19.which_ref, bf16[512,128]{1,0:T(8,128)(2,1)S(1)} %bitcast.6, bf16[2,64,512]{2,1,0:T(8,128)(2,1)S(1)} %copy-done, bf16[2,8,4096]{2,1,0:T(8,128)(2,1)S(1)} %copy-done.1), custom_call_target="tpu_custom_call" | custom-call | flops 50331648 | bytes 393216 | tf_op jit(solution)/shard_map/pallas_call | solution.py:340
  27.5 7.0 %all-to-all-start.1 = ((bf16[8,128,128]{2,1,0:T(8,128)(2,1)}), bf16[8,128,128]{2,1,0:T(8,128)(2,1)S(1)}, u32[]{:S(2)}, u32[]{:S(2)}) async-start(bf16[8,128,128]{2,1,0:T(8,128)(2,1)} %shard_map.68), calls=%async_computation.1 | async-start | bytes 524288 | tf_op jit(solution)/shard_map/all_to_all | solution.py:349
  34.5 0.0 copy-start.4
  34.5 0.0 collective-permute-done.got_ref
  34.5 2.0 %shard_map.66 = (f32[2,64,512]{2,1,0:T(8,128)S(1)}, bf16[2,64,512]{2,1,0:T(8,128)(2,1)S(1)}) custom-call(bf16[64,512]{1,0:T(8,128)(2,1)S(1)} %copy-done.2, bf16[512,4096]{1,0:T(8,128)(2,1)} %weight_ref.3, bf16[4,64,512]{2,1,0:T(8,128)(2,1)S(1)} %collective-permute-done.got_ref), custom_call_target="tpu_custom_call" | custom-call | flops 17179869184 | bytes 1048576 | tf_op jit(solution)/shard_map/pallas_call | solution.py:353
  36.6 3.1 %collective-permute-start.1 = (bf16[2,64,512]{2,1,0:T(8,128)(2,1)S(1)}, bf16[2,64,512]{2,1,0:T(8,128)(2,1)S(1)}, u32[]{:S(2)}, u32[]{:S(2)}) collective-permute-start(bf16[2,64,512]{2,1,0:T(8,128)(2,1)S(1)} %get-tuple-element.17), channel_id=1, source_target_pairs={{0,256},{64,320},{128,384},{192,448},{256,0},{320,64},{384,128},{4... | collective-permute-start | bytes 393224 | tf_op jit(solution)/shard_map/ppermute | solution.py:360
  39.7 0.0 all-to-all-done.1.low_ref.up_ref
  39.7 1.1 %shard_map.69 = bf16[512,128]{1,0:T(8,128)(2,1)} custom-call(s32[64,1]{1,0:T(8,128)S(1)} %get-tuple-element.19.which_ref, bf16[8,128,128]{2,1,0:T(8,128)(2,1)S(1)} %all-to-all-done.1.low_ref.up_ref, bf16[8,128,128]{2,1,0:T(8,128)(2,1)S(1)} %all-to-all-done.1.low_ref.up_ref), custom_call_target="tpu_custom_call" | custom-call | flops 50331648 | bytes 393216 | tf_op jit(solution)/shard_map/pallas_call | solution.py:362
  40.8 10.9 %all-to-all-start.2 = ((bf16[64,8,128]{2,1,0:T(8,128)(2,1)}), bf16[64,8,128]{2,1,0:T(8,128)(2,1)S(1)}, u32[]{:S(2)}, u32[]{:S(2)}) async-start(bf16[64,8,128]{2,1,0:T(8,128)(2,1)} %bitcast.3), calls=%async_computation.2 | async-start | bytes 262144 | tf_op jit(solution)/shard_map/all_to_all | solution.py:374
  51.8 0.0 collective-permute-done.1.got_ref
  51.8 0.0 copy-done.4
  51.8 0.2 shard_map.67
  52.0 1.9 %collective-permute-start.2 = (bf16[64,512]{1,0:T(8,128)(2,1)S(1)}, bf16[64,512]{1,0:T(8,128)(2,1)S(1)}, u32[]{:S(2)}, u32[]{:S(2)}) collective-permute-start(bf16[64,512]{1,0:T(8,128)(2,1)S(1)} %get-tuple-element.22), channel_id=1, source_target_pairs={{0,128},{64,192},{128,0},{192,64},{256,384},{320,448},{384,256},{4... | collective-permute-start | bytes 196616 | tf_op jit(solution)/shard_map/ppermute | solution.py:383
  53.9 3.8 %all-to-all-done.2 = bf16[64,8,128]{2,1,0:T(8,128)(2,1)S(1)} async-done(((bf16[64,8,128]{2,1,0:T(8,128)(2,1)}), bf16[64,8,128]{2,1,0:T(8,128)(2,1)S(1)}, u32[]{:S(2)}, u32[]{:S(2)}) %all-to-all-start.2) | async-done | bytes 131104 | tf_op jit(solution)/shard_map/all_to_all | solution.py:374
  57.8 0.2 shard_map.70.lora_ref
  58.0 0.0 collective-permute-done.2.got_ref
  58.0 0.7 %shard_map.71 = bf16[64,512]{1,0:T(8,128)(2,1)} custom-call(f32[64,512]{1,0:T(8,128)S(1)} %shard_map.70.lora_ref, f32[64,512]{1,0:T(8,128)S(1)} %get-tuple-element.21.mine_ref, bf16[64,512]{1,0:T(8,128)(2,1)S(1)} %collective-permute-done.2.got_ref), custom_call_target="tpu_custom_call" | custom-call | tf_op jit(solution)/shard_map/pallas_call | solution.py:392
Async XLA Ops:
  0.0 20.3 %copy-start.2 = (bf16[64,512]{1,0:T(8,128)(2,1)S(1)}, bf16[64,512]{1,0:T(8,128)(2,1)}, u32[]{:S(2)}) copy-start(bf16[64,512]{1,0:T(8,128)(2,1)} %attention_ref.5) | copy-start | bytes 196612
  0.0 20.4 %copy-start.3 = (s32[64,64]{1,0:T(8,128)S(1)}, s32[64,64]{1,0:T(8,128)}, u32[]{:S(2)}) copy-start(s32[64,64]{1,0:T(8,128)} %requested_ref.3) | copy-start | bytes 49156
  2.0 24.3 %all-to-all-start = ((bf16[64,8,128]{2,1,0:T(8,128)(2,1)}), bf16[64,8,128]{2,1,0:T(8,128)(2,1)S(1)}, u32[]{:S(2)}, u32[]{:S(2)}) async-start(bf16[64,8,128]{2,1,0:T(8,128)(2,1)} %bitcast.7), calls=%async_computation | async-start | bytes 262144 | tf_op jit(solution)/shard_map/all_to_all | solution.py:316
  20.4 6.0 %copy-start = (bf16[2,64,512]{2,1,0:T(8,128)(2,1)S(1)}, bf16[2,64,512]{2,1,0:T(8,128)(2,1)}, u32[]{:S(2)}) copy-start(bf16[2,64,512]{2,1,0:T(8,128)(2,1)} %down_ref.1) | copy-start | bytes 393220
  20.4 6.0 %copy-start.1 = (bf16[2,8,4096]{2,1,0:T(8,128)(2,1)S(1)}, bf16[2,8,4096]{2,1,0:T(8,128)(2,1)}, u32[]{:S(2)}) copy-start(bf16[2,8,4096]{2,1,0:T(8,128)(2,1)} %up_ref.1) | copy-start | bytes 393220
  22.4 12.1 %collective-permute-start = (bf16[4,64,512]{2,1,0:T(8,128)(2,1)S(1)}, bf16[4,64,512]{2,1,0:T(8,128)(2,1)S(1)}, u32[]{:S(2)}, u32[]{:S(2)}) collective-permute-start(bf16[4,64,512]{2,1,0:T(8,128)(2,1)S(1)} %get-tuple-element.15), channel_id=1, source_target_pairs={{0,64},{64,0},{128,192},{192,128},{256,320},{320,256},{384,448},{4... | collective-permute-start | bytes 786440 | tf_op jit(solution)/shard_map/ppermute | solution.py:337
  27.5 12.2 %all-to-all-start.1 = ((bf16[8,128,128]{2,1,0:T(8,128)(2,1)}), bf16[8,128,128]{2,1,0:T(8,128)(2,1)S(1)}, u32[]{:S(2)}, u32[]{:S(2)}) async-start(bf16[8,128,128]{2,1,0:T(8,128)(2,1)} %shard_map.68), calls=%async_computation.1 | async-start | bytes 524288 | tf_op jit(solution)/shard_map/all_to_all | solution.py:349
  34.5 17.3 %copy-start.4 = (s32[1,64]{1,0:T(1,128)S(1)}, s32[1,64]{1,0:T(1,128)}, u32[]{:S(2)}) copy-start(s32[1,64]{1,0:T(1,128)} %get-tuple-element.14.goes_ref) | copy-start | bytes 772
  36.6 15.2 %collective-permute-start.1 = (bf16[2,64,512]{2,1,0:T(8,128)(2,1)S(1)}, bf16[2,64,512]{2,1,0:T(8,128)(2,1)S(1)}, u32[]{:S(2)}, u32[]{:S(2)}) collective-permute-start(bf16[2,64,512]{2,1,0:T(8,128)(2,1)S(1)} %get-tuple-element.17), channel_id=1, source_target_pairs={{0,256},{64,320},{128,384},{192,448},{256,0},{320,64},{384,128},{4... | collective-permute-start | bytes 393224 | tf_op jit(solution)/shard_map/ppermute | solution.py:360
  40.8 16.9 %all-to-all-start.2 = ((bf16[64,8,128]{2,1,0:T(8,128)(2,1)}), bf16[64,8,128]{2,1,0:T(8,128)(2,1)S(1)}, u32[]{:S(2)}, u32[]{:S(2)}) async-start(bf16[64,8,128]{2,1,0:T(8,128)(2,1)} %bitcast.3), calls=%async_computation.2 | async-start | bytes 262144 | tf_op jit(solution)/shard_map/all_to_all | solution.py:374
  52.0 6.0 %collective-permute-start.2 = (bf16[64,512]{1,0:T(8,128)(2,1)S(1)}, bf16[64,512]{1,0:T(8,128)(2,1)S(1)}, u32[]{:S(2)}, u32[]{:S(2)}) collective-permute-start(bf16[64,512]{1,0:T(8,128)(2,1)S(1)} %get-tuple-element.22), channel_id=1, source_target_pairs={{0,128},{64,192},{128,0},{192,64},{256,384},{320,448},{384,256},{4... | collective-permute-start | bytes 196616 | tf_op jit(solution)/shard_map/ppermute | solution.py:383
